TPU v7x, 32 devices: a whole 2x2x4 slice. The times are simulated.
32 devices in a mesh: inline: 4 (over z), xline: 8 (over y, x, core).
Axes of the slice: x: 2, y: 2, z: 4, core: 2. Of those that a mesh axis runs over, the one named last changes fastest.
Arguments:
- right_side: float32 [32, 256, 128], P('inline', 'xline'), may hold values from -9 to 9, as said below
- facies: int32 [32, 256, 128], P('inline', 'xline'), may hold values from 0 to 7
- facies_table: float32 [2, 8], replicated, may hold values from 0.2 to 5
- thickness: float32 [32, 256, 128], P('inline', 'xline'), may hold values from 0.5 to 2
- accumulation: float32 [32, 256, 128], P('inline', 'xline'), may hold values from 0.2 to 2
- perforation_cell: int32 [131072], P(('inline', 'xline')), may hold values from 0 to 32767
- perf_owner: int32 [131072, 1], P(('inline', 'xline')), may hold values from 0 to 31; in each aligned block of 4096 rows (0 to 4095, 4096 to 8191, ...) at most 512 rows name the same one
- perf_well: int32 [131072], P(('inline', 'xline')), may hold values from 0 to 159
- perf_index: float32 [131072], P(('inline', 'xline')), may hold values from 0.5 to 5
Outputs:
- pressure: float32 [32, 256, 128], P('inline', 'xline')
- residual: float32 [32, 256, 128], P('inline', 'xline')
Inputs may be any that keep to these rules, and one draw needn't show every extreme that they name: `perforation_cell`: local flat index of a cell of the device that holds the row. `perf_owner`: device index over inline+xline; among the rows of one device at most 512 name the same owner, and that bound is reached. `right_side`: rough values of either sign.
All inputs are finite; a program needn't handle non-finite values.
Results may differ from a plain program's by a relative error of at most 0.0001.
Values sent between devices are 32-bit elements; how exact they have to be, the bound alone decides.
No kernel may reach another device: no remote copies, remote signals or barrier semaphores. Data moves between devices by JAX's collectives and lax.ppermute only.
A program may use at most 64 MiB of HBM per device.

v0:
```python
import jax
import jax.numpy as jnp
from jax import lax
from jax.sharding import PartitionSpec as P

SWEEPS = 3
WELL_DEV = 160


LOW_BOUND = 0.1
HIGH_BOUND = 2.0


def extended(cells, sides, width):
    for axis, dim in sides:
        count = lax.axis_size(axis)
        ends = count - 1
        head = lax.slice_in_dim(cells, 0, width, axis=dim)
        tail = lax.slice_in_dim(cells, cells.shape[dim] - width, cells.shape[dim], axis=dim)
        cells = jnp.concatenate(
            [
                lax.ppermute(tail, axis, [(i, (i + 1) % count) for i in range(ends)]),
                cells,
                lax.ppermute(head, axis, [((i + 1) % count, i) for i in range(ends)]),
            ],
            axis=dim,
        )
    return cells


def harmonic_average(first, second):
    return 2.0 * first * second / (first + second)


def lookup(facies, table_row):
    result = jnp.zeros(facies.shape, jnp.float32)
    for entry in range(table_row.shape[0]):
        result = jnp.where(facies == entry, table_row[entry], result)
    return result


def well_sum(values, numbers, wells):
    matches = numbers[:, None] == jnp.arange(wells, dtype=jnp.int32)[None, :]
    return jnp.sum(jnp.where(matches, values[:, None], 0.0), axis=0)


def well_pick(table, numbers):
    matches = numbers[:, None] == jnp.arange(table.shape[0], dtype=jnp.int32)[None, :]
    return jnp.sum(jnp.where(matches, table[None, :], 0.0), axis=1)


def to_owners(values):
    return lax.all_to_all(values, ("inline", "xline"), split_axis=0, concat_axis=0, tiled=True)


def from_owners(values):
    return lax.all_to_all(values, ("inline", "xline"), split_axis=0, concat_axis=0, tiled=True)


def setup_owners(weights, numbers):
    return (
        lax.all_to_all(weights, ("inline", "xline"), split_axis=0, concat_axis=0, tiled=True),
        lax.all_to_all(numbers, ("inline", "xline"), split_axis=0, concat_axis=0, tiled=True),
    )


def body(
    right_side,
    facies,
    facies_table,
    thickness,
    accumulation,
    perforation_cell,
    perf_owner,
    perf_well,
    perf_index,
):
    lateral = lookup(facies, facies_table[0]) * thickness
    vertical_trans = lookup(facies, facies_table[1]) / thickness
    padded = extended(lateral, (("inline", 0), ("xline", 1)), 1)
    inline_lower_face = harmonic_average(lateral, padded[:-2, 1:-1])
    face_iplus = harmonic_average(lateral, padded[2:, 1:-1])
    face_jmin = harmonic_average(lateral, padded[1:-1, :-2])
    face_jplus = harmonic_average(lateral, padded[1:-1, 2:])
    vertical_padding = jnp.pad(vertical_trans, ((0, 0), (0, 0), (1, 1)))
    depth_lower_face = harmonic_average(vertical_trans, vertical_padding[:, :, :-2])
    depth_upper_face = harmonic_average(vertical_trans, vertical_padding[:, :, 2:])
    shape = right_side.shape
    ncell = shape[0] * shape[1] * shape[2]
    cell_wi = jnp.zeros((ncell,), jnp.float32).at[perforation_cell].add(perf_index).reshape(shape)
    diagonal = (
        accumulation
        + inline_lower_face
        + face_iplus
        + face_jmin
        + face_jplus
        + depth_lower_face
        + depth_upper_face
        + cell_wi
    )
    n_dev = lax.axis_size("inline") * lax.axis_size("xline")
    n_perf = perforation_cell.shape[0]
    owner = perf_owner[:, 0]
    capacity = 4 * n_perf // n_dev
    order = jnp.argsort(owner, stable=True)
    sorted_owner = owner[order]
    counts = jnp.sum(
        (owner[:, None] == jnp.arange(n_dev, dtype=jnp.int32)[None, :]).astype(jnp.int32), axis=0
    )
    starts = jnp.cumsum(counts) - counts
    rank_sorted = jnp.arange(n_perf, dtype=jnp.int32) - starts[sorted_owner]
    rank = jnp.zeros((n_perf,), jnp.int32).at[order].set(rank_sorted)
    slot = owner * capacity + rank
    slots_total = n_dev * capacity
    weight_buf = jnp.zeros((slots_total,), jnp.float32).at[slot].set(perf_index)
    number_holder = jnp.zeros((slots_total,), jnp.int32).at[slot].set(perf_well)
    send_cell = jnp.zeros((slots_total,), jnp.int32).at[slot].set(perforation_cell)
    recv_weight, recv_number = setup_owners(weight_buf, number_holder)
    storage = 1.0 + well_sum(recv_weight, recv_number, WELL_DEV)
    theta = (HIGH_BOUND + LOW_BOUND) / 2.0
    delta = (HIGH_BOUND - LOW_BOUND) / 2.0
    sigma = theta / delta
    rho_now = 1.0 / sigma
    pressure = jnp.zeros_like(right_side)
    residual = right_side
    direction = residual / (theta * diagonal)
    for sweep in range(SWEEPS):
        pressure = pressure + direction
        beside_all = extended(direction, (("inline", 0), ("xline", 1)), 1)
        zpad = jnp.pad(direction, ((0, 0), (0, 0), (1, 1)))
        grid = accumulation * direction
        grid = (
            grid
            + inline_lower_face * (direction - beside_all[:-2, 1:-1])
            + face_iplus * (direction - beside_all[2:, 1:-1])
        )
        grid = (
            grid
            + face_jmin * (direction - beside_all[1:-1, :-2])
            + face_jplus * (direction - beside_all[1:-1, 2:])
        )
        grid = (
            grid
            + depth_lower_face * (direction - zpad[:, :, :-2])
            + depth_upper_face * (direction - zpad[:, :, 2:])
        )
        sent = direction.reshape(-1)[send_cell]
        arrived = to_owners(sent)
        bottom = well_sum(recv_weight * arrived, recv_number, WELL_DEV) / storage
        terms = recv_weight * (arrived - well_pick(bottom, recv_number))
        returned = from_owners(terms)
        residual = residual - (
            grid + jnp.zeros((ncell,), jnp.float32).at[send_cell].add(returned).reshape(shape)
        )
        if sweep + 1 < SWEEPS:
            rho_next = 1.0 / (2.0 * sigma - rho_now)
            direction = rho_next * rho_now * direction + 2.0 * rho_next / delta * (
                residual / diagonal
            )
            rho_now = rho_next
    return (pressure, residual)


def solution(mesh):
    in_specs = (
        P("inline", "xline", None),
        P("inline", "xline", None),
        P(),
        P("inline", "xline", None),
        P("inline", "xline", None),
        P(("inline", "xline")),
        P(("inline", "xline"), None),
        P(("inline", "xline")),
        P(("inline", "xline")),
    )
    out_specs = (P("inline", "xline", None), P("inline", "xline", None))
    return jax.shard_map(body, mesh=mesh, in_specs=in_specs, out_specs=out_specs, check_vma=False)
```

profile of v0, /device:TPU:0, one launch (start us, length us, event | category | flops | bytes accessed | tf_op | source)
XLA Modules:
  0.0 1070.3 jit_solution(8102050150380889421)
XLA Ops:
  0.6 0.9 convert_reduce_fusion
  1.9 0.7 fusion.93
  2.6 0.7 fusion.92
  3.3 5.8 sort.17
  9.1 23.0 %gather_fusion = s32[4096]{0:T(1024)S(1)} fusion(s32[4096]{0:T(1024)S(1)} %bitcast.81, s32[4096]{0:T(1024)S(1)} %get-tuple-element.68), kind=kCustom, calls=%fused_computation | custom fusion | bytes 49152 | tf_op jit(solution)/shard_map/gather | solution.py:106
  32.1 4.4 compare_select_fusion.2
  36.6 1.2 compare_reduce_fusion.24
  37.8 15.8 %select_subtract_fusion = s32[4096]{0:T(1024)S(1)} fusion(pred[4096]{0:T(1024)(128)(4,1)S(1)} %get-tuple-element.30, pred[4096]{0:T(1024)(128)(4,1)S(1)} %get-tuple-element.29, pred[4096]{0:T(1024)(128)(4,1)S(1)} %get-tuple-element.28, pred[4096]{0:T(1024)(128)(4,1)S(1)} %get-tuple-element.27, pred[4096]{0:T(1024)(128)(4,1)S(1)} %get-tuple-element.26, ...), kind=kLoop, calls=%fused_computation.204 | loop fusion | flops 106496 | bytes 135268 | tf_op jit(solution)/shard_map/sub | solution.py:111
  53.6 15.5 %scatter_custom_fusion.1 = s32[4096]{0:T(1024)S(1)} fusion(s32[4096]{0:T(1024)S(1)} %get-tuple-element.69, s32[4096]{0:T(1024)S(1)} %select_subtract_fusion, s32[]{:T(128)} %constant.28.clone.1), kind=kCustom, calls=%fused_computation.206 | custom fusion | bytes 16388 | tf_op jit(solution)/shard_map/scatter | solution.py:112
  69.1 16.4 %scatter_custom_fusion.3 = f32[16384]{0:T(1024)} fusion(s32[4096]{0:T(1024)S(1)} %compare_select_fusion.8, f32[4096]{0:T(1024)} %param.17, f32[]{:T(128)} %constant.3.clone.1), kind=kCustom, calls=%fused_computation.198 | custom fusion | bytes 66048 | tf_op jit(solution)/shard_map/scatter | solution.py:115
  85.6 7.3 all-to-all-start
  92.9 0.7 fusion.91
  93.6 5.2 select_multiply_fusion
  98.8 3.7 collective-permute-start
  102.5 1.3 collective-permute-start.1
  103.8 15.6 %scatter_custom_fusion.2 = s32[16384]{0:T(1024)S(1)} fusion(s32[4096]{0:T(1024)S(1)} %compare_select_fusion.8, s32[4096]{0:T(1024)S(1)} %copy-done.6, s32[]{:T(128)} %constant.28.clone.1), kind=kCustom, calls=%fused_computation.202 | custom fusion | bytes 65540 | tf_op jit(solution)/shard_map/scatter | solution.py:117
  119.4 5.1 select_divide_fusion
  124.5 1.9 collective-permute-start.2
  126.5 1.3 collective-permute-start.3
  127.8 22.1 %scatter_custom_fusion = f32[32768]{0:T(1024)S(1)} fusion(s32[4096]{0:T(1024)S(1)} %compare_select_fusion.10, f32[4096]{0:T(1024)} %param.17, f32[]{:T(128)} %constant.3.clone.1), kind=kCustom, calls=%fused_computation.153 | custom fusion | flops 4096 | bytes 131584 | tf_op jit(solution)/shard_map/scatter-add | solution.py:90
  150.1 160.6 %gather_fusion.1 = f32[16384]{0:T(1024)} fusion(f32[32768]{0:T(1024)S(1)} %bitcast.76, s32[16384]{0:T(1024)S(1)} %get-tuple-element.66), kind=kCustom, calls=%fused_computation.1 | custom fusion | bytes 196608 | tf_op jit(solution)/shard_map/gather | solution.py:147
  310.8 9.2 all-to-all-start.1
  320.0 16.3 %scatter_custom_fusion.4 = s32[16384]{0:T(1024)} fusion(s32[4096]{0:T(1024)S(1)} %compare_select_fusion.8, s32[4096]{0:T(1024)} %param.16, s32[]{:T(128)} %constant.28.clone.1), kind=kCustom, calls=%fused_computation.200 | custom fusion | bytes 66048 | tf_op jit(solution)/shard_map/scatter | solution.py:116
  336.3 5.8 all-to-all-start.2
  342.1 3.7 collective-permute-start.4
  345.8 1.5 collective-permute-start.5
  347.3 2.2 all-to-all-done.2
  349.5 3.4 select_reduce_fusion.5
  353.0 1.6 select_reduce_fusion.4
  354.6 0.7 copy.34
  355.3 4.5 all-to-all-start.3
  359.8 2.2 collective-permute-start.6
  362.0 1.3 collective-permute-start.7
  363.3 3.9 all-to-all-done.3
  367.2 106.6 %scatter_custom_fusion.5 = f32[32768]{0:T(1024)S(1)} fusion(s32[16384]{0:T(1024)S(1)} %get-tuple-element.67, f32[16384]{0:T(1024)S(1)} %bitcast.101, f32[]{:T(128)} %constant.3.clone.1), kind=kCustom, calls=%fused_computation.151 | custom fusion | flops 16384 | bytes 131076 | tf_op jit(solution)/shard_map/scatter-add | solution.py:153
  474.1 160.6 %gather_fusion.2 = f32[16384]{0:T(1024)} fusion(f32[32768]{0:T(1024)S(1)} %bitcast.78, s32[16384]{0:T(1024)S(1)} %get-tuple-element.66), kind=kCustom, calls=%fused_computation.2 | custom fusion | bytes 196608 | tf_op jit(solution)/shard_map/gather | solution.py:147
  634.7 4.1 all-to-all-start.4
  638.8 3.7 collective-permute-start.8
  642.4 1.3 collective-permute-start.9
  643.7 2.4 all-to-all-done.4
  646.2 1.9 select_reduce_fusion.3
  648.0 1.6 select_reduce_fusion.2
  649.6 0.7 copy.38
  650.3 4.3 all-to-all-start.5
  654.7 2.2 collective-permute-start.10
  656.9 1.5 collective-permute-start.11
  658.4 3.7 all-to-all-done.5
  662.1 106.6 %scatter_custom_fusion.6 = f32[32768]{0:T(1024)S(1)} fusion(s32[16384]{0:T(1024)S(1)} %get-tuple-element.67, f32[16384]{0:T(1024)S(1)} %bitcast.102, f32[]{:T(128)} %constant.3.clone.1), kind=kCustom, calls=%fused_computation.149 | custom fusion | flops 16384 | bytes 131076 | tf_op jit(solution)/shard_map/scatter-add | solution.py:153
  768.7 0.3 multiply_add_fusion
  769.0 2.5 collective-permute-start.12
  771.5 1.3 collective-permute-start.13
  772.8 160.6 %gather_fusion.3 = f32[16384]{0:T(1024)} fusion(f32[32768]{0:T(1024)S(1)} %bitcast.77, s32[16384]{0:T(1024)S(1)} %get-tuple-element.66), kind=kCustom, calls=%fused_computation.3 | custom fusion | bytes 196608 | tf_op jit(solution)/shard_map/gather | solution.py:147
  933.4 6.3 all-to-all-start.6
  939.8 2.2 collective-permute-start.14
  941.9 1.3 collective-permute-start.15
  943.2 3.9 all-to-all-done.6
  947.2 1.9 select_reduce_fusion.1
  949.0 1.6 select_reduce_fusion
  950.6 0.7 copy.42
  951.3 4.1 all-to-all-start.7
  955.4 0.7 add_add_fusion
  956.1 6.7 all-to-all-done.7
  962.8 106.6 %scatter_custom_fusion.7 = f32[32768]{0:T(1024)S(1)} fusion(s32[16384]{0:T(1024)S(1)} %get-tuple-element.67, f32[16384]{0:T(1024)S(1)} %bitcast.103, f32[]{:T(128)} %constant.3.clone.1), kind=kCustom, calls=%fused_computation.147 | custom fusion | flops 16384 | bytes 131076 | tf_op jit(solution)/shard_map/scatter-add | solution.py:153
  1069.4 0.9 fusion.21
  (63 shorter events, 1.1 us)
Async XLA Ops:
  0.6 2.7 copy-start
  53.6 39.3 %copy-start.5 = (f32[2,8]{1,0:T(2,128)S(1)}, f32[2,8]{1,0:T(2,128)}, u32[]{:S(2)}) copy-start(f32[2,8]{1,0:T(2,128)} %param.11) | copy-start | bytes 196
  69.1 24.5 %copy-start.4 = (s32[8,32,128]{2,1,0:T(8,128)S(1)}, s32[8,32,128]{2,1,0:T(8,128)}, u32[]{:S(2)}) copy-start(s32[8,32,128]{2,1,0:T(8,128)} %param.10) | copy-start | bytes 393220
  69.1 24.5 %copy-start.3 = (f32[8,32,128]{2,1,0:T(8,128)S(1)}, f32[8,32,128]{2,1,0:T(8,128)}, u32[]{:S(2)}) copy-start(f32[8,32,128]{2,1,0:T(8,128)} %param.12) | copy-start | bytes 393220
  85.6 225.2 %all-to-all-start = ((f32[32,512,1]{1,2,0:T(1,128)}), f32[32,512,1]{1,2,0:T(1,128)S(1)}, u32[]{:S(2)}, u32[]{:S(2)}) async-start(f32[32,512,1]{1,2,0:T(1,128)} %bitcast.53), calls=%async_computation | async-start | bytes 131072 | tf_op jit(solution)/shard_map/all_to_all | solution.py:62
  93.6 10.2 copy-start.6
  98.8 25.7 %collective-permute-start = (f32[1,32,128]{2,1,0:T(8,128)S(1)}, f32[1,32,128]{2,1,0:T(8,128)S(1)}, u32[]{:S(2)}, u32[]{:S(2)}) collective-permute-start(f32[1,32,128]{2,1,0:T(8,128)S(1)} %get-tuple-element.64), channel_id=1, source_target_pairs={{0,8},{8,16},{16,24},{1,9},{9,17},{17,25},{2,10},{10,18},{18,26},{... | collective-permute-start | bytes 49160 | tf_op jit(solution)/shard_map/ppermute | solution.py:22
  102.5 22.0 %collective-permute-start.1 = (f32[1,32,128]{2,1,0:T(8,128)S(1)}, f32[1,32,128]{2,1,0:T(8,128)S(1)}, u32[]{:S(2)}, u32[]{:S(2)}) collective-permute-start(f32[1,32,128]{2,1,0:T(8,128)S(1)} %get-tuple-element.65), channel_id=1, source_target_pairs={{8,0},{16,8},{24,16},{9,1},{17,9},{25,17},{10,2},{18,10},{26,18},{... | collective-permute-start | bytes 49160 | tf_op jit(solution)/shard_map/ppermute | solution.py:24
  124.5 25.4 %copy-start.1 = (f32[8,32,128]{2,1,0:T(8,128)S(1)}, f32[8,32,128]{2,1,0:T(8,128)}, u32[]{:S(2)}) copy-start(f32[8,32,128]{2,1,0:T(8,128)} %param.9) | copy-start | bytes 393220
  124.5 25.4 %copy-start.2 = (f32[8,32,128]{2,1,0:T(8,128)S(1)}, f32[8,32,128]{2,1,0:T(8,128)}, u32[]{:S(2)}) copy-start(f32[8,32,128]{2,1,0:T(8,128)} %param.13) | copy-start | bytes 393220
  124.5 25.4 %collective-permute-start.2 = (f32[10,1,128]{2,1,0:T(1,128)S(1)}, f32[10,1,128]{2,1,0:T(1,128)S(1)}, u32[]{:S(2)}, u32[]{:S(2)}) collective-permute-start(f32[10,1,128]{2,1,0:T(1,128)S(1)} %get-tuple-element.56), channel_id=1, source_target_pairs={{0,1},{1,2},{2,3},{3,4},{4,5},{5,6},{6,7},{8,9},{9,10},{10,11},{11... | collective-permute-start | bytes 15368 | tf_op jit(solution)/shard_map/ppermute | solution.py:22
  126.5 23.4 %collective-permute-start.3 = (f32[10,1,128]{2,1,0:T(1,128)S(1)}, f32[10,1,128]{2,1,0:T(1,128)S(1)}, u32[]{:S(2)}, u32[]{:S(2)}) collective-permute-start(f32[10,1,128]{2,1,0:T(1,128)S(1)} %get-tuple-element.57), channel_id=1, source_target_pairs={{1,0},{2,1},{3,2},{4,3},{5,4},{6,5},{7,6},{9,8},{10,9},{11,10},{12... | collective-permute-start | bytes 15368 | tf_op jit(solution)/shard_map/ppermute | solution.py:24
  310.8 25.5 %all-to-all-start.1 = ((f32[32,512,1]{1,2,0:T(1,128)}), f32[32,512,1]{1,2,0:T(1,128)S(1)}, u32[]{:S(2)}, u32[]{:S(2)}) async-start(f32[32,512,1]{1,2,0:T(1,128)} %bitcast.55), calls=%async_computation.1 | async-start | bytes 131072 | tf_op jit(solution)/shard_map/all_to_all | solution.py:53
  336.3 13.2 %all-to-all-start.2 = ((s32[32,512,1]{1,2,0:T(1,128)}), s32[32,512,1]{1,2,0:T(1,128)S(1)}, u32[]{:S(2)}, u32[]{:S(2)}) async-start(s32[32,512,1]{1,2,0:T(1,128)} %bitcast.56), calls=%async_computation.2 | async-start | bytes 131072 | tf_op jit(solution)/shard_map/all_to_all | solution.py:63
  342.1 17.7 %collective-permute-start.4 = (f32[1,32,128]{2,1,0:T(8,128)S(1)}, f32[1,32,128]{2,1,0:T(8,128)S(1)}, u32[]{:S(2)}, u32[]{:S(2)}) collective-permute-start(f32[1,32,128]{2,1,0:T(8,128)S(1)} %get-tuple-element.62), channel_id=1, source_target_pairs={{0,8},{8,16},{16,24},{1,9},{9,17},{17,25},{2,10},{10,18},{18,26},{... | collective-permute-start | bytes 49160 | tf_op jit(solution)/shard_map/ppermute | solution.py:22
  345.8 14.0 %collective-permute-start.5 = (f32[1,32,128]{2,1,0:T(8,128)S(1)}, f32[1,32,128]{2,1,0:T(8,128)S(1)}, u32[]{:S(2)}, u32[]{:S(2)}) collective-permute-start(f32[1,32,128]{2,1,0:T(8,128)S(1)} %get-tuple-element.63), channel_id=1, source_target_pairs={{8,0},{16,8},{24,16},{9,1},{17,9},{25,17},{10,2},{18,10},{26,18},{... | collective-permute-start | bytes 49160 | tf_op jit(solution)/shard_map/ppermute | solution.py:24
  355.3 11.9 %all-to-all-start.3 = ((f32[32,512,1]{1,2,0:T(1,128)}), f32[32,512,1]{1,2,0:T(1,128)S(1)}, u32[]{:S(2)}, u32[]{:S(2)}) async-start(f32[32,512,1]{1,2,0:T(1,128)} %copy.34), calls=%async_computation.3 | async-start | bytes 131072 | tf_op jit(solution)/shard_map/all_to_all | solution.py:57
  359.8 114.0 %collective-permute-start.6 = (f32[10,1,128]{2,1,0:T(1,128)S(1)}, f32[10,1,128]{2,1,0:T(1,128)S(1)}, u32[]{:S(2)}, u32[]{:S(2)}) collective-permute-start(f32[10,1,128]{2,1,0:T(1,128)S(1)} %get-tuple-element.54), channel_id=1, source_target_pairs={{0,1},{1,2},{2,3},{3,4},{4,5},{5,6},{6,7},{8,9},{9,10},{10,11},{11... | collective-permute-start | bytes 15368 | tf_op jit(solution)/shard_map/ppermute | solution.py:22
  362.0 111.8 %collective-permute-start.7 = (f32[10,1,128]{2,1,0:T(1,128)S(1)}, f32[10,1,128]{2,1,0:T(1,128)S(1)}, u32[]{:S(2)}, u32[]{:S(2)}) collective-permute-start(f32[10,1,128]{2,1,0:T(1,128)S(1)} %get-tuple-element.55), channel_id=1, source_target_pairs={{1,0},{2,1},{3,2},{4,3},{5,4},{6,5},{7,6},{9,8},{10,9},{11,10},{12... | collective-permute-start | bytes 15368 | tf_op jit(solution)/shard_map/ppermute | solution.py:24
  634.7 11.5 %all-to-all-start.4 = ((f32[32,512,1]{1,2,0:T(1,128)}), f32[32,512,1]{1,2,0:T(1,128)S(1)}, u32[]{:S(2)}, u32[]{:S(2)}) async-start(f32[32,512,1]{1,2,0:T(1,128)} %bitcast.63), calls=%async_computation.4 | async-start | bytes 131072 | tf_op jit(solution)/shard_map/all_to_all | solution.py:53
  638.8 15.9 %collective-permute-start.8 = (f32[1,32,128]{2,1,0:T(8,128)S(1)}, f32[1,32,128]{2,1,0:T(8,128)S(1)}, u32[]{:S(2)}, u32[]{:S(2)}) collective-permute-start(f32[1,32,128]{2,1,0:T(8,128)S(1)} %get-tuple-element.60), channel_id=1, source_target_pairs={{0,8},{8,16},{16,24},{1,9},{9,17},{17,25},{2,10},{10,18},{18,26},{... | collective-permute-start | bytes 49160 | tf_op jit(solution)/shard_map/ppermute | solution.py:22
  642.4 12.2 %collective-permute-start.9 = (f32[1,32,128]{2,1,0:T(8,128)S(1)}, f32[1,32,128]{2,1,0:T(8,128)S(1)}, u32[]{:S(2)}, u32[]{:S(2)}) collective-permute-start(f32[1,32,128]{2,1,0:T(8,128)S(1)} %get-tuple-element.61), channel_id=1, source_target_pairs={{8,0},{16,8},{24,16},{9,1},{17,9},{25,17},{10,2},{18,10},{26,18},{... | collective-permute-start | bytes 49160 | tf_op jit(solution)/shard_map/ppermute | solution.py:24
  650.3 11.7 %all-to-all-start.5 = ((f32[32,512,1]{1,2,0:T(1,128)}), f32[32,512,1]{1,2,0:T(1,128)S(1)}, u32[]{:S(2)}, u32[]{:S(2)}) async-start(f32[32,512,1]{1,2,0:T(1,128)} %copy.38), calls=%async_computation.5 | async-start | bytes 131072 | tf_op jit(solution)/shard_map/all_to_all | solution.py:57
  654.7 114.0 %collective-permute-start.10 = (f32[10,1,128]{2,1,0:T(1,128)S(1)}, f32[10,1,128]{2,1,0:T(1,128)S(1)}, u32[]{:S(2)}, u32[]{:S(2)}) collective-permute-start(f32[10,1,128]{2,1,0:T(1,128)S(1)} %get-tuple-element.52), channel_id=1, source_target_pairs={{0,1},{1,2},{2,3},{3,4},{4,5},{5,6},{6,7},{8,9},{9,10},{10,11},{11... | collective-permute-start | bytes 15368 | tf_op jit(solution)/shard_map/ppermute | solution.py:22
  656.9 111.8 %collective-permute-start.11 = (f32[10,1,128]{2,1,0:T(1,128)S(1)}, f32[10,1,128]{2,1,0:T(1,128)S(1)}, u32[]{:S(2)}, u32[]{:S(2)}) collective-permute-start(f32[10,1,128]{2,1,0:T(1,128)S(1)} %get-tuple-element.53), channel_id=1, source_target_pairs={{1,0},{2,1},{3,2},{4,3},{5,4},{6,5},{7,6},{9,8},{10,9},{11,10},{12... | collective-permute-start | bytes 15368 | tf_op jit(solution)/shard_map/ppermute | solution.py:24
  769.0 170.8 %collective-permute-start.12 = (f32[1,32,128]{2,1,0:T(8,128)S(1)}, f32[1,32,128]{2,1,0:T(8,128)S(1)}, u32[]{:S(2)}, u32[]{:S(2)}) collective-permute-start(f32[1,32,128]{2,1,0:T(8,128)S(1)} %get-tuple-element.58), channel_id=1, source_target_pairs={{0,8},{8,16},{16,24},{1,9},{9,17},{17,25},{2,10},{10,18},{18,26},{... | collective-permute-start | bytes 49160 | tf_op jit(solution)/shard_map/ppermute | solution.py:22
  771.5 168.2 %collective-permute-start.13 = (f32[1,32,128]{2,1,0:T(8,128)S(1)}, f32[1,32,128]{2,1,0:T(8,128)S(1)}, u32[]{:S(2)}, u32[]{:S(2)}) collective-permute-start(f32[1,32,128]{2,1,0:T(8,128)S(1)} %get-tuple-element.59), channel_id=1, source_target_pairs={{8,0},{16,8},{24,16},{9,1},{17,9},{25,17},{10,2},{18,10},{26,18},{... | collective-permute-start | bytes 49160 | tf_op jit(solution)/shard_map/ppermute | solution.py:24
  933.4 13.7 %all-to-all-start.6 = ((f32[32,512,1]{1,2,0:T(1,128)}), f32[32,512,1]{1,2,0:T(1,128)S(1)}, u32[]{:S(2)}, u32[]{:S(2)}) async-start(f32[32,512,1]{1,2,0:T(1,128)} %bitcast.68), calls=%async_computation.6 | async-start | bytes 131072 | tf_op jit(solution)/shard_map/all_to_all | solution.py:53
  939.8 129.6 %collective-permute-start.14 = (f32[10,1,128]{2,1,0:T(1,128)S(1)}, f32[10,1,128]{2,1,0:T(1,128)S(1)}, u32[]{:S(2)}, u32[]{:S(2)}) collective-permute-start(f32[10,1,128]{2,1,0:T(1,128)S(1)} %get-tuple-element.50), channel_id=1, source_target_pairs={{0,1},{1,2},{2,3},{3,4},{4,5},{5,6},{6,7},{8,9},{9,10},{10,11},{11... | collective-permute-start | bytes 15368 | tf_op jit(solution)/shard_map/ppermute | solution.py:22
  941.9 127.5 %collective-permute-start.15 = (f32[10,1,128]{2,1,0:T(1,128)S(1)}, f32[10,1,128]{2,1,0:T(1,128)S(1)}, u32[]{:S(2)}, u32[]{:S(2)}) collective-permute-start(f32[10,1,128]{2,1,0:T(1,128)S(1)} %get-tuple-element.51), channel_id=1, source_target_pairs={{1,0},{2,1},{3,2},{4,3},{5,4},{6,5},{7,6},{9,8},{10,9},{11,10},{12... | collective-permute-start | bytes 15368 | tf_op jit(solution)/shard_map/ppermute | solution.py:24
  951.3 11.5 %all-to-all-start.7 = ((f32[32,512,1]{1,2,0:T(1,128)}), f32[32,512,1]{1,2,0:T(1,128)S(1)}, u32[]{:S(2)}, u32[]{:S(2)}) async-start(f32[32,512,1]{1,2,0:T(1,128)} %copy.42), calls=%async_computation.7 | async-start | bytes 131072 | tf_op jit(solution)/shard_map/all_to_all | solution.py:57
where the time goes:
time: 1070 us
  local copies, waits for them, and re-layouts  573 us (54%)
  other arithmetic  395 us (37%)
  starting transfers between devices  78.2 us (7%)
  waiting for transfers between devices  22.9 us (2%)
    gather x3, local copies, waits for them, and re-layouts, body(): sent = direction.reshape(-1)[send_cell]  482 us
    scatter-add x3, other arithmetic, body(): jnp.zeros((ncell,), jnp.float32).at[send_cell].add(returned).reshape(shape)  320 us
    gather x1, local copies, waits for them, and re-layouts, body(): sorted_owner = owner[order]  23 us
    scatter-add x1, other arithmetic, body(): jnp.zeros((ncell,), jnp.float32).at[perforation_cell].add(perf_index)  22.1 us
    ppermute x8, starting transfers between devices, extended(): lax.ppermute(tail, axis, [(i, (i + 1) % count) for i in range(ends)])  21.9 us
  transfers between devices with their start and end apart: 24, of which 6 were waited for; matrix products, arithmetic and copies ran while one was open for 67% of the time, Pallas kernels for 0%

commit v1 on v0

v1 whole, which is shorter than its diff:
```python
import functools

import jax
import jax.numpy as jnp
from jax import lax
from jax.experimental import pallas as pl
from jax.experimental.pallas import tpu as pltpu
from jax.sharding import PartitionSpec as P

SWEEPS = 3
WELL_DEV = 160
LANES = 128
LOW_BOUND = 0.1
HIGH_BOUND = 2.0
CHUNK = 512
MESH_AXES = ("inline", "xline")

VMEM = pl.BlockSpec(memory_space=pltpu.VMEM)
SMEM = pl.BlockSpec(memory_space=pltpu.SMEM)
PARAMS = pltpu.CompilerParams(vmem_limit_bytes=40 * 1024 * 1024)


def xor_permute(value, axis, mask):
    count = lax.axis_size(axis)
    return lax.ppermute(value, axis, [(i, i ^ mask) for i in range(count)])


def bits_of(count):
    bits = count.bit_length() - 1
    if 1 << bits != count:
        raise ValueError("axis size")
    return bits


def side_masks(count):
    return [(2 << s) - 1 for s in range(bits_of(count))]


def stages_of(count):
    bits = bits_of(count)
    cuts = ([1] if bits % 2 else []) + [2] * (bits // 2)
    stages, low = [], 0
    for width in cuts:
        masks = []
        for pattern in range(1, 1 << width):
            mask = pattern << low
            if pattern & (pattern + 1) == 0:
                mask |= (1 << low) - 1
            masks.append(mask)
        stages.append(masks)
        low += width
    return stages


def all_sum(value, sides):
    arrived = {}
    rows = value.shape[0]
    for axis in ("xline", "inline"):
        count = lax.axis_size(axis)
        carried = side_masks(count)
        for masks in stages_of(count):
            total = value
            for mask in masks:
                if mask in carried:
                    face = sides[axis][0 if mask == 1 else 1]
                    got = xor_permute(jnp.concatenate([value, face], axis=0), axis, mask)
                    arrived[axis, mask] = got[rows:]
                    total = total + got[:rows]
                else:
                    total = total + xor_permute(value, axis, mask)
            value = total
    return value, halos(arrived)


def side_exchange(sides):
    arrived = {}
    for axis in ("inline", "xline"):
        for mask in side_masks(lax.axis_size(axis)):
            arrived[axis, mask] = xor_permute(sides[axis][0 if mask == 1 else 1], axis, mask)
    return halos(arrived)


def halos(arrived):
    result = {}
    for axis in MESH_AXES:
        index = lax.axis_index(axis)
        even = index % 2 == 0
        other = jnp.where(even, index - 1, index + 1)
        beside = arrived[axis, 1]
        far = beside
        for mask in side_masks(lax.axis_size(axis))[1:]:
            far = jnp.where((index ^ other) == mask, arrived[axis, mask], far)
        result[axis] = (jnp.where(even, far, beside), jnp.where(even, beside, far))
    return result


def sides_of(lower, upper, axis):
    even = lax.axis_index(axis) % 2 == 0
    return jnp.where(even, upper, lower), jnp.where(even, lower, upper)


def all_sides(cells):
    return {
        "inline": sides_of(cells[0], cells[-1], "inline"),
        "xline": sides_of(cells[:, 0], cells[:, -1], "xline"),
    }


def harmonic_average(first, second):
    return 2.0 * first * second / (first + second)


def split2(value):
    high = value.astype(jnp.bfloat16)
    low = (value - high.astype(jnp.float32)).astype(jnp.bfloat16)
    return high, low


def dot_nt(a, b):
    return lax.dot_general(a, b, (((1,), (1,)), ((), ())), preferred_element_type=jnp.float32)


def dot_nn(a, b):
    return lax.dot_general(a, b, (((1,), (0,)), ((), ())), preferred_element_type=jnp.float32)


def one_hot(index_row, rows):
    shape = (rows, index_row.shape[1])
    return lax.broadcasted_iota(jnp.int32, shape, 0) == index_row


def well_place(owner_ref, well_ref, part):
    number = owner_ref[:, part] * WELL_DEV + well_ref[:, part]
    return number >> 7, number & (LANES - 1)


def fill_rows(cell_ref, row_ref):
    for start in range(0, cell_ref.shape[1], CHUNK):
        part = pl.ds(start, CHUNK)
        row_ref[:, part] = jnp.where(one_hot(cell_ref[:, part] >> 7, row_ref.shape[0]), 1.0, 0.0).astype(jnp.bfloat16)


def place_values(cell_ref, part, values, col_ref):
    hit = one_hot(cell_ref[:, part] & (LANES - 1), LANES)
    high, low = split2(values)
    col_ref[0:LANES, part] = jnp.where(hit, high.astype(jnp.float32), 0.0).astype(jnp.bfloat16)
    col_ref[LANES:, part] = jnp.where(hit, low.astype(jnp.float32), 0.0).astype(jnp.bfloat16)


def cells_sum(row_ref, col_ref):
    both = dot_nt(row_ref[...], col_ref[...])
    return both[:, :LANES] + both[:, LANES:]


def well_values(values, row, col, wells):
    hit = one_hot(row, wells)
    high, low = split2(values)
    weights = jnp.concatenate(
        [
            jnp.where(hit, high.astype(jnp.float32), 0.0),
            jnp.where(hit, low.astype(jnp.float32), 0.0),
        ],
        axis=0,
    ).astype(jnp.bfloat16)
    places = jnp.where(one_hot(col, LANES), 1.0, 0.0).astype(jnp.bfloat16)
    both = dot_nt(weights, places)
    return both[:wells] + both[wells:]


def gather_cells(fieldt, row_ref, cell_ref, part):
    both = dot_nn(fieldt, row_ref[:, part])
    picked = jnp.where(
        one_hot(cell_ref[:, part] & (LANES - 1), LANES), both[:LANES] + both[LANES:], 0.0
    )
    return jnp.sum(picked, axis=0, keepdims=True)


def gather_wells(table, row, col, wells):
    places = jnp.where(one_hot(col, LANES), 1.0, 0.0).astype(jnp.bfloat16)
    both = dot_nn(table, places)
    picked = jnp.where(one_hot(row, wells), both[:wells] + both[wells:], 0.0)
    return jnp.sum(picked, axis=0, keepdims=True)


def stack_split(value):
    high, low = split2(value)
    return jnp.concatenate([high.astype(jnp.float32), low.astype(jnp.float32)], axis=0).astype(jnp.bfloat16)


def lookup(facies, table_ref, row):
    result = jnp.full(facies.shape, table_ref[row, 0], jnp.float32)
    for entry in range(1, table_ref.shape[1]):
        result = jnp.where(facies == entry, table_ref[row, entry], result)
    return result


def lateral_kernel(table_ref, facies_ref, thickness_ref, lateral_ref):
    lateral_ref[...] = lookup(facies_ref[...], table_ref, 0) * thickness_ref[...]


def neighbours(cells, lower, upper, dim):
    if dim == 0:
        return (
            jnp.concatenate([lower[None], cells[:-1]], axis=0),
            jnp.concatenate([cells[1:], upper[None]], axis=0),
        )
    size = cells.shape[1]
    place = lax.broadcasted_iota(jnp.int32, cells.shape, 1)
    return (
        jnp.where(place == 0, lower[:, None], pltpu.roll(cells, 1, 1)),
        jnp.where(place == size - 1, upper[:, None], pltpu.roll(cells, size - 1, 1)),
    )


def layers(cells):
    return pltpu.roll(cells, 1, 2), pltpu.roll(cells, LANES - 1, 2)


def perforation_kernel(
    table_ref, facies_ref, thickness_ref, cell_ref, owner_ref, well_ref, index_ref,
    cellwi_ref, storage_ref, zlow_ref, zup_ref, row_ref, col_ref,
):
    vertical = lookup(facies_ref[...], table_ref, 1) / thickness_ref[...]
    below, above = layers(vertical)
    place = lax.broadcasted_iota(jnp.int32, vertical.shape, 2)
    zlow_ref[...] = jnp.where(place == 0, 0.0, harmonic_average(vertical, below))
    zup_ref[...] = jnp.where(place == LANES - 1, 0.0, harmonic_average(vertical, above))
    fill_rows(cell_ref, row_ref)
    total = jnp.zeros(storage_ref.shape, jnp.float32)
    for start in range(0, cell_ref.shape[1], CHUNK):
        part = pl.ds(start, CHUNK)
        place_values(cell_ref, part, index_ref[:, part], col_ref)
        row, col = well_place(owner_ref, well_ref, part)
        total = total + well_values(index_ref[:, part], row, col, storage_ref.shape[0])
    storage_ref[...] = total
    cellwi_ref[...] = cells_sum(row_ref, col_ref).reshape(cellwi_ref.shape)


def start_kernel(
    edge_ref, right_ref, lateral_ref, accumulation_ref, cellwi_ref, zlow_ref, zup_ref,
    ilow_ref, iup_ref, xlow_ref, xup_ref, cell_ref, owner_ref, well_ref, index_ref,
    til_ref, tiu_ref, txl_ref, txu_ref, diagonal_ref, inverse_ref, direction_ref, sums_ref, row_ref,
    *, scale,
):
    lateral = lateral_ref[...]
    low, up = neighbours(
        lateral,
        jnp.where(edge_ref[0] == 1, 0.0, ilow_ref[...]),
        jnp.where(edge_ref[1] == 1, 0.0, iup_ref[...]),
        0,
    )
    til, tiu = harmonic_average(lateral, low), harmonic_average(lateral, up)
    low, up = neighbours(
        lateral,
        jnp.where(edge_ref[2] == 1, 0.0, xlow_ref[...]),
        jnp.where(edge_ref[3] == 1, 0.0, xup_ref[...]),
        1,
    )
    txl, txu = harmonic_average(lateral, low), harmonic_average(lateral, up)
    til_ref[...], tiu_ref[...], txl_ref[...], txu_ref[...] = til, tiu, txl, txu
    diagonal = accumulation_ref[...] + til + tiu + txl + txu + zlow_ref[...] + zup_ref[...] + cellwi_ref[...]
    inverse = 1.0 / diagonal
    direction = right_ref[...] * inverse * scale
    diagonal_ref[...] = diagonal
    inverse_ref[...] = inverse
    direction_ref[...] = direction
    fill_rows(cell_ref, row_ref)
    sums_ref[...] = perforation_sums(direction, row_ref, cell_ref, owner_ref, well_ref, index_ref, sums_ref.shape[0])


def perforation_sums(direction, row_ref, cell_ref, owner_ref, well_ref, index_ref, wells):
    fieldt = stack_split(direction.reshape(-1, LANES).T)
    total = jnp.zeros((wells, LANES), jnp.float32)
    for start in range(0, cell_ref.shape[1], CHUNK):
        part = pl.ds(start, CHUNK)
        values = index_ref[:, part] * gather_cells(fieldt, row_ref, cell_ref, part)
        row, col = well_place(owner_ref, well_ref, part)
        total = total + well_values(values, row, col, wells)
    return total


def sweep_kernel(
    residual_ref, direction_ref, pressure_ref, diagonal_ref, inverse_ref,
    til_ref, tiu_ref, txl_ref, txu_ref, zlow_ref, zup_ref,
    ilow_ref, iup_ref, xlow_ref, xup_ref, sums_ref, storage_ref,
    cell_ref, owner_ref, well_ref, index_ref,
    *rest, keep, gain, first,
):
    last = keep is None
    if last:
        next_pressure_ref, next_residual_ref, row_ref, col_ref = rest
    else:
        next_pressure_ref, next_residual_ref, next_direction_ref, next_sums_ref, row_ref, col_ref = rest
    wells = sums_ref.shape[0]
    fill_rows(cell_ref, row_ref)
    bottom = stack_split(sums_ref[...] / (1.0 + storage_ref[...]))
    for start in range(0, cell_ref.shape[1], CHUNK):
        part = pl.ds(start, CHUNK)
        row, col = well_place(owner_ref, well_ref, part)
        values = index_ref[:, part] * gather_wells(bottom, row, col, wells)
        place_values(cell_ref, part, values, col_ref)
    direction = direction_ref[...]
    ilow, iup = neighbours(direction, ilow_ref[...], iup_ref[...], 0)
    xlow, xup = neighbours(direction, xlow_ref[...], xup_ref[...], 1)
    below, above = layers(direction)
    beside = (
        til_ref[...] * ilow + tiu_ref[...] * iup + txl_ref[...] * xlow + txu_ref[...] * xup
        + zlow_ref[...] * below + zup_ref[...] * above
    )
    wells_term = cells_sum(row_ref, col_ref).reshape(direction.shape)
    residual = residual_ref[...] - (diagonal_ref[...] * direction - beside - wells_term)
    next_residual_ref[...] = residual
    if first:
        next_pressure_ref[...] = direction
    else:
        next_pressure_ref[...] = pressure_ref[...] + direction
    if not last:
        following = keep * direction + gain * (residual * inverse_ref[...])
        next_direction_ref[...] = following
        next_sums_ref[...] = perforation_sums(
            following, row_ref, cell_ref, owner_ref, well_ref, index_ref, wells
        )


def body(
    right_side,
    facies,
    facies_table,
    thickness,
    accumulation,
    perforation_cell,
    perf_owner,
    perf_well,
    perf_index,
):
    shape = right_side.shape
    f32 = jnp.float32
    grid = jax.ShapeDtypeStruct(shape, f32)
    n_perf = perforation_cell.shape[0]
    n_dev = lax.axis_size("inline") * lax.axis_size("xline")
    wells = -(-n_dev * WELL_DEV // (8 * LANES)) * 8
    sums = jax.ShapeDtypeStruct((wells, LANES), f32)
    cell = perforation_cell.reshape(1, n_perf)
    owner = perf_owner.reshape(1, n_perf)
    well = perf_well.reshape(1, n_perf)
    index = perf_index.reshape(1, n_perf)
    perforations = (cell, owner, well, index)
    rows = shape[0] * shape[1]
    row_scratch = pltpu.VMEM((rows, n_perf), jnp.bfloat16)
    col_scratch = pltpu.VMEM((2 * LANES, n_perf), jnp.bfloat16)

    lateral = pl.pallas_call(
        lateral_kernel, out_shape=grid, in_specs=[SMEM, VMEM, VMEM], out_specs=VMEM,
    )(facies_table, facies, thickness)
    lateral_halo = side_exchange(all_sides(lateral))
    cellwi, storage, zlow, zup = pl.pallas_call(
        perforation_kernel,
        out_shape=(grid, sums, grid, grid),
        in_specs=[SMEM] + [VMEM] * 6,
        out_specs=(VMEM,) * 4,
        scratch_shapes=[row_scratch, col_scratch],
        compiler_params=PARAMS,
    )(facies_table, facies, thickness, *perforations)

    gi, gx = lax.axis_index("inline"), lax.axis_index("xline")
    edges = jnp.stack(
        [gi == 0, gi == lax.axis_size("inline") - 1, gx == 0, gx == lax.axis_size("xline") - 1]
    ).astype(jnp.int32)

    theta = (HIGH_BOUND + LOW_BOUND) / 2.0
    delta = (HIGH_BOUND - LOW_BOUND) / 2.0
    sigma = theta / delta
    rho_now = 1.0 / sigma
    til, tiu, txl, txu, diagonal, inverse, direction, partial = pl.pallas_call(
        functools.partial(start_kernel, scale=1.0 / theta),
        out_shape=(grid,) * 7 + (sums,),
        in_specs=[SMEM] + [VMEM] * 14,
        out_specs=(VMEM,) * 8,
        scratch_shapes=[row_scratch],
        compiler_params=PARAMS,
    )(edges, right_side, lateral, accumulation, cellwi, zlow, zup,
      *lateral_halo["inline"], *lateral_halo["xline"], *perforations)

    residual, pressure = right_side, right_side
    for sweep in range(SWEEPS):
        last = sweep + 1 == SWEEPS
        if sweep == 0:
            both, halo = all_sum(jnp.concatenate([partial, storage], axis=0), all_sides(direction))
            total, storage = both[:wells], both[wells:]
        else:
            total, halo = all_sum(partial, all_sides(direction))
        keep = gain = None
        if not last:
            rho_next = 1.0 / (2.0 * sigma - rho_now)
            keep, gain = rho_next * rho_now, 2.0 * rho_next / delta
            rho_now = rho_next
        results = pl.pallas_call(
            functools.partial(sweep_kernel, keep=keep, gain=gain, first=sweep == 0),
            out_shape=(grid, grid) if last else (grid, grid, grid, sums),
            in_specs=[VMEM] * 21,
            out_specs=(VMEM,) * (2 if last else 4),
            scratch_shapes=[row_scratch, col_scratch],
            compiler_params=PARAMS,
        )(residual, direction, pressure, diagonal, inverse, til, tiu, txl, txu, zlow, zup,
          *halo["inline"], *halo["xline"], total, storage, *perforations)
        if last:
            pressure, residual = results
        else:
            pressure, residual, direction, partial = results
    return pressure, residual


def solution(mesh):
    in_specs = (
        P("inline", "xline", None),
        P("inline", "xline", None),
        P(),
        P("inline", "xline", None),
        P("inline", "xline", None),
        P(("inline", "xline")),
        P(("inline", "xline"), None),
        P(("inline", "xline")),
        P(("inline", "xline")),
    )
    out_specs = (P("inline", "xline", None), P("inline", "xline", None))
    return jax.shard_map(body, mesh=mesh, in_specs=in_specs, out_specs=out_specs, check_vma=False)
```

time: 1070 us -> 73.3 us (0.07)
  local copies, waits for them, and re-layouts: 573 us -> 1.74 us
  other arithmetic: 395 us -> 1.06 us
  starting transfers between devices: 78.2 us -> 28.4 us
  Pallas kernels: 0 us -> 17.2 us
    gather x6 -> x0, local copies, waits for them, and re-layouts: 506 us -> none  [the longest x3 482 us: body(): sent = direction.reshape(-1)[send_cell]]
    scatter-add x4 -> x0, other arithmetic: 342 us -> none  [the longest x3 320 us: body(): jnp.zeros((ncell,), jnp.float32).at[send_cell].add(returned).reshape(shape)]
    scatter x4 -> x0, local copies, waits for them, and re-layouts: 63.8 us -> none  [the longest x1 16.4 us: body(): weight_buf = jnp.zeros((slots_total,), jnp.float32).at[slot].set(perf_index)]
    all_to_all x8 -> x0, starting transfers between devices: 45.6 us -> none  [the longest x3 19.6 us: to_owners(): lax.all_to_all(values, ('inline', 'xline'), split_axis=0, concat_axis=0,...]
    ppermute x16 -> x26, waiting for transfers between devices: 0.04 us -> 23.5 us  [xor_permute(): return lax.ppermute(value, axis, [(i, i ^ mask) for i in range(count)])]
    all_to_all x8 -> x0, waiting for transfers between devices: 22.8 us -> none  [the longest x3 14.3 us: from_owners(): lax.all_to_all(values, ('inline', 'xline'), split_axis=0, concat_axis=0,...]
    pallas_call x0 -> x6, Pallas kernels: none -> 17.2 us  [the longest x3 10.5 us: body(): pl.pallas_call(functools.partial(sweep_kernel, keep=keep, gain=gain, firs...]
    sub x3 -> x0, other arithmetic: 16.7 us -> none  [the longest x1 15.8 us: body(): rank_sorted = jnp.arange(n_perf, dtype=jnp.int32) - starts[sorted_owner]]
  transfers between devices with their start and end apart: 24 -> 26, of which waited for: 6 -> 19; matrix products, arithmetic and copies ran while one was open for 67% -> 1% of each run, Pallas kernels for 0% -> 3%
where the time goes in v1:
time: 73.3 us; the launch traced here: 72.8 us
  starting transfers between devices  28.4 us (39%)
  waiting for transfers between devices  23.5 us (32%)
  Pallas kernels  17.2 us (23%)
  local copies, waits for them, and re-layouts  1.74 us (2%)
  other arithmetic  1.06 us (1%)
  between operations  0.97 us (1%)
    ppermute x26, starting transfers between devices, xor_permute(): return lax.ppermute(value, axis, [(i, i ^ mask) for i in range(count)])  28.4 us
    ppermute x26, waiting for transfers between devices, xor_permute(): return lax.ppermute(value, axis, [(i, i ^ mask) for i in range(count)])  23.5 us
    pallas_call x3, Pallas kernels, body(): pl.pallas_call(functools.partial(sweep_kernel, keep=keep, gain=gain, firs...  10.5 us
    pallas_call x1, Pallas kernels, body(): pl.pallas_call(functools.partial(start_kernel, scale=1.0 / theta), out_sh...  3.06 us
    pallas_call x1, Pallas kernels, body(): pl.pallas_call(perforation_kernel, out_shape=(grid, sums, grid, grid), in...  1.98 us
    pallas_call x1, Pallas kernels, body(): pl.pallas_call(lateral_kernel, out_shape=grid, in_specs=[SMEM, VMEM, VMEM...  1.74 us
  transfers between devices with their start and end apart: 26, of which 19 were waited for; matrix products, arithmetic and copies ran while one was open for 1% of the time, Pallas kernels for 3%

profile of v1, /device:TPU:0, one launch (start us, length us, event | category | flops | bytes accessed | tf_op | source)
XLA Modules:
  0.0 72.8 jit_solution(17949690236841480065)
XLA Ops:
  0.7 1.7 %shard_map.104.lateral_ref = f32[8,32,128]{2,1,0:T(8,128)} custom-call(f32[2,8]{1,0:T(2,128)} %table_ref.3, s32[8,32,128]{2,1,0:T(8,128)} %facies_ref.3, f32[8,32,128]{2,1,0:T(8,128)} %thickness_ref.3), custom_call_target="tpu_custom_call" | custom-call | tf_op jit(solution)/shard_map/pallas_call | solution.py:352
  2.4 0.8 %fusion.14 = (f32[8,1,128]{2,1,0:T(1,128)S(1)}, f32[8,1,128]{2,1,0:T(1,128)S(1)}) fusion(f32[8,32,128]{2,1,0:T(8,128)} %shard_map.104.lateral_ref), kind=kLoop, calls=%fused_computation.73 | loop fusion | bytes 16384 | tf_op jit(solution)/shard_map/slice | solution.py:105
  3.2 2.4 %collective-permute-start.3 = (f32[8,128]{1,0:T(8,128)S(1)}, f32[8,128]{1,0:T(8,128)S(1)}, u32[]{:S(2)}, u32[]{:S(2)}) collective-permute-start(f32[8,128]{1,0:T(8,128)S(1)} %get-tuple-element.82), channel_id=1, source_target_pairs={{0,3},{1,2},{2,1},{3,0},{4,7},{5,6},{6,5},{7,4},{8,11},{9,10},{10,... | collective-permute-start | bytes 12296 | tf_op jit(solution)/shard_map/ppermute | solution.py:25
  5.7 1.8 %collective-permute-start.2 = (f32[8,128]{1,0:T(8,128)S(1)}, f32[8,128]{1,0:T(8,128)S(1)}, u32[]{:S(2)}, u32[]{:S(2)}) collective-permute-start(f32[8,128]{1,0:T(8,128)S(1)} %get-tuple-element.82), channel_id=1, source_target_pairs={{0,7},{1,6},{2,5},{3,4},{4,3},{5,2},{6,1},{7,0},{8,15},{9,14},{10,... | collective-permute-start | bytes 12296 | tf_op jit(solution)/shard_map/ppermute | solution.py:25
  7.4 0.0 collective-permute-start.4
  7.4 0.8 %select_bitcast_fusion.7 = (f32[32,128]{1,0:T(8,128)S(1)}, f32[32,128]{1,0:T(8,128)S(1)}) fusion(f32[8,32,128]{2,1,0:T(8,128)} %shard_map.104.lateral_ref, pred[]{:T(512)S(6)} %eq.71), kind=kLoop, calls=%fused_computation.48 | loop fusion | flops 8192 | bytes 65537 | tf_op jit(solution)/shard_map/jit(_where)/select_n | solution.py:99
  8.2 3.6 %collective-permute-start = (f32[32,128]{1,0:T(8,128)S(1)}, f32[32,128]{1,0:T(8,128)S(1)}, u32[]{:S(2)}, u32[]{:S(2)}) collective-permute-start(f32[32,128]{1,0:T(8,128)S(1)} %get-tuple-element.62), channel_id=1, source_target_pairs={{0,24},{8,16},{16,8},{24,0},{1,25},{9,17},{17,9},{25,1},{2,26},{10... | collective-permute-start | bytes 49160 | tf_op jit(solution)/shard_map/ppermute | solution.py:25
  11.8 0.0 collective-permute-start.1
  11.8 0.1 add_convert_fusion.edge_ref
  11.9 0.6 copy-done.6
  12.5 0.0 copy-done.5
  12.5 0.0 copy-done.4
  12.6 2.0 %shard_map.105 = (f32[8,32,128]{2,1,0:T(8,128)S(1)}, f32[40,128]{1,0:T(8,128)S(1)}, f32[8,32,128]{2,1,0:T(8,128)S(1)}, f32[8,32,128]{2,1,0:T(8,128)S(1)}) custom-call(f32[2,8]{1,0:T(2,128)S(1)} %copy-done.9, s32[8,32,128]{2,1,0:T(8,128)S(1)} %copy-done.2, f32[8,32,128]{2,1,0:T(8,128)S(1)} %copy-done.3, s32[1,4096]{1,0:T(1,128)S(1)} %bitcast.42, ...), custom_call_target="tpu_custom_call" | custom-call | tf_op jit(solution)/shard_map/pallas_call | solution.py:356
  14.5 0.0 collective-permute-done.4
  14.6 0.0 collective-permute-done.3
  14.6 0.0 collective-permute-done.2
  14.6 0.0 collective-permute-done
  14.6 0.9 %collective-permute-done.1 = f32[32,128]{1,0:T(8,128)S(1)} collective-permute-done((f32[32,128]{1,0:T(8,128)S(1)}, f32[32,128]{1,0:T(8,128)S(1)}, u32[]{:S(2)}, u32[]{:S(2)}) %collective-permute-start.1) | collective-permute-done | bytes 16416 | tf_op jit(solution)/shard_map/ppermute | solution.py:25
  15.6 3.1 %shard_map.106 = (f32[8,32,128]{2,1,0:T(8,128)S(1)}, f32[8,32,128]{2,1,0:T(8,128)S(1)}, f32[8,32,128]{2,1,0:T(8,128)S(1)}, f32[8,32,128]{2,1,0:T(8,128)S(1)}, f3...) custom-call(s32[4]{0:T(128)S(1)} %add_convert_fusion.edge_ref, ...), custom_call_target="tpu_custom_call" | custom-call | tf_op jit(solution)/shard_map/pallas_call | solution.py:374
  18.6 0.1 copy.13
  18.8 0.1 collective-permute-start.5
  18.8 1.2 %collective-permute-done.5 = f32[88,128]{1,0:T(8,128)S(1)} collective-permute-done((f32[88,128]{1,0:T(8,128)S(1)}, f32[88,128]{1,0:T(8,128)S(1)}, u32[]{:S(2)}, u32[]{:S(2)}) %collective-permute-start.5) | collective-permute-done | bytes 45088 | tf_op jit(solution)/shard_map/ppermute | solution.py:25
  20.1 0.5 collective-permute-start.7
  20.6 1.9 %collective-permute-start.8 = (f32[88,128]{1,0:T(8,128)S(1)}, f32[88,128]{1,0:T(8,128)S(1)}, u32[]{:S(2)}, u32[]{:S(2)}) collective-permute-start(f32[88,128]{1,0:T(8,128)S(1)} %pad_maximum_fusion.3), channel_id=1, source_target_pairs={{0,7},{1,6},{2,5},{3,4},{4,3},{5,2},{6,1},{7,0},{8,15},{9,14},{10,... | collective-permute-start | bytes 135176 | tf_op jit(solution)/shard_map/ppermute | solution.py:25
  22.5 0.8 %collective-permute-start.6 = (f32[88,128]{1,0:T(8,128)S(1)}, f32[88,128]{1,0:T(8,128)S(1)}, u32[]{:S(2)}, u32[]{:S(2)}) collective-permute-start(f32[88,128]{1,0:T(8,128)S(1)} %pad_maximum_fusion.3), channel_id=1, source_target_pairs={{0,3},{1,2},{2,1},{3,0},{4,7},{5,6},{6,5},{7,4},{8,11},{9,10},{10,... | collective-permute-start | bytes 135176 | tf_op jit(solution)/shard_map/ppermute | solution.py:25
  23.3 0.8 %collective-permute-done.7 = f32[80,128]{1,0:T(8,128)S(1)} collective-permute-done((f32[80,128]{1,0:T(8,128)S(1)}, f32[80,128]{1,0:T(8,128)S(1)}, u32[]{:S(2)}, u32[]{:S(2)}) %collective-permute-start.7) | collective-permute-done | bytes 40992 | tf_op jit(solution)/shard_map/ppermute | solution.py:25
  24.1 1.3 %collective-permute-done.8 = f32[88,128]{1,0:T(8,128)S(1)} collective-permute-done((f32[88,128]{1,0:T(8,128)S(1)}, f32[88,128]{1,0:T(8,128)S(1)}, u32[]{:S(2)}, u32[]{:S(2)}) %collective-permute-start.8) | collective-permute-done | bytes 45088 | tf_op jit(solution)/shard_map/ppermute | solution.py:25
  25.3 0.6 collective-permute-done.6
  26.0 0.1 collective-permute-start.11
  26.1 3.5 %collective-permute-start.9 = (f32[112,128]{1,0:T(8,128)S(1)}, f32[112,128]{1,0:T(8,128)S(1)}, u32[]{:S(2)}, u32[]{:S(2)}) collective-permute-start(f32[112,128]{1,0:T(8,128)S(1)} %get-tuple-element.72), channel_id=1, source_target_pairs={{0,24},{8,16},{16,8},{24,0},{1,25},{9,17},{17,9},{25,1},{2,26},{10... | collective-permute-start | bytes 172040 | tf_op jit(solution)/shard_map/ppermute | solution.py:25
  29.6 0.0 collective-permute-start.10
  29.6 3.8 %collective-permute-done.11 = f32[80,128]{1,0:T(8,128)S(1)} collective-permute-done((f32[80,128]{1,0:T(8,128)S(1)}, f32[80,128]{1,0:T(8,128)S(1)}, u32[]{:S(2)}, u32[]{:S(2)}) %collective-permute-start.11) | collective-permute-done | bytes 40992 | tf_op jit(solution)/shard_map/ppermute | solution.py:25
  33.4 1.0 %collective-permute-done.10 = f32[112,128]{1,0:T(8,128)S(1)} collective-permute-done((f32[112,128]{1,0:T(8,128)S(1)}, f32[112,128]{1,0:T(8,128)S(1)}, u32[]{:S(2)}, u32[]{:S(2)}) %collective-permute-start.10) | collective-permute-done | bytes 57376 | tf_op jit(solution)/shard_map/ppermute | solution.py:25
  34.4 4.3 %shard_map.107 = (f32[8,32,128]{2,1,0:T(8,128)S(1)}, f32[8,32,128]{2,1,0:T(8,128)S(1)}, f32[8,32,128]{2,1,0:T(8,128)S(1)}, f32[40,128]{1,0:T(8,128)S(1)}) custom-call(f32[8,32,128]{2,1,0:T(8,128)S(1)} %copy-done, f32[8,32,128]{2,1,0:T(8,128)S(1)} %get-tuple-element.25.direction_ref, f32[8,32,128]{2,1,0:T(8,128)S(1)} %copy-done, ...), custom_call_target="tpu_custom_call" | custom-call | tf_op jit(solution)/shard_map/pallas_call | solution.py:397
  38.7 0.1 copy.15
  38.8 0.1 collective-permute-start.12
  38.9 1.2 %collective-permute-done.12 = f32[48,128]{1,0:T(8,128)S(1)} collective-permute-done((f32[48,128]{1,0:T(8,128)S(1)}, f32[48,128]{1,0:T(8,128)S(1)}, u32[]{:S(2)}, u32[]{:S(2)}) %collective-permute-start.12) | collective-permute-done | bytes 24608 | tf_op jit(solution)/shard_map/ppermute | solution.py:25
  40.1 0.6 collective-permute-start.14
  40.7 1.8 %collective-permute-start.15 = (f32[48,128]{1,0:T(8,128)S(1)}, f32[48,128]{1,0:T(8,128)S(1)}, u32[]{:S(2)}, u32[]{:S(2)}) collective-permute-start(f32[48,128]{1,0:T(8,128)S(1)} %pad_maximum_fusion.9), channel_id=1, source_target_pairs={{0,7},{1,6},{2,5},{3,4},{4,3},{5,2},{6,1},{7,0},{8,15},{9,14},{10,... | collective-permute-start | bytes 73736 | tf_op jit(solution)/shard_map/ppermute | solution.py:25
  42.5 0.8 %collective-permute-start.13 = (f32[48,128]{1,0:T(8,128)S(1)}, f32[48,128]{1,0:T(8,128)S(1)}, u32[]{:S(2)}, u32[]{:S(2)}) collective-permute-start(f32[48,128]{1,0:T(8,128)S(1)} %pad_maximum_fusion.9), channel_id=1, source_target_pairs={{0,3},{1,2},{2,1},{3,0},{4,7},{5,6},{6,5},{7,4},{8,11},{9,10},{10,... | collective-permute-start | bytes 73736 | tf_op jit(solution)/shard_map/ppermute | solution.py:25
  43.3 0.6 collective-permute-done.14
  43.9 1.2 %collective-permute-done.15 = f32[48,128]{1,0:T(8,128)S(1)} collective-permute-done((f32[48,128]{1,0:T(8,128)S(1)}, f32[48,128]{1,0:T(8,128)S(1)}, u32[]{:S(2)}, u32[]{:S(2)}) %collective-permute-start.15) | collective-permute-done | bytes 24608 | tf_op jit(solution)/shard_map/ppermute | solution.py:25
  45.0 0.7 %collective-permute-done.13 = f32[48,128]{1,0:T(8,128)S(1)} collective-permute-done((f32[48,128]{1,0:T(8,128)S(1)}, f32[48,128]{1,0:T(8,128)S(1)}, u32[]{:S(2)}, u32[]{:S(2)}) %collective-permute-start.13) | collective-permute-done | bytes 24608 | tf_op jit(solution)/shard_map/ppermute | solution.py:25
  45.8 0.2 collective-permute-start.18
  46.0 2.7 %collective-permute-start.16 = (f32[72,128]{1,0:T(8,128)S(1)}, f32[72,128]{1,0:T(8,128)S(1)}, u32[]{:S(2)}, u32[]{:S(2)}) collective-permute-start(f32[72,128]{1,0:T(8,128)S(1)} %get-tuple-element.78), channel_id=1, source_target_pairs={{0,24},{8,16},{16,8},{24,0},{1,25},{9,17},{17,9},{25,1},{2,26},{10... | collective-permute-start | bytes 110600 | tf_op jit(solution)/shard_map/ppermute | solution.py:25
  48.8 0.6 collective-permute-start.17
  49.4 2.6 %collective-permute-done.16 = f32[72,128]{1,0:T(8,128)S(1)} collective-permute-done((f32[72,128]{1,0:T(8,128)S(1)}, f32[72,128]{1,0:T(8,128)S(1)}, u32[]{:S(2)}, u32[]{:S(2)}) %collective-permute-start.16) | collective-permute-done | bytes 36896 | tf_op jit(solution)/shard_map/ppermute | solution.py:25
  51.9 0.8 %collective-permute-done.17 = f32[72,128]{1,0:T(8,128)S(1)} collective-permute-done((f32[72,128]{1,0:T(8,128)S(1)}, f32[72,128]{1,0:T(8,128)S(1)}, u32[]{:S(2)}, u32[]{:S(2)}) %collective-permute-start.17) | collective-permute-done | bytes 36896 | tf_op jit(solution)/shard_map/ppermute | solution.py:25
  52.8 4.3 %shard_map.108 = (f32[8,32,128]{2,1,0:T(8,128)S(1)}, f32[8,32,128]{2,1,0:T(8,128)S(1)}, f32[8,32,128]{2,1,0:T(8,128)S(1)}, f32[40,128]{1,0:T(8,128)S(1)}) custom-call(f32[8,32,128]{2,1,0:T(8,128)S(1)} %get-tuple-element.34.residual_ref, f32[8,32,128]{2,1,0:T(8,128)S(1)} %get-tuple-element.35.direction_ref, f32[8,32,128]{2,1,0:T(8,128)S(1)} %get-tuple-element.36.pressure_ref, ...), custom_call_target="tpu_custom_call" | custom-call | tf_op jit(solution)/shard_map/pallas_call | solution.py:397
  57.1 0.1 copy.17
  57.2 0.1 collective-permute-start.19
  57.3 1.2 %collective-permute-done.19 = f32[48,128]{1,0:T(8,128)S(1)} collective-permute-done((f32[48,128]{1,0:T(8,128)S(1)}, f32[48,128]{1,0:T(8,128)S(1)}, u32[]{:S(2)}, u32[]{:S(2)}) %collective-permute-start.19) | collective-permute-done | bytes 24608 | tf_op jit(solution)/shard_map/ppermute | solution.py:25
  58.5 0.7 collective-permute-start.21
  59.2 1.3 %collective-permute-start.22 = (f32[48,128]{1,0:T(8,128)S(1)}, f32[48,128]{1,0:T(8,128)S(1)}, u32[]{:S(2)}, u32[]{:S(2)}) collective-permute-start(f32[48,128]{1,0:T(8,128)S(1)} %pad_maximum_fusion.11), channel_id=1, source_target_pairs={{0,7},{1,6},{2,5},{3,4},{4,3},{5,2},{6,1},{7,0},{8,15},{9,14},{10,... | collective-permute-start | bytes 73736 | tf_op jit(solution)/shard_map/ppermute | solution.py:25
  60.4 1.2 %collective-permute-start.20 = (f32[48,128]{1,0:T(8,128)S(1)}, f32[48,128]{1,0:T(8,128)S(1)}, u32[]{:S(2)}, u32[]{:S(2)}) collective-permute-start(f32[48,128]{1,0:T(8,128)S(1)} %pad_maximum_fusion.11), channel_id=1, source_target_pairs={{0,3},{1,2},{2,1},{3,0},{4,7},{5,6},{6,5},{7,4},{8,11},{9,10},{10,... | collective-permute-start | bytes 73736 | tf_op jit(solution)/shard_map/ppermute | solution.py:25
  61.7 0.6 collective-permute-done.21
  62.2 1.3 %collective-permute-done.22 = f32[48,128]{1,0:T(8,128)S(1)} collective-permute-done((f32[48,128]{1,0:T(8,128)S(1)}, f32[48,128]{1,0:T(8,128)S(1)}, u32[]{:S(2)}, u32[]{:S(2)}) %collective-permute-start.22) | collective-permute-done | bytes 24608 | tf_op jit(solution)/shard_map/ppermute | solution.py:25
  63.5 0.2 collective-permute-done.20
  63.7 0.9 %collective-permute-start.25 = (f32[40,128]{1,0:T(8,128)S(1)}, f32[40,128]{1,0:T(8,128)S(1)}, u32[]{:S(2)}, u32[]{:S(2)}) collective-permute-start(f32[40,128]{1,0:T(8,128)S(1)} %slice_add_fusion.7), channel_id=1, source_target_pairs={{0,16},{8,24},{16,0},{24,8},{1,17},{9,25},{17,1},{25,9},{2,18},{10... | collective-permute-start | bytes 61448 | tf_op jit(solution)/shard_map/ppermute | solution.py:25
  64.6 2.1 %collective-permute-start.23 = (f32[72,128]{1,0:T(8,128)S(1)}, f32[72,128]{1,0:T(8,128)S(1)}, u32[]{:S(2)}, u32[]{:S(2)}) collective-permute-start(f32[72,128]{1,0:T(8,128)S(1)} %get-tuple-element.76), channel_id=1, source_target_pairs={{0,24},{8,16},{16,8},{24,0},{1,25},{9,17},{17,9},{25,1},{2,26},{10... | collective-permute-start | bytes 110600 | tf_op jit(solution)/shard_map/ppermute | solution.py:25
  66.7 0.6 collective-permute-start.24
  67.3 3.2 %collective-permute-done.23 = f32[72,128]{1,0:T(8,128)S(1)} collective-permute-done((f32[72,128]{1,0:T(8,128)S(1)}, f32[72,128]{1,0:T(8,128)S(1)}, u32[]{:S(2)}, u32[]{:S(2)}) %collective-permute-start.23) | collective-permute-done | bytes 36896 | tf_op jit(solution)/shard_map/ppermute | solution.py:25
  70.5 0.4 collective-permute-done.24
  70.9 1.9 %shard_map.109 = (f32[8,32,128]{2,1,0:T(8,128)}, f32[8,32,128]{2,1,0:T(8,128)}) custom-call(f32[8,32,128]{2,1,0:T(8,128)S(1)} %get-tuple-element.38.residual_ref, f32[8,32,128]{2,1,0:T(8,128)S(1)} %get-tuple-element.39.direction_ref, f32[8,32,128]{2,1,0:T(8,128)S(1)} %get-tuple-element.40.pressure_ref, f32[8,32,128]{2,1,0:T(8,128)S(1)} %get-tuple-element.26.diagonal_ref, ...), custom_call_target="tpu_custom_call" | custom-call | tf_op jit(solution)/shard_map/pallas_call | solution.py:397
  (57 shorter events, 0.3 us)
Async XLA Ops:
  0.6 11.3 %copy-start.3 = (f32[8,32,128]{2,1,0:T(8,128)S(1)}, f32[8,32,128]{2,1,0:T(8,128)}, u32[]{:S(2)}) copy-start(f32[8,32,128]{2,1,0:T(8,128)} %thickness_ref.3) | copy-start | bytes 393220
  0.7 11.2 %copy-start.7 = (f32[4096]{0:T(1024)S(1)}, f32[4096]{0:T(1024)}, u32[]{:S(2)}) copy-start(f32[4096]{0:T(1024)} %param.17) | copy-start | bytes 49156
  2.4 9.5 %copy-start.2 = (s32[8,32,128]{2,1,0:T(8,128)S(1)}, s32[8,32,128]{2,1,0:T(8,128)}, u32[]{:S(2)}) copy-start(s32[8,32,128]{2,1,0:T(8,128)} %facies_ref.3) | copy-start | bytes 393220
  3.2 11.3 %collective-permute-start.3 = (f32[8,128]{1,0:T(8,128)S(1)}, f32[8,128]{1,0:T(8,128)S(1)}, u32[]{:S(2)}, u32[]{:S(2)}) collective-permute-start(f32[8,128]{1,0:T(8,128)S(1)} %get-tuple-element.82), channel_id=1, source_target_pairs={{0,3},{1,2},{2,1},{3,0},{4,7},{5,6},{6,5},{7,4},{8,11},{9,10},{10,... | collective-permute-start | bytes 12296 | tf_op jit(solution)/shard_map/ppermute | solution.py:25
  5.7 8.9 %collective-permute-start.2 = (f32[8,128]{1,0:T(8,128)S(1)}, f32[8,128]{1,0:T(8,128)S(1)}, u32[]{:S(2)}, u32[]{:S(2)}) collective-permute-start(f32[8,128]{1,0:T(8,128)S(1)} %get-tuple-element.82), channel_id=1, source_target_pairs={{0,7},{1,6},{2,5},{3,4},{4,3},{5,2},{6,1},{7,0},{8,15},{9,14},{10,... | collective-permute-start | bytes 12296 | tf_op jit(solution)/shard_map/ppermute | solution.py:25
  7.4 7.1 %collective-permute-start.4 = (f32[8,128]{1,0:T(8,128)S(1)}, f32[8,128]{1,0:T(8,128)S(1)}, u32[]{:S(2)}, u32[]{:S(2)}) collective-permute-start(f32[8,128]{1,0:T(8,128)S(1)} %get-tuple-element.83), channel_id=1, source_target_pairs={{0,1},{1,0},{2,3},{3,2},{4,5},{5,4},{6,7},{7,6},{8,9},{9,8},{10,11... | collective-permute-start | bytes 12296 | tf_op jit(solution)/shard_map/ppermute | solution.py:25
  7.4 4.5 %copy-start.9 = (f32[2,8]{1,0:T(2,128)S(1)}, f32[2,8]{1,0:T(2,128)}, u32[]{:S(2)}) copy-start(f32[2,8]{1,0:T(2,128)} %table_ref.3) | copy-start | bytes 196
  8.2 6.4 %collective-permute-start = (f32[32,128]{1,0:T(8,128)S(1)}, f32[32,128]{1,0:T(8,128)S(1)}, u32[]{:S(2)}, u32[]{:S(2)}) collective-permute-start(f32[32,128]{1,0:T(8,128)S(1)} %get-tuple-element.62), channel_id=1, source_target_pairs={{0,24},{8,16},{16,8},{24,0},{1,25},{9,17},{17,9},{25,1},{2,26},{10... | collective-permute-start | bytes 49160 | tf_op jit(solution)/shard_map/ppermute | solution.py:25
  11.8 0.7 copy-start.6
  11.8 3.7 %collective-permute-start.1 = (f32[32,128]{1,0:T(8,128)S(1)}, f32[32,128]{1,0:T(8,128)S(1)}, u32[]{:S(2)}, u32[]{:S(2)}) collective-permute-start(f32[32,128]{1,0:T(8,128)S(1)} %get-tuple-element.63), channel_id=1, source_target_pairs={{0,8},{8,0},{16,24},{24,16},{1,9},{9,1},{17,25},{25,17},{2,10},{10... | collective-permute-start | bytes 49160 | tf_op jit(solution)/shard_map/ppermute | solution.py:25
  11.8 0.7 %copy-start.5 = (s32[4096,1]{0,1:T(1,128)S(1)}, s32[4096,1]{0,1:T(1,128)}, u32[]{:S(2)}) copy-start(s32[4096,1]{0,1:T(1,128)} %param.15) | copy-start | bytes 49156
  11.8 0.7 %copy-start.4 = (s32[4096]{0:T(1024)S(1)}, s32[4096]{0:T(1024)}, u32[]{:S(2)}) copy-start(s32[4096]{0:T(1024)} %param.14) | copy-start | bytes 49156
  12.6 3.0 %copy-start = (f32[8,32,128]{2,1,0:T(8,128)S(1)}, f32[8,32,128]{2,1,0:T(8,128)}, u32[]{:S(2)}) copy-start(f32[8,32,128]{2,1,0:T(8,128)} %pressure_ref.1) | copy-start | bytes 393220
  12.6 3.0 %copy-start.1 = (f32[8,32,128]{2,1,0:T(8,128)S(1)}, f32[8,32,128]{2,1,0:T(8,128)}, u32[]{:S(2)}) copy-start(f32[8,32,128]{2,1,0:T(8,128)} %shard_map.104.lateral_ref) | copy-start | bytes 393220
  12.6 3.0 %copy-start.8 = (f32[8,32,128]{2,1,0:T(8,128)S(1)}, f32[8,32,128]{2,1,0:T(8,128)}, u32[]{:S(2)}) copy-start(f32[8,32,128]{2,1,0:T(8,128)} %accumulation_ref.1) | copy-start | bytes 393220
  18.8 1.3 %collective-permute-start.5 = (f32[88,128]{1,0:T(8,128)S(1)}, f32[88,128]{1,0:T(8,128)S(1)}, u32[]{:S(2)}, u32[]{:S(2)}) collective-permute-start(f32[88,128]{1,0:T(8,128)S(1)} %pad_maximum_fusion.2), channel_id=1, source_target_pairs={{0,1},{1,0},{2,3},{3,2},{4,5},{5,4},{6,7},{7,6},{8,9},{9,8},{10,11... | collective-permute-start | bytes 135176 | tf_op jit(solution)/shard_map/ppermute | solution.py:25
  20.1 4.0 %collective-permute-start.7 = (f32[80,128]{1,0:T(8,128)S(1)}, f32[80,128]{1,0:T(8,128)S(1)}, u32[]{:S(2)}, u32[]{:S(2)}) collective-permute-start(f32[80,128]{1,0:T(8,128)S(1)} %slice_add_fusion.4), channel_id=1, source_target_pairs={{0,4},{1,5},{2,6},{3,7},{4,0},{5,1},{6,2},{7,3},{8,12},{9,13},{10,... | collective-permute-start | bytes 122888 | tf_op jit(solution)/shard_map/ppermute | solution.py:25
  20.6 4.8 %collective-permute-start.8 = (f32[88,128]{1,0:T(8,128)S(1)}, f32[88,128]{1,0:T(8,128)S(1)}, u32[]{:S(2)}, u32[]{:S(2)}) collective-permute-start(f32[88,128]{1,0:T(8,128)S(1)} %pad_maximum_fusion.3), channel_id=1, source_target_pairs={{0,7},{1,6},{2,5},{3,4},{4,3},{5,2},{6,1},{7,0},{8,15},{9,14},{10,... | collective-permute-start | bytes 135176 | tf_op jit(solution)/shard_map/ppermute | solution.py:25
  22.5 3.5 %collective-permute-start.6 = (f32[88,128]{1,0:T(8,128)S(1)}, f32[88,128]{1,0:T(8,128)S(1)}, u32[]{:S(2)}, u32[]{:S(2)}) collective-permute-start(f32[88,128]{1,0:T(8,128)S(1)} %pad_maximum_fusion.3), channel_id=1, source_target_pairs={{0,3},{1,2},{2,1},{3,0},{4,7},{5,6},{6,5},{7,4},{8,11},{9,10},{10,... | collective-permute-start | bytes 135176 | tf_op jit(solution)/shard_map/ppermute | solution.py:25
  26.0 7.4 %collective-permute-start.11 = (f32[80,128]{1,0:T(8,128)S(1)}, f32[80,128]{1,0:T(8,128)S(1)}, u32[]{:S(2)}, u32[]{:S(2)}) collective-permute-start(f32[80,128]{1,0:T(8,128)S(1)} %slice_add_fusion.2), channel_id=1, source_target_pairs={{0,16},{8,24},{16,0},{24,8},{1,17},{9,25},{17,1},{25,9},{2,18},{10... | collective-permute-start | bytes 122888 | tf_op jit(solution)/shard_map/ppermute | solution.py:25
  26.1 7.3 %collective-permute-start.9 = (f32[112,128]{1,0:T(8,128)S(1)}, f32[112,128]{1,0:T(8,128)S(1)}, u32[]{:S(2)}, u32[]{:S(2)}) collective-permute-start(f32[112,128]{1,0:T(8,128)S(1)} %get-tuple-element.72), channel_id=1, source_target_pairs={{0,24},{8,16},{16,8},{24,0},{1,25},{9,17},{17,9},{25,1},{2,26},{10... | collective-permute-start | bytes 172040 | tf_op jit(solution)/shard_map/ppermute | solution.py:25
  29.6 4.8 %collective-permute-start.10 = (f32[112,128]{1,0:T(8,128)S(1)}, f32[112,128]{1,0:T(8,128)S(1)}, u32[]{:S(2)}, u32[]{:S(2)}) collective-permute-start(f32[112,128]{1,0:T(8,128)S(1)} %get-tuple-element.73), channel_id=1, source_target_pairs={{0,8},{8,0},{16,24},{24,16},{1,9},{9,1},{17,25},{25,17},{2,10},{10... | collective-permute-start | bytes 172040 | tf_op jit(solution)/shard_map/ppermute | solution.py:25
  38.8 1.3 %collective-permute-start.12 = (f32[48,128]{1,0:T(8,128)S(1)}, f32[48,128]{1,0:T(8,128)S(1)}, u32[]{:S(2)}, u32[]{:S(2)}) collective-permute-start(f32[48,128]{1,0:T(8,128)S(1)} %pad_maximum_fusion.8), channel_id=1, source_target_pairs={{0,1},{1,0},{2,3},{3,2},{4,5},{5,4},{6,7},{7,6},{8,9},{9,8},{10,11... | collective-permute-start | bytes 73736 | tf_op jit(solution)/shard_map/ppermute | solution.py:25
  40.1 3.8 %collective-permute-start.14 = (f32[40,128]{1,0:T(8,128)S(1)}, f32[40,128]{1,0:T(8,128)S(1)}, u32[]{:S(2)}, u32[]{:S(2)}) collective-permute-start(f32[40,128]{1,0:T(8,128)S(1)} %slice_add_fusion.14), channel_id=1, source_target_pairs={{0,4},{1,5},{2,6},{3,7},{4,0},{5,1},{6,2},{7,3},{8,12},{9,13},{10,... | collective-permute-start | bytes 61448 | tf_op jit(solution)/shard_map/ppermute | solution.py:25
  40.7 4.3 %collective-permute-start.15 = (f32[48,128]{1,0:T(8,128)S(1)}, f32[48,128]{1,0:T(8,128)S(1)}, u32[]{:S(2)}, u32[]{:S(2)}) collective-permute-start(f32[48,128]{1,0:T(8,128)S(1)} %pad_maximum_fusion.9), channel_id=1, source_target_pairs={{0,7},{1,6},{2,5},{3,4},{4,3},{5,2},{6,1},{7,0},{8,15},{9,14},{10,... | collective-permute-start | bytes 73736 | tf_op jit(solution)/shard_map/ppermute | solution.py:25
  42.5 3.3 %collective-permute-start.13 = (f32[48,128]{1,0:T(8,128)S(1)}, f32[48,128]{1,0:T(8,128)S(1)}, u32[]{:S(2)}, u32[]{:S(2)}) collective-permute-start(f32[48,128]{1,0:T(8,128)S(1)} %pad_maximum_fusion.9), channel_id=1, source_target_pairs={{0,3},{1,2},{2,1},{3,0},{4,7},{5,6},{6,5},{7,4},{8,11},{9,10},{10,... | collective-permute-start | bytes 73736 | tf_op jit(solution)/shard_map/ppermute | solution.py:25
  45.8 7.0 %collective-permute-start.18 = (f32[40,128]{1,0:T(8,128)S(1)}, f32[40,128]{1,0:T(8,128)S(1)}, u32[]{:S(2)}, u32[]{:S(2)}) collective-permute-start(f32[40,128]{1,0:T(8,128)S(1)} %slice_add_fusion.12), channel_id=1, source_target_pairs={{0,16},{8,24},{16,0},{24,8},{1,17},{9,25},{17,1},{25,9},{2,18},{10... | collective-permute-start | bytes 61448 | tf_op jit(solution)/shard_map/ppermute | solution.py:25
  46.0 5.9 %collective-permute-start.16 = (f32[72,128]{1,0:T(8,128)S(1)}, f32[72,128]{1,0:T(8,128)S(1)}, u32[]{:S(2)}, u32[]{:S(2)}) collective-permute-start(f32[72,128]{1,0:T(8,128)S(1)} %get-tuple-element.78), channel_id=1, source_target_pairs={{0,24},{8,16},{16,8},{24,0},{1,25},{9,17},{17,9},{25,1},{2,26},{10... | collective-permute-start | bytes 110600 | tf_op jit(solution)/shard_map/ppermute | solution.py:25
  48.8 4.0 %collective-permute-start.17 = (f32[72,128]{1,0:T(8,128)S(1)}, f32[72,128]{1,0:T(8,128)S(1)}, u32[]{:S(2)}, u32[]{:S(2)}) collective-permute-start(f32[72,128]{1,0:T(8,128)S(1)} %get-tuple-element.79), channel_id=1, source_target_pairs={{0,8},{8,0},{16,24},{24,16},{1,9},{9,1},{17,25},{25,17},{2,10},{10... | collective-permute-start | bytes 110600 | tf_op jit(solution)/shard_map/ppermute | solution.py:25
  57.2 1.3 %collective-permute-start.19 = (f32[48,128]{1,0:T(8,128)S(1)}, f32[48,128]{1,0:T(8,128)S(1)}, u32[]{:S(2)}, u32[]{:S(2)}) collective-permute-start(f32[48,128]{1,0:T(8,128)S(1)} %pad_maximum_fusion.10), channel_id=1, source_target_pairs={{0,1},{1,0},{2,3},{3,2},{4,5},{5,4},{6,7},{7,6},{8,9},{9,8},{10,11... | collective-permute-start | bytes 73736 | tf_op jit(solution)/shard_map/ppermute | solution.py:25
  58.5 3.8 %collective-permute-start.21 = (f32[40,128]{1,0:T(8,128)S(1)}, f32[40,128]{1,0:T(8,128)S(1)}, u32[]{:S(2)}, u32[]{:S(2)}) collective-permute-start(f32[40,128]{1,0:T(8,128)S(1)} %slice_add_fusion.9), channel_id=1, source_target_pairs={{0,4},{1,5},{2,6},{3,7},{4,0},{5,1},{6,2},{7,3},{8,12},{9,13},{10,... | collective-permute-start | bytes 61448 | tf_op jit(solution)/shard_map/ppermute | solution.py:25
  59.2 4.3 %collective-permute-start.22 = (f32[48,128]{1,0:T(8,128)S(1)}, f32[48,128]{1,0:T(8,128)S(1)}, u32[]{:S(2)}, u32[]{:S(2)}) collective-permute-start(f32[48,128]{1,0:T(8,128)S(1)} %pad_maximum_fusion.11), channel_id=1, source_target_pairs={{0,7},{1,6},{2,5},{3,4},{4,3},{5,2},{6,1},{7,0},{8,15},{9,14},{10,... | collective-permute-start | bytes 73736 | tf_op jit(solution)/shard_map/ppermute | solution.py:25
  60.4 3.3 %collective-permute-start.20 = (f32[48,128]{1,0:T(8,128)S(1)}, f32[48,128]{1,0:T(8,128)S(1)}, u32[]{:S(2)}, u32[]{:S(2)}) collective-permute-start(f32[48,128]{1,0:T(8,128)S(1)} %pad_maximum_fusion.11), channel_id=1, source_target_pairs={{0,3},{1,2},{2,1},{3,0},{4,7},{5,6},{6,5},{7,4},{8,11},{9,10},{10,... | collective-permute-start | bytes 73736 | tf_op jit(solution)/shard_map/ppermute | solution.py:25
  63.7 7.2 %collective-permute-start.25 = (f32[40,128]{1,0:T(8,128)S(1)}, f32[40,128]{1,0:T(8,128)S(1)}, u32[]{:S(2)}, u32[]{:S(2)}) collective-permute-start(f32[40,128]{1,0:T(8,128)S(1)} %slice_add_fusion.7), channel_id=1, source_target_pairs={{0,16},{8,24},{16,0},{24,8},{1,17},{9,25},{17,1},{25,9},{2,18},{10... | collective-permute-start | bytes 61448 | tf_op jit(solution)/shard_map/ppermute | solution.py:25
  64.6 5.9 %collective-permute-start.23 = (f32[72,128]{1,0:T(8,128)S(1)}, f32[72,128]{1,0:T(8,128)S(1)}, u32[]{:S(2)}, u32[]{:S(2)}) collective-permute-start(f32[72,128]{1,0:T(8,128)S(1)} %get-tuple-element.76), channel_id=1, source_target_pairs={{0,24},{8,16},{16,8},{24,0},{1,25},{9,17},{17,9},{25,1},{2,26},{10... | collective-permute-start | bytes 110600 | tf_op jit(solution)/shard_map/ppermute | solution.py:25
  66.7 4.2 %collective-permute-start.24 = (f32[72,128]{1,0:T(8,128)S(1)}, f32[72,128]{1,0:T(8,128)S(1)}, u32[]{:S(2)}, u32[]{:S(2)}) collective-permute-start(f32[72,128]{1,0:T(8,128)S(1)} %get-tuple-element.77), channel_id=1, source_target_pairs={{0,8},{8,0},{16,24},{24,16},{1,9},{9,1},{17,25},{25,17},{2,10},{10... | collective-permute-start | bytes 110600 | tf_op jit(solution)/shard_map/ppermute | solution.py:25

commit v2 on v1

v2 whole, which is shorter than its diff:
```python
import functools

import jax
import jax.numpy as jnp
from jax import lax
from jax.experimental import pallas as pl
from jax.experimental.pallas import tpu as pltpu
from jax.sharding import PartitionSpec as P

SWEEPS = 3
WELL_DEV = 160
LANES = 128
LOW_BOUND = 0.1
HIGH_BOUND = 2.0
CHUNK = 512
MESH_AXES = ("inline", "xline")

VMEM = pl.BlockSpec(memory_space=pltpu.VMEM)
HBM = pl.BlockSpec(memory_space=pltpu.HBM)
PARAMS = pltpu.CompilerParams(vmem_limit_bytes=16 * 1024 * 1024)
SMALL = pltpu.CompilerParams(vmem_limit_bytes=4 * 1024 * 1024)


def pair_permute(value, partner):
    ni, nx = lax.axis_size("inline"), lax.axis_size("xline")
    pairs = []
    for i in range(ni):
        for j in range(nx):
            i2, j2 = partner(i, j)
            pairs.append((i * nx + j, i2 * nx + j2))
    return lax.ppermute(value, MESH_AXES, pairs)


def xor_permute(value, inline_mask, xline_mask):
    return pair_permute(value, lambda i, j: (i ^ inline_mask, j ^ xline_mask))


def bits_of(count):
    bits = count.bit_length() - 1
    if 1 << bits != count:
        raise ValueError("axis size")
    return bits


def side_masks(count):
    return [(2 << s) - 1 for s in range(bits_of(count))]


def stages_of(count):
    bits = bits_of(count)
    cuts = ([1] if bits % 2 else []) + [2] * (bits // 2)
    stages, low = [], 0
    for width in cuts:
        stages.append([pattern << low | (1 << low) - 1 for pattern in range(1, 1 << width)])
        low += width
    return stages


def all_sum(value, sides):
    arrived = {}
    rows = value.shape[0]
    xa, xb = sides["xline"]
    mates = None
    for masks in stages_of(lax.axis_size("xline")):
        total = value
        for mask in masks:
            if mask == 1:
                got = xor_permute(jnp.concatenate([value, xa, *sides["inline"]], axis=0), 0, mask)
                lines = xa.shape[0]
                arrived["xline", mask] = got[rows : rows + lines]
                mates = jnp.split(got[rows + lines :], 2, axis=0)
            elif mask in side_masks(lax.axis_size("xline")):
                got = xor_permute(jnp.concatenate([value, xb], axis=0), 0, mask)
                arrived["xline", mask] = got[rows:]
            else:
                got = xor_permute(value, 0, mask)
            total = total + got[:rows]
        value = total
    for masks in stages_of(lax.axis_size("inline")):
        total = value
        for mask in masks:
            if mask in side_masks(lax.axis_size("inline")):
                face = mates[0 if mask == 1 else 1]
                got = xor_permute(jnp.concatenate([value, face], axis=0), mask, 1)
                arrived["inline", mask] = got[rows:]
            else:
                got = xor_permute(value, mask, 1)
            total = total + got[:rows]
        value = total
    return value, halos(arrived)


def beyond(index, count):
    other = index - 1 if index % 2 == 0 else index + 1
    return other if 0 <= other < count else None


def side_exchange(sides):
    ni, nx = lax.axis_size("inline"), lax.axis_size("xline")

    def inline_far(i, j):
        other = beyond(i, ni)
        return (i, j ^ 1) if other is None else (other, j)

    def xline_far(i, j):
        other = beyond(j, nx)
        return (i ^ 1, j) if other is None else (i, other)

    return {
        "inline": ordered("inline", xor_permute(sides["inline"][0], 1, 0), pair_permute(sides["inline"][1], inline_far)),
        "xline": ordered("xline", xor_permute(sides["xline"][0], 0, 1), pair_permute(sides["xline"][1], xline_far)),
    }


def ordered(axis, beside, far):
    even = lax.axis_index(axis) % 2 == 0
    return jnp.where(even, far, beside), jnp.where(even, beside, far)


def halos(arrived):
    result = {}
    for axis in MESH_AXES:
        index = lax.axis_index(axis)
        other = jnp.where(index % 2 == 0, index - 1, index + 1)
        far = arrived[axis, 1]
        for mask in side_masks(lax.axis_size(axis))[1:]:
            far = jnp.where((index ^ other) == mask, arrived[axis, mask], far)
        result[axis] = ordered(axis, arrived[axis, 1], far)
    return result


def sides_of(lower, upper, axis):
    even = lax.axis_index(axis) % 2 == 0
    return jnp.where(even, upper, lower), jnp.where(even, lower, upper)


def all_sides(cells):
    return {
        "inline": sides_of(cells[0], cells[-1], "inline"),
        "xline": sides_of(cells[:, 0], cells[:, -1], "xline"),
    }


def harmonic_average(first, second):
    return 2.0 * first * second / (first + second)


def split2(value):
    high = value.astype(jnp.bfloat16)
    low = (value - high.astype(jnp.float32)).astype(jnp.bfloat16)
    return high, low


def stack_split(value):
    return jnp.concatenate(split2(value), axis=0)


def dot_nt(a, b):
    return lax.dot_general(a, b, (((1,), (1,)), ((), ())), preferred_element_type=jnp.float32)


def dot_nn(a, b):
    return lax.dot_general(a, b, (((1,), (0,)), ((), ())), preferred_element_type=jnp.float32)


def halves_sum(both):
    half = both.shape[0] // 2
    return both[:half] + both[half:]


def one_hot(index_row, rows):
    shape = (rows, index_row.shape[1])
    hit = lax.broadcasted_iota(jnp.int32, shape, 0) == index_row
    return jnp.where(hit, 1.0, 0.0).astype(jnp.bfloat16)


def scaled(hot, values):
    rows, count = hot.shape
    tiles = hot.reshape(rows // 16, 16, count)
    pieces = split2(jnp.broadcast_to(values, (16, count)))
    return [(tiles * piece[None]).reshape(rows, count) for piece in pieces]


def picked_sum(hot, values):
    return jnp.sum(hot.astype(jnp.float32) * values, axis=0, keepdims=True)


def parts(count):
    return [pl.ds(start, CHUNK) for start in range(0, count, CHUNK)]


def lookup(facies, table_ref, row):
    result = jnp.full(facies.shape, table_ref[row, 0], jnp.float32)
    for entry in range(1, table_ref.shape[1]):
        result = jnp.where(facies == entry, table_ref[row, entry], result)
    return result


def neighbours(cells, lower, upper, dim):
    if dim == 0:
        return (
            jnp.concatenate([lower[None], cells[:-1]], axis=0),
            jnp.concatenate([cells[1:], upper[None]], axis=0),
        )
    size = cells.shape[1]
    place = lax.broadcasted_iota(jnp.int32, cells.shape, 1)
    return (
        jnp.where(place == 0, lower[:, None], pltpu.roll(cells, 1, 1)),
        jnp.where(place == size - 1, upper[:, None], pltpu.roll(cells, size - 1, 1)),
    )


def layers(cells):
    return pltpu.roll(cells, 1, 2), pltpu.roll(cells, LANES - 1, 2)


def load_kernel(
    table_hbm, facies_hbm, thickness_hbm, right_hbm, accumulation_hbm, cell_hbm, owner_hbm, well_hbm, index_hbm,
    ia_ref, ib_ref, xa_ref, xb_ref, lateral_ref, vertical_ref,
    right_ref, accumulation_ref, cell_ref, number_ref, index_ref,
    table_ref, facies_ref, thickness_ref, owner_ref, well_ref, sems,
):
    copies = [
        pltpu.make_async_copy(source, target, sems.at[slot])
        for slot, (source, target) in enumerate(
            (
                (table_hbm, table_ref), (facies_hbm, facies_ref), (thickness_hbm, thickness_ref),
                (owner_hbm, owner_ref), (well_hbm, well_ref), (right_hbm, right_ref),
                (accumulation_hbm, accumulation_ref), (cell_hbm, cell_ref), (index_hbm, index_ref),
            )
        )
    ]
    for copy in copies:
        copy.start()
    for copy in copies:
        copy.wait()
    facies, thickness = facies_ref[...], thickness_ref[...]
    lateral = lookup(facies, table_ref, 0) * thickness
    lateral_ref[...] = lateral
    vertical_ref[...] = lookup(facies, table_ref, 1) / thickness
    for axis, lower, upper, a_ref, b_ref in (
        ("inline", lateral[0], lateral[-1], ia_ref, ib_ref),
        ("xline", lateral[:, 0], lateral[:, -1], xa_ref, xb_ref),
    ):
        odd = lax.axis_index(axis) % 2 == 1
        a_ref[...] = jnp.where(odd, lower, upper)
        b_ref[...] = jnp.where(odd, upper, lower)
    number_ref[...] = owner_ref[...] * WELL_DEV + well_ref[...]


def perforation_kernel(
    vertical_ref, cell_ref, number_ref, index_ref,
    cellwi_ref, storage_ref, zlow_ref, zup_ref, row_ref, col_ref, wrow_ref, wcol_ref, scaled_ref,
):
    vertical = vertical_ref[...]
    below, above = layers(vertical)
    place = lax.broadcasted_iota(jnp.int32, vertical.shape, 2)
    zlow_ref[...] = jnp.where(place == 0, 0.0, harmonic_average(vertical, below))
    zup_ref[...] = jnp.where(place == LANES - 1, 0.0, harmonic_average(vertical, above))
    for part in parts(cell_ref.shape[1]):
        cell, number = cell_ref[:, part], number_ref[:, part]
        row_ref[:, part] = one_hot(cell >> 7, row_ref.shape[0])
        col_ref[:, part] = one_hot(cell & (LANES - 1), LANES)
        wrow_ref[:, part] = one_hot(number >> 7, wrow_ref.shape[0])
        wcol_ref[:, part] = one_hot(number & (LANES - 1), LANES)
    cellwi_ref[...] = cells_sum(index_ref, row_ref, col_ref, scaled_ref).reshape(cellwi_ref.shape)
    total = 0.0
    for part in parts(cell_ref.shape[1]):
        total = total + wells_sum(index_ref[:, part], wrow_ref, wcol_ref, part)
    storage_ref[...] = total[: storage_ref.shape[0]]


def put_scaled(values, col_ref, scaled_ref, part):
    scaled_ref[0:LANES, part], scaled_ref[LANES:, part] = scaled(col_ref[:, part], values)


def cells_sum(values_ref, row_ref, col_ref, scaled_ref):
    if values_ref is not None:
        for part in parts(row_ref.shape[1]):
            put_scaled(values_ref[:, part], col_ref, scaled_ref, part)
    both = dot_nt(row_ref[...], scaled_ref[...])
    return both[:, :LANES] + both[:, LANES:]


def wells_sum(values, wrow_ref, wcol_ref, part):
    pieces = scaled(wrow_ref[:, part], values)
    return halves_sum(dot_nt(jnp.concatenate(pieces, axis=0), wcol_ref[:, part]))


def perforation_sums(direction, row_ref, col_ref, wrow_ref, wcol_ref, index_ref, wells):
    fieldt = stack_split(direction.reshape(-1, LANES).T)
    total = 0.0
    for part in parts(row_ref.shape[1]):
        values = picked_sum(col_ref[:, part], halves_sum(dot_nn(fieldt, row_ref[:, part])))
        total = total + wells_sum(index_ref[:, part] * values, wrow_ref, wcol_ref, part)
    return total[:wells]


def start_kernel(
    right_ref, lateral_ref, accumulation_ref, cellwi_ref, zlow_ref, zup_ref,
    ilow_ref, iup_ref, xlow_ref, xup_ref, row_ref, col_ref, wrow_ref, wcol_ref, index_ref,
    til_ref, tiu_ref, txl_ref, txu_ref, diagonal_ref, inverse_ref, direction_ref, sums_ref,
    *, scale,
):
    lateral = lateral_ref[...]
    gi, gx = lax.axis_index("inline"), lax.axis_index("xline")
    low, up = neighbours(
        lateral,
        jnp.where(gi == 0, 0.0, ilow_ref[...]),
        jnp.where(gi == lax.axis_size("inline") - 1, 0.0, iup_ref[...]),
        0,
    )
    til, tiu = harmonic_average(lateral, low), harmonic_average(lateral, up)
    low, up = neighbours(
        lateral,
        jnp.where(gx == 0, 0.0, xlow_ref[...]),
        jnp.where(gx == lax.axis_size("xline") - 1, 0.0, xup_ref[...]),
        1,
    )
    txl, txu = harmonic_average(lateral, low), harmonic_average(lateral, up)
    til_ref[...], tiu_ref[...], txl_ref[...], txu_ref[...] = til, tiu, txl, txu
    diagonal = accumulation_ref[...] + til + tiu + txl + txu + zlow_ref[...] + zup_ref[...] + cellwi_ref[...]
    inverse = 1.0 / diagonal
    direction = right_ref[...] * inverse * scale
    diagonal_ref[...] = diagonal
    inverse_ref[...] = inverse
    direction_ref[...] = direction
    sums_ref[...] = perforation_sums(direction, row_ref, col_ref, wrow_ref, wcol_ref, index_ref, sums_ref.shape[0])


def sweep_kernel(
    residual_ref, direction_ref, pressure_ref, diagonal_ref, inverse_ref,
    til_ref, tiu_ref, txl_ref, txu_ref, zlow_ref, zup_ref,
    ilow_ref, iup_ref, xlow_ref, xup_ref, sums_ref, storage_ref,
    row_ref, col_ref, wrow_ref, wcol_ref, index_ref,
    *rest, keep, gain, first,
):
    last = keep is None
    if last:
        next_pressure_ref, next_residual_ref, scaled_ref = rest
    else:
        next_pressure_ref, next_residual_ref, next_direction_ref, next_sums_ref, scaled_ref = rest
    wells = sums_ref.shape[0]
    bottom = sums_ref[...] / (1.0 + storage_ref[...])
    spare = wrow_ref.shape[0] - wells
    if spare:
        bottom = jnp.concatenate([bottom, jnp.zeros((spare, LANES), jnp.float32)], axis=0)
    table = stack_split(bottom)
    for part in parts(row_ref.shape[1]):
        values = picked_sum(wrow_ref[:, part], halves_sum(dot_nn(table, wcol_ref[:, part])))
        put_scaled(index_ref[:, part] * values, col_ref, scaled_ref, part)
    direction = direction_ref[...]
    ilow, iup = neighbours(direction, ilow_ref[...], iup_ref[...], 0)
    xlow, xup = neighbours(direction, xlow_ref[...], xup_ref[...], 1)
    below, above = layers(direction)
    beside = (
        til_ref[...] * ilow + tiu_ref[...] * iup + txl_ref[...] * xlow + txu_ref[...] * xup
        + zlow_ref[...] * below + zup_ref[...] * above
    )
    wells_term = cells_sum(None, row_ref, col_ref, scaled_ref).reshape(direction.shape)
    residual = residual_ref[...] - (diagonal_ref[...] * direction - beside - wells_term)
    next_residual_ref[...] = residual
    if first:
        next_pressure_ref[...] = direction
    else:
        next_pressure_ref[...] = pressure_ref[...] + direction
    if not last:
        following = keep * direction + gain * (residual * inverse_ref[...])
        next_direction_ref[...] = following
        next_sums_ref[...] = perforation_sums(following, row_ref, col_ref, wrow_ref, wcol_ref, index_ref, wells)


def body(
    right_side,
    facies,
    facies_table,
    thickness,
    accumulation,
    perforation_cell,
    perf_owner,
    perf_well,
    perf_index,
):
    shape = right_side.shape
    f32 = jnp.float32
    grid = jax.ShapeDtypeStruct(shape, f32)
    n_perf = perforation_cell.shape[0]
    n_dev = lax.axis_size("inline") * lax.axis_size("xline")
    wells = -(-n_dev * WELL_DEV // (8 * LANES)) * 8
    wells_hot = -(-wells // 16) * 16
    sums = jax.ShapeDtypeStruct((wells, LANES), f32)
    faces = [jax.ShapeDtypeStruct((size, LANES), f32) for size in (shape[1], shape[1], shape[0], shape[0])]
    cell = perforation_cell.reshape(1, n_perf)
    owner = perf_owner.reshape(1, n_perf)
    well = perf_well.reshape(1, n_perf)
    index = perf_index.reshape(1, n_perf)
    rows = shape[0] * shape[1]
    hots = tuple(jax.ShapeDtypeStruct((size, n_perf), jnp.bfloat16) for size in (rows, LANES, wells_hot, LANES))
    scaled_scratch = pltpu.VMEM((2 * LANES, n_perf), jnp.bfloat16)

    row_i32 = jax.ShapeDtypeStruct((1, n_perf), jnp.int32)
    row_f32 = jax.ShapeDtypeStruct((1, n_perf), f32)
    ia, ib, xa, xb, lateral, vertical, right_side, accumulation, cell, number, index = pl.pallas_call(
        load_kernel,
        out_shape=(*faces, grid, grid, grid, grid, row_i32, row_i32, row_f32),
        in_specs=[HBM] * 9,
        out_specs=(VMEM,) * 11,
        scratch_shapes=[
            pltpu.SMEM(facies_table.shape, f32),
            pltpu.VMEM(shape, jnp.int32),
            pltpu.VMEM(shape, f32),
            pltpu.VMEM((1, n_perf), jnp.int32),
            pltpu.VMEM((1, n_perf), jnp.int32),
            pltpu.SemaphoreType.DMA((9,)),
        ],
        compiler_params=SMALL,
    )(*(
        pltpu.with_memory_space_constraint(value, pltpu.HBM)
        for value in (facies_table, facies, thickness, right_side, accumulation, cell, owner, well, index)
    ))
    lateral_halo = side_exchange({"inline": (ia, ib), "xline": (xa, xb)})
    cellwi, storage, zlow, zup, *hot = pl.pallas_call(
        perforation_kernel,
        out_shape=(grid, sums, grid, grid, *hots),
        in_specs=[VMEM] * 4,
        out_specs=(VMEM,) * 8,
        scratch_shapes=[scaled_scratch],
        compiler_params=PARAMS,
    )(vertical, cell, number, index)

    theta = (HIGH_BOUND + LOW_BOUND) / 2.0
    delta = (HIGH_BOUND - LOW_BOUND) / 2.0
    sigma = theta / delta
    rho_now = 1.0 / sigma
    til, tiu, txl, txu, diagonal, inverse, direction, partial = pl.pallas_call(
        functools.partial(start_kernel, scale=1.0 / theta),
        out_shape=(grid,) * 7 + (sums,),
        in_specs=[VMEM] * 15,
        out_specs=(VMEM,) * 8,
        compiler_params=PARAMS,
    )(right_side, lateral, accumulation, cellwi, zlow, zup,
      *lateral_halo["inline"], *lateral_halo["xline"], *hot, index)

    residual, pressure = right_side, right_side
    for sweep in range(SWEEPS):
        last = sweep + 1 == SWEEPS
        if sweep == 0:
            both, halo = all_sum(jnp.concatenate([partial, storage], axis=0), all_sides(direction))
            total, storage = both[:wells], both[wells:]
        else:
            total, halo = all_sum(partial, all_sides(direction))
        keep = gain = None
        if not last:
            rho_next = 1.0 / (2.0 * sigma - rho_now)
            keep, gain = rho_next * rho_now, 2.0 * rho_next / delta
            rho_now = rho_next
        results = pl.pallas_call(
            functools.partial(sweep_kernel, keep=keep, gain=gain, first=sweep == 0),
            out_shape=(grid, grid) if last else (grid, grid, grid, sums),
            in_specs=[VMEM] * 22,
            out_specs=(VMEM,) * (2 if last else 4),
            scratch_shapes=[scaled_scratch],
            compiler_params=PARAMS,
        )(residual, direction, pressure, diagonal, inverse, til, tiu, txl, txu, zlow, zup,
          *halo["inline"], *halo["xline"], total, storage, *hot, index)
        if last:
            pressure, residual = results
        else:
            pressure, residual, direction, partial = results
    return pressure, residual


def solution(mesh):
    in_specs = (
        P("inline", "xline", None),
        P("inline", "xline", None),
        P(),
        P("inline", "xline", None),
        P("inline", "xline", None),
        P(("inline", "xline")),
        P(("inline", "xline"), None),
        P(("inline", "xline")),
        P(("inline", "xline")),
    )
    out_specs = (P("inline", "xline", None), P("inline", "xline", None))
    return jax.shard_map(body, mesh=mesh, in_specs=in_specs, out_specs=out_specs, check_vma=False)
```

time: 73.3 us -> 66.1 us (0.902)
  Pallas kernels: 17.2 us -> 14.3 us
  starting transfers between devices: 28.4 us -> 25.9 us
  local copies, waits for them, and re-layouts: 1.74 us -> 0.27 us
  other arithmetic: 1.06 us -> 0.3 us
    ppermute x26 -> x25, starting transfers between devices: 28.4 us -> 25.9 us  [pair_permute(): return lax.ppermute(value, MESH_AXES, pairs)]
    pallas_call x1, Pallas kernels: 3.06 us -> 1.89 us  [body(): pl.pallas_call(functools.partial(start_kernel, scale=1.0 / theta), out_sh...]
    pallas_call x2, Pallas kernels: 3.71 us -> 2.77 us  [the longest x1 1.41 us: body(): pl.pallas_call(perforation_kernel, out_shape=(grid, sums, grid, grid, *ho...]
    slice x1 -> x0, local copies, waits for them, and re-layouts: 0.82 us -> none  [all_sides(): cells[:, 0]]
    pallas_call x3, Pallas kernels: 10.5 us -> 9.67 us  [body(): pl.pallas_call(functools.partial(sweep_kernel, keep=keep, gain=gain, firs...]
    ppermute x26 -> x25, waiting for transfers between devices: 23.5 us -> 24.2 us  [pair_permute(): return lax.ppermute(value, MESH_AXES, pairs)]
  transfers between devices with their start and end apart: 26 -> 25, of which waited for: 19 -> 20; matrix products, arithmetic and copies ran while one was open for 1% -> 0% of each run, Pallas kernels for 3% -> 2%
where the time goes in v2:
time: 66.1 us; the launch traced here: 65.9 us
  starting transfers between devices  25.9 us (39%)
  waiting for transfers between devices  24.2 us (37%)
  Pallas kernels  14.3 us (22%)
  between operations  0.9 us (1%)
    ppermute x25, starting transfers between devices, pair_permute(): return lax.ppermute(value, MESH_AXES, pairs)  25.9 us
    ppermute x25, waiting for transfers between devices, pair_permute(): return lax.ppermute(value, MESH_AXES, pairs)  24.2 us
    pallas_call x3, Pallas kernels, body(): pl.pallas_call(functools.partial(sweep_kernel, keep=keep, gain=gain, firs...  9.67 us
    pallas_call x1, Pallas kernels, body(): pl.pallas_call(functools.partial(start_kernel, scale=1.0 / theta), out_sh...  1.89 us
    pallas_call x1, Pallas kernels, body(): pl.pallas_call(perforation_kernel, out_shape=(grid, sums, grid, grid, *ho...  1.41 us
    pallas_call x1, Pallas kernels, body(): pl.pallas_call(load_kernel, out_shape=(*faces, grid, grid, grid, grid, ro...  1.36 us
  transfers between devices with their start and end apart: 25, of which 20 were waited for; matrix products, arithmetic and copies ran while one was open for 0% of the time, Pallas kernels for 2%

profile of v2, /device:TPU:0, one launch (start us, length us, event | category | flops | bytes accessed | tf_op | source)
XLA Modules:
  0.0 65.9 jit_solution(6183138519394043185)
XLA Ops:
  0.6 1.4 %shard_map.104 = (f32[32,128]{1,0:T(8,128)S(1)}, f32[32,128]{1,0:T(8,128)S(1)}, f32[8,128]{1,0:T(8,128)S(1)}, f32[8,128]{1,0:T(8,128)S(1)}, f32[8,32,128]{2,1,0:...) custom-call(f32[2,8]{1,0:T(2,128)} %table_hbm.1, ...), custom_call_target="tpu_custom_call" | custom-call | tf_op jit(solution)/shard_map/pallas_call | solution.py:403
  2.0 3.1 %collective-permute-start.2 = (f32[8,128]{1,0:T(8,128)S(1)}, f32[8,128]{1,0:T(8,128)S(1)}, u32[]{:S(2)}, u32[]{:S(2)}) collective-permute-start(f32[8,128]{1,0:T(8,128)S(1)} %get-tuple-element.49), channel_id=1, source_target_pairs={{0,8},{1,2},{2,1},{3,4},{4,3},{5,6},{6,5},{7,15},{8,0},{9,10},{10,... | collective-permute-start | bytes 12296 | tf_op jit(solution)/shard_map/ppermute | solution.py:31
  5.1 0.0 collective-permute-start.3
  5.1 0.5 collective-permute-start
  5.6 2.7 %collective-permute-start.1 = (f32[32,128]{1,0:T(8,128)S(1)}, f32[32,128]{1,0:T(8,128)S(1)}, u32[]{:S(2)}, u32[]{:S(2)}) collective-permute-start(f32[32,128]{1,0:T(8,128)S(1)} %get-tuple-element.48), channel_id=1, source_target_pairs={{0,8},{1,9},{2,10},{3,11},{4,12},{5,13},{6,14},{7,15},{8,0},{9,1},... | collective-permute-start | bytes 49160 | tf_op jit(solution)/shard_map/ppermute | solution.py:31
  8.3 1.4 %shard_map.105 = (f32[8,32,128]{2,1,0:T(8,128)S(1)}, f32[40,128]{1,0:T(8,128)S(1)}, f32[8,32,128]{2,1,0:T(8,128)S(1)}, f32[8,32,128]{2,1,0:T(8,128)S(1)}, bf16[2...) custom-call(f32[8,32,128]{2,1,0:T(8,128)S(1)} %get-tuple-element.40., ...), custom_call_target="tpu_custom_call" | custom-call | tf_op jit(solution)/shard_map/pallas_call | solution.py:422
  9.7 0.0 collective-permute-done.2
  9.7 0.0 collective-permute-done.3
  9.7 0.0 collective-permute-done
  9.7 0.3 collective-permute-done.1
  10.0 1.9 %shard_map.106 = (f32[8,32,128]{2,1,0:T(8,128)S(1)}, f32[8,32,128]{2,1,0:T(8,128)S(1)}, f32[8,32,128]{2,1,0:T(8,128)S(1)}, f32[8,32,128]{2,1,0:T(8,128)S(1)}, f3...) custom-call(f32[8,32,128]{2,1,0:T(8,128)S(1)} %get-tuple-element.37.righ, ...), custom_call_target="tpu_custom_call" | custom-call | tf_op jit(solution)/shard_map/pallas_call | solution.py:435
  11.9 0.1 copy.11
  12.1 0.1 collective-permute-start.4
  12.2 1.2 %collective-permute-done.4 = f32[152,128]{1,0:T(8,128)S(1)} collective-permute-done((f32[152,128]{1,0:T(8,128)S(1)}, f32[152,128]{1,0:T(8,128)S(1)}, u32[]{:S(2)}, u32[]{:S(2)}) %collective-permute-start.4) | collective-permute-done | bytes 77856 | tf_op jit(solution)/shard_map/ppermute | solution.py:31
  13.4 1.3 %collective-permute-start.6 = (f32[80,128]{1,0:T(8,128)S(1)}, f32[80,128]{1,0:T(8,128)S(1)}, u32[]{:S(2)}, u32[]{:S(2)}) collective-permute-start(f32[80,128]{1,0:T(8,128)S(1)} %slice_add_fusion.4), channel_id=1, source_target_pairs={{0,5},{1,4},{2,7},{3,6},{4,1},{5,0},{6,3},{7,2},{8,13},{9,12},{10,... | collective-permute-start | bytes 122888 | tf_op jit(solution)/shard_map/ppermute | solution.py:31
  14.7 1.4 %collective-permute-start.7 = (f32[88,128]{1,0:T(8,128)S(1)}, f32[88,128]{1,0:T(8,128)S(1)}, u32[]{:S(2)}, u32[]{:S(2)}) collective-permute-start(f32[88,128]{1,0:T(8,128)S(1)} %pad_maximum_fusion.4), channel_id=1, source_target_pairs={{0,7},{1,6},{2,5},{3,4},{4,3},{5,2},{6,1},{7,0},{8,15},{9,14},{10,... | collective-permute-start | bytes 135176 | tf_op jit(solution)/shard_map/ppermute | solution.py:31
  16.1 0.3 collective-permute-start.5
  16.4 0.5 collective-permute-done.6
  16.9 2.1 %collective-permute-done.7 = f32[88,128]{1,0:T(8,128)S(1)} collective-permute-done((f32[88,128]{1,0:T(8,128)S(1)}, f32[88,128]{1,0:T(8,128)S(1)}, u32[]{:S(2)}, u32[]{:S(2)}) %collective-permute-start.7) | collective-permute-done | bytes 45088 | tf_op jit(solution)/shard_map/ppermute | solution.py:31
  19.1 0.6 collective-permute-done.5
  19.7 1.8 %collective-permute-start.10 = (f32[80,128]{1,0:T(8,128)S(1)}, f32[80,128]{1,0:T(8,128)S(1)}, u32[]{:S(2)}, u32[]{:S(2)}) collective-permute-start(f32[80,128]{1,0:T(8,128)S(1)} %slice_add_fusion.2), channel_id=1, source_target_pairs={{0,17},{1,16},{2,19},{3,18},{4,21},{5,20},{6,23},{7,22},{8,25},{9,... | collective-permute-start | bytes 122888 | tf_op jit(solution)/shard_map/ppermute | solution.py:31
  21.5 2.5 %collective-permute-start.8 = (f32[112,128]{1,0:T(8,128)S(1)}, f32[112,128]{1,0:T(8,128)S(1)}, u32[]{:S(2)}, u32[]{:S(2)}) collective-permute-start(f32[112,128]{1,0:T(8,128)S(1)} %get-tuple-element.100), channel_id=1, source_target_pairs={{0,25},{1,24},{2,27},{3,26},{4,29},{5,28},{6,31},{7,30},{8,17},{9,... | collective-permute-start | bytes 172040 | tf_op jit(solution)/shard_map/ppermute | solution.py:31
  24.0 0.0 collective-permute-start.9
  24.0 0.2 collective-permute-done.10
  24.2 3.0 %collective-permute-done.8 = f32[112,128]{1,0:T(8,128)S(1)} collective-permute-done((f32[112,128]{1,0:T(8,128)S(1)}, f32[112,128]{1,0:T(8,128)S(1)}, u32[]{:S(2)}, u32[]{:S(2)}) %collective-permute-start.8) | collective-permute-done | bytes 57376 | tf_op jit(solution)/shard_map/ppermute | solution.py:31
  27.2 1.6 %collective-permute-done.9 = f32[112,128]{1,0:T(8,128)S(1)} collective-permute-done((f32[112,128]{1,0:T(8,128)S(1)}, f32[112,128]{1,0:T(8,128)S(1)}, u32[]{:S(2)}, u32[]{:S(2)}) %collective-permute-start.9) | collective-permute-done | bytes 57376 | tf_op jit(solution)/shard_map/ppermute | solution.py:31
  28.9 4.0 %shard_map.107 = (f32[8,32,128]{2,1,0:T(8,128)S(1)}, f32[8,32,128]{2,1,0:T(8,128)S(1)}, f32[8,32,128]{2,1,0:T(8,128)S(1)}, f32[40,128]{1,0:T(8,128)S(1)}) custom-call(f32[8,32,128]{2,1,0:T(8,128)S(1)} %get-tuple-element.37.right_ref.residual_ref.pressure_ref, f32[8,32,128]{2,1,0:T(8,128)S(1)} %get-tuple-element.55.direction_ref, ...), custom_call_target="tpu_custom_call" | custom-call | tf_op jit(solution)/shard_map/pallas_call | solution.py:457
  32.9 0.1 copy.13
  33.0 0.2 collective-permute-start.11
  33.2 1.1 %collective-permute-done.11 = f32[112,128]{1,0:T(8,128)S(1)} collective-permute-done((f32[112,128]{1,0:T(8,128)S(1)}, f32[112,128]{1,0:T(8,128)S(1)}, u32[]{:S(2)}, u32[]{:S(2)}) %collective-permute-start.11) | collective-permute-done | bytes 57376 | tf_op jit(solution)/shard_map/ppermute | solution.py:31
  34.3 0.8 %collective-permute-start.13 = (f32[40,128]{1,0:T(8,128)S(1)}, f32[40,128]{1,0:T(8,128)S(1)}, u32[]{:S(2)}, u32[]{:S(2)}) collective-permute-start(f32[40,128]{1,0:T(8,128)S(1)} %slice_add_fusion.14), channel_id=1, source_target_pairs={{0,5},{1,4},{2,7},{3,6},{4,1},{5,0},{6,3},{7,2},{8,13},{9,12},{10,... | collective-permute-start | bytes 61448 | tf_op jit(solution)/shard_map/ppermute | solution.py:31
  35.1 1.3 %collective-permute-start.14 = (f32[48,128]{1,0:T(8,128)S(1)}, f32[48,128]{1,0:T(8,128)S(1)}, u32[]{:S(2)}, u32[]{:S(2)}) collective-permute-start(f32[48,128]{1,0:T(8,128)S(1)} %pad_maximum_fusion.9), channel_id=1, source_target_pairs={{0,7},{1,6},{2,5},{3,4},{4,3},{5,2},{6,1},{7,0},{8,15},{9,14},{10,... | collective-permute-start | bytes 73736 | tf_op jit(solution)/shard_map/ppermute | solution.py:31
  36.5 0.8 %collective-permute-start.12 = (f32[48,128]{1,0:T(8,128)S(1)}, f32[48,128]{1,0:T(8,128)S(1)}, u32[]{:S(2)}, u32[]{:S(2)}) collective-permute-start(f32[48,128]{1,0:T(8,128)S(1)} %pad_maximum_fusion.9), channel_id=1, source_target_pairs={{0,3},{1,2},{2,1},{3,0},{4,7},{5,6},{6,5},{7,4},{8,11},{9,10},{10,... | collective-permute-start | bytes 73736 | tf_op jit(solution)/shard_map/ppermute | solution.py:31
  37.3 0.2 collective-permute-done.13
  37.5 1.8 %collective-permute-done.14 = f32[48,128]{1,0:T(8,128)S(1)} collective-permute-done((f32[48,128]{1,0:T(8,128)S(1)}, f32[48,128]{1,0:T(8,128)S(1)}, u32[]{:S(2)}, u32[]{:S(2)}) %collective-permute-start.14) | collective-permute-done | bytes 24608 | tf_op jit(solution)/shard_map/ppermute | solution.py:31
  39.3 0.4 collective-permute-done.12
  39.7 0.1 collective-permute-start.17
  39.9 2.3 %collective-permute-start.15 = (f32[72,128]{1,0:T(8,128)S(1)}, f32[72,128]{1,0:T(8,128)S(1)}, u32[]{:S(2)}, u32[]{:S(2)}) collective-permute-start(f32[72,128]{1,0:T(8,128)S(1)} %get-tuple-element.106), channel_id=1, source_target_pairs={{0,25},{1,24},{2,27},{3,26},{4,29},{5,28},{6,31},{7,30},{8,17},{9,... | collective-permute-start | bytes 110600 | tf_op jit(solution)/shard_map/ppermute | solution.py:31
  42.2 0.6 collective-permute-start.16
  42.8 2.4 %collective-permute-done.15 = f32[72,128]{1,0:T(8,128)S(1)} collective-permute-done((f32[72,128]{1,0:T(8,128)S(1)}, f32[72,128]{1,0:T(8,128)S(1)}, u32[]{:S(2)}, u32[]{:S(2)}) %collective-permute-start.15) | collective-permute-done | bytes 36896 | tf_op jit(solution)/shard_map/ppermute | solution.py:31
  45.2 1.1 %collective-permute-done.16 = f32[72,128]{1,0:T(8,128)S(1)} collective-permute-done((f32[72,128]{1,0:T(8,128)S(1)}, f32[72,128]{1,0:T(8,128)S(1)}, u32[]{:S(2)}, u32[]{:S(2)}) %collective-permute-start.16) | collective-permute-done | bytes 36896 | tf_op jit(solution)/shard_map/ppermute | solution.py:31
  46.3 0.0 collective-permute-done.17
  46.4 4.0 %shard_map.108 = (f32[8,32,128]{2,1,0:T(8,128)S(1)}, f32[8,32,128]{2,1,0:T(8,128)S(1)}, f32[8,32,128]{2,1,0:T(8,128)S(1)}, f32[40,128]{1,0:T(8,128)S(1)}) custom-call(f32[8,32,128]{2,1,0:T(8,128)S(1)} %get-tuple-element.64.residual_ref, f32[8,32,128]{2,1,0:T(8,128)S(1)} %get-tuple-element.65.direction_ref, f32[8,32,128]{2,1,0:T(8,128)S(1)} %get-tuple-element.66.pressure_ref, ...), custom_call_target="tpu_custom_call" | custom-call | tf_op jit(solution)/shard_map/pallas_call | solution.py:457
  50.4 0.1 copy.15
  50.5 0.2 collective-permute-start.18
  50.7 1.1 %collective-permute-done.18 = f32[112,128]{1,0:T(8,128)S(1)} collective-permute-done((f32[112,128]{1,0:T(8,128)S(1)}, f32[112,128]{1,0:T(8,128)S(1)}, u32[]{:S(2)}, u32[]{:S(2)}) %collective-permute-start.18) | collective-permute-done | bytes 57376 | tf_op jit(solution)/shard_map/ppermute | solution.py:31
  51.8 0.7 %collective-permute-start.20 = (f32[40,128]{1,0:T(8,128)S(1)}, f32[40,128]{1,0:T(8,128)S(1)}, u32[]{:S(2)}, u32[]{:S(2)}) collective-permute-start(f32[40,128]{1,0:T(8,128)S(1)} %slice_add_fusion.9), channel_id=1, source_target_pairs={{0,5},{1,4},{2,7},{3,6},{4,1},{5,0},{6,3},{7,2},{8,13},{9,12},{10,... | collective-permute-start | bytes 61448 | tf_op jit(solution)/shard_map/ppermute | solution.py:31
  52.5 1.5 %collective-permute-start.21 = (f32[48,128]{1,0:T(8,128)S(1)}, f32[48,128]{1,0:T(8,128)S(1)}, u32[]{:S(2)}, u32[]{:S(2)}) collective-permute-start(f32[48,128]{1,0:T(8,128)S(1)} %pad_maximum_fusion.10), channel_id=1, source_target_pairs={{0,7},{1,6},{2,5},{3,4},{4,3},{5,2},{6,1},{7,0},{8,15},{9,14},{10,... | collective-permute-start | bytes 73736 | tf_op jit(solution)/shard_map/ppermute | solution.py:31
  54.0 0.7 %collective-permute-start.19 = (f32[48,128]{1,0:T(8,128)S(1)}, f32[48,128]{1,0:T(8,128)S(1)}, u32[]{:S(2)}, u32[]{:S(2)}) collective-permute-start(f32[48,128]{1,0:T(8,128)S(1)} %pad_maximum_fusion.10), channel_id=1, source_target_pairs={{0,3},{1,2},{2,1},{3,0},{4,7},{5,6},{6,5},{7,4},{8,11},{9,10},{10,... | collective-permute-start | bytes 73736 | tf_op jit(solution)/shard_map/ppermute | solution.py:31
  54.8 0.2 collective-permute-done.20
  55.0 1.7 %collective-permute-done.21 = f32[48,128]{1,0:T(8,128)S(1)} collective-permute-done((f32[48,128]{1,0:T(8,128)S(1)}, f32[48,128]{1,0:T(8,128)S(1)}, u32[]{:S(2)}, u32[]{:S(2)}) %collective-permute-start.21) | collective-permute-done | bytes 24608 | tf_op jit(solution)/shard_map/ppermute | solution.py:31
  56.7 0.6 collective-permute-done.19
  57.3 0.4 collective-permute-start.24
  57.7 2.1 %collective-permute-start.22 = (f32[72,128]{1,0:T(8,128)S(1)}, f32[72,128]{1,0:T(8,128)S(1)}, u32[]{:S(2)}, u32[]{:S(2)}) collective-permute-start(f32[72,128]{1,0:T(8,128)S(1)} %get-tuple-element.104), channel_id=1, source_target_pairs={{0,25},{1,24},{2,27},{3,26},{4,29},{5,28},{6,31},{7,30},{8,17},{9,... | collective-permute-start | bytes 110600 | tf_op jit(solution)/shard_map/ppermute | solution.py:31
  59.7 0.6 collective-permute-start.23
  60.3 2.7 %collective-permute-done.22 = f32[72,128]{1,0:T(8,128)S(1)} collective-permute-done((f32[72,128]{1,0:T(8,128)S(1)}, f32[72,128]{1,0:T(8,128)S(1)}, u32[]{:S(2)}, u32[]{:S(2)}) %collective-permute-start.22) | collective-permute-done | bytes 36896 | tf_op jit(solution)/shard_map/ppermute | solution.py:31
  63.0 1.1 %collective-permute-done.23 = f32[72,128]{1,0:T(8,128)S(1)} collective-permute-done((f32[72,128]{1,0:T(8,128)S(1)}, f32[72,128]{1,0:T(8,128)S(1)}, u32[]{:S(2)}, u32[]{:S(2)}) %collective-permute-start.23) | collective-permute-done | bytes 36896 | tf_op jit(solution)/shard_map/ppermute | solution.py:31
  64.1 0.0 collective-permute-done.24
  64.1 1.7 %shard_map.109 = (f32[8,32,128]{2,1,0:T(8,128)}, f32[8,32,128]{2,1,0:T(8,128)}) custom-call(f32[8,32,128]{2,1,0:T(8,128)S(1)} %get-tuple-element.68.residual_ref, f32[8,32,128]{2,1,0:T(8,128)S(1)} %get-tuple-element.69.direction_ref, f32[8,32,128]{2,1,0:T(8,128)S(1)} %get-tuple-element.70.pressure_ref, f32[8,32,128]{2,1,0:T(8,128)S(1)} %get-tuple-element.56.diagonal_ref, ...), custom_call_target="tpu_custom_call" | custom-call | tf_op jit(solution)/shard_map/pallas_call | solution.py:457
  (42 shorter events, 0.3 us)
Async XLA Ops:
  2.0 7.7 %collective-permute-start.2 = (f32[8,128]{1,0:T(8,128)S(1)}, f32[8,128]{1,0:T(8,128)S(1)}, u32[]{:S(2)}, u32[]{:S(2)}) collective-permute-start(f32[8,128]{1,0:T(8,128)S(1)} %get-tuple-element.49), channel_id=1, source_target_pairs={{0,8},{1,2},{2,1},{3,4},{4,3},{5,6},{6,5},{7,15},{8,0},{9,10},{10,... | collective-permute-start | bytes 12296 | tf_op jit(solution)/shard_map/ppermute | solution.py:31
  5.1 4.6 %collective-permute-start.3 = (f32[8,128]{1,0:T(8,128)S(1)}, f32[8,128]{1,0:T(8,128)S(1)}, u32[]{:S(2)}, u32[]{:S(2)}) collective-permute-start(f32[8,128]{1,0:T(8,128)S(1)} %get-tuple-element.50), channel_id=1, source_target_pairs={{0,1},{1,0},{2,3},{3,2},{4,5},{5,4},{6,7},{7,6},{8,9},{9,8},{10,11... | collective-permute-start | bytes 12296 | tf_op jit(solution)/shard_map/ppermute | solution.py:31
  5.1 4.6 %collective-permute-start = (f32[32,128]{1,0:T(8,128)S(1)}, f32[32,128]{1,0:T(8,128)S(1)}, u32[]{:S(2)}, u32[]{:S(2)}) collective-permute-start(f32[32,128]{1,0:T(8,128)S(1)} %get-tuple-element.47), channel_id=1, source_target_pairs={{0,1},{1,0},{2,3},{3,2},{4,5},{5,4},{6,7},{7,6},{8,16},{9,17},{10,... | collective-permute-start | bytes 49160 | tf_op jit(solution)/shard_map/ppermute | solution.py:31
  5.6 4.4 %collective-permute-start.1 = (f32[32,128]{1,0:T(8,128)S(1)}, f32[32,128]{1,0:T(8,128)S(1)}, u32[]{:S(2)}, u32[]{:S(2)}) collective-permute-start(f32[32,128]{1,0:T(8,128)S(1)} %get-tuple-element.48), channel_id=1, source_target_pairs={{0,8},{1,9},{2,10},{3,11},{4,12},{5,13},{6,14},{7,15},{8,0},{9,1},... | collective-permute-start | bytes 49160 | tf_op jit(solution)/shard_map/ppermute | solution.py:31
  12.1 1.3 %collective-permute-start.4 = (f32[152,128]{1,0:T(8,128)S(1)}, f32[152,128]{1,0:T(8,128)S(1)}, u32[]{:S(2)}, u32[]{:S(2)}) collective-permute-start(f32[152,128]{1,0:T(8,128)S(1)} %bitcast_dynamic-update-slice_fusion), channel_id=1, source_target_pairs={{0,1},{1,0},{2,3},{3,2},{4,5},{5,4},{6,7},{7,6},{8,9},{9,8},{10,11... | collective-permute-start | bytes 233480 | tf_op jit(solution)/shard_map/ppermute | solution.py:31
  13.4 3.5 %collective-permute-start.6 = (f32[80,128]{1,0:T(8,128)S(1)}, f32[80,128]{1,0:T(8,128)S(1)}, u32[]{:S(2)}, u32[]{:S(2)}) collective-permute-start(f32[80,128]{1,0:T(8,128)S(1)} %slice_add_fusion.4), channel_id=1, source_target_pairs={{0,5},{1,4},{2,7},{3,6},{4,1},{5,0},{6,3},{7,2},{8,13},{9,12},{10,... | collective-permute-start | bytes 122888 | tf_op jit(solution)/shard_map/ppermute | solution.py:31
  14.7 4.4 %collective-permute-start.7 = (f32[88,128]{1,0:T(8,128)S(1)}, f32[88,128]{1,0:T(8,128)S(1)}, u32[]{:S(2)}, u32[]{:S(2)}) collective-permute-start(f32[88,128]{1,0:T(8,128)S(1)} %pad_maximum_fusion.4), channel_id=1, source_target_pairs={{0,7},{1,6},{2,5},{3,4},{4,3},{5,2},{6,1},{7,0},{8,15},{9,14},{10,... | collective-permute-start | bytes 135176 | tf_op jit(solution)/shard_map/ppermute | solution.py:31
  16.1 3.6 %collective-permute-start.5 = (f32[88,128]{1,0:T(8,128)S(1)}, f32[88,128]{1,0:T(8,128)S(1)}, u32[]{:S(2)}, u32[]{:S(2)}) collective-permute-start(f32[88,128]{1,0:T(8,128)S(1)} %pad_maximum_fusion.4), channel_id=1, source_target_pairs={{0,3},{1,2},{2,1},{3,0},{4,7},{5,6},{6,5},{7,4},{8,11},{9,10},{10,... | collective-permute-start | bytes 135176 | tf_op jit(solution)/shard_map/ppermute | solution.py:31
  19.7 4.5 %collective-permute-start.10 = (f32[80,128]{1,0:T(8,128)S(1)}, f32[80,128]{1,0:T(8,128)S(1)}, u32[]{:S(2)}, u32[]{:S(2)}) collective-permute-start(f32[80,128]{1,0:T(8,128)S(1)} %slice_add_fusion.2), channel_id=1, source_target_pairs={{0,17},{1,16},{2,19},{3,18},{4,21},{5,20},{6,23},{7,22},{8,25},{9,... | collective-permute-start | bytes 122888 | tf_op jit(solution)/shard_map/ppermute | solution.py:31
  21.5 5.7 %collective-permute-start.8 = (f32[112,128]{1,0:T(8,128)S(1)}, f32[112,128]{1,0:T(8,128)S(1)}, u32[]{:S(2)}, u32[]{:S(2)}) collective-permute-start(f32[112,128]{1,0:T(8,128)S(1)} %get-tuple-element.100), channel_id=1, source_target_pairs={{0,25},{1,24},{2,27},{3,26},{4,29},{5,28},{6,31},{7,30},{8,17},{9,... | collective-permute-start | bytes 172040 | tf_op jit(solution)/shard_map/ppermute | solution.py:31
  24.0 4.9 %collective-permute-start.9 = (f32[112,128]{1,0:T(8,128)S(1)}, f32[112,128]{1,0:T(8,128)S(1)}, u32[]{:S(2)}, u32[]{:S(2)}) collective-permute-start(f32[112,128]{1,0:T(8,128)S(1)} %get-tuple-element.101), channel_id=1, source_target_pairs={{0,9},{1,8},{2,11},{3,10},{4,13},{5,12},{6,15},{7,14},{8,1},{9,0},... | collective-permute-start | bytes 172040 | tf_op jit(solution)/shard_map/ppermute | solution.py:31
  33.0 1.3 %collective-permute-start.11 = (f32[112,128]{1,0:T(8,128)S(1)}, f32[112,128]{1,0:T(8,128)S(1)}, u32[]{:S(2)}, u32[]{:S(2)}) collective-permute-start(f32[112,128]{1,0:T(8,128)S(1)} %pad_maximum_fusion.2), channel_id=1, source_target_pairs={{0,1},{1,0},{2,3},{3,2},{4,5},{5,4},{6,7},{7,6},{8,9},{9,8},{10,11... | collective-permute-start | bytes 172040 | tf_op jit(solution)/shard_map/ppermute | solution.py:31
  34.3 3.2 %collective-permute-start.13 = (f32[40,128]{1,0:T(8,128)S(1)}, f32[40,128]{1,0:T(8,128)S(1)}, u32[]{:S(2)}, u32[]{:S(2)}) collective-permute-start(f32[40,128]{1,0:T(8,128)S(1)} %slice_add_fusion.14), channel_id=1, source_target_pairs={{0,5},{1,4},{2,7},{3,6},{4,1},{5,0},{6,3},{7,2},{8,13},{9,12},{10,... | collective-permute-start | bytes 61448 | tf_op jit(solution)/shard_map/ppermute | solution.py:31
  35.1 4.2 %collective-permute-start.14 = (f32[48,128]{1,0:T(8,128)S(1)}, f32[48,128]{1,0:T(8,128)S(1)}, u32[]{:S(2)}, u32[]{:S(2)}) collective-permute-start(f32[48,128]{1,0:T(8,128)S(1)} %pad_maximum_fusion.9), channel_id=1, source_target_pairs={{0,7},{1,6},{2,5},{3,4},{4,3},{5,2},{6,1},{7,0},{8,15},{9,14},{10,... | collective-permute-start | bytes 73736 | tf_op jit(solution)/shard_map/ppermute | solution.py:31
  36.5 3.3 %collective-permute-start.12 = (f32[48,128]{1,0:T(8,128)S(1)}, f32[48,128]{1,0:T(8,128)S(1)}, u32[]{:S(2)}, u32[]{:S(2)}) collective-permute-start(f32[48,128]{1,0:T(8,128)S(1)} %pad_maximum_fusion.9), channel_id=1, source_target_pairs={{0,3},{1,2},{2,1},{3,0},{4,7},{5,6},{6,5},{7,4},{8,11},{9,10},{10,... | collective-permute-start | bytes 73736 | tf_op jit(solution)/shard_map/ppermute | solution.py:31
  39.7 6.6 %collective-permute-start.17 = (f32[40,128]{1,0:T(8,128)S(1)}, f32[40,128]{1,0:T(8,128)S(1)}, u32[]{:S(2)}, u32[]{:S(2)}) collective-permute-start(f32[40,128]{1,0:T(8,128)S(1)} %slice_add_fusion.12), channel_id=1, source_target_pairs={{0,17},{1,16},{2,19},{3,18},{4,21},{5,20},{6,23},{7,22},{8,25},{9,... | collective-permute-start | bytes 61448 | tf_op jit(solution)/shard_map/ppermute | solution.py:31
  39.9 5.3 %collective-permute-start.15 = (f32[72,128]{1,0:T(8,128)S(1)}, f32[72,128]{1,0:T(8,128)S(1)}, u32[]{:S(2)}, u32[]{:S(2)}) collective-permute-start(f32[72,128]{1,0:T(8,128)S(1)} %get-tuple-element.106), channel_id=1, source_target_pairs={{0,25},{1,24},{2,27},{3,26},{4,29},{5,28},{6,31},{7,30},{8,17},{9,... | collective-permute-start | bytes 110600 | tf_op jit(solution)/shard_map/ppermute | solution.py:31
  42.2 4.1 %collective-permute-start.16 = (f32[72,128]{1,0:T(8,128)S(1)}, f32[72,128]{1,0:T(8,128)S(1)}, u32[]{:S(2)}, u32[]{:S(2)}) collective-permute-start(f32[72,128]{1,0:T(8,128)S(1)} %get-tuple-element.107), channel_id=1, source_target_pairs={{0,9},{1,8},{2,11},{3,10},{4,13},{5,12},{6,15},{7,14},{8,1},{9,0},... | collective-permute-start | bytes 110600 | tf_op jit(solution)/shard_map/ppermute | solution.py:31
  50.5 1.3 %collective-permute-start.18 = (f32[112,128]{1,0:T(8,128)S(1)}, f32[112,128]{1,0:T(8,128)S(1)}, u32[]{:S(2)}, u32[]{:S(2)}) collective-permute-start(f32[112,128]{1,0:T(8,128)S(1)} %pad_maximum_fusion.3), channel_id=1, source_target_pairs={{0,1},{1,0},{2,3},{3,2},{4,5},{5,4},{6,7},{7,6},{8,9},{9,8},{10,11... | collective-permute-start | bytes 172040 | tf_op jit(solution)/shard_map/ppermute | solution.py:31
  51.8 3.2 %collective-permute-start.20 = (f32[40,128]{1,0:T(8,128)S(1)}, f32[40,128]{1,0:T(8,128)S(1)}, u32[]{:S(2)}, u32[]{:S(2)}) collective-permute-start(f32[40,128]{1,0:T(8,128)S(1)} %slice_add_fusion.9), channel_id=1, source_target_pairs={{0,5},{1,4},{2,7},{3,6},{4,1},{5,0},{6,3},{7,2},{8,13},{9,12},{10,... | collective-permute-start | bytes 61448 | tf_op jit(solution)/shard_map/ppermute | solution.py:31
  52.5 4.2 %collective-permute-start.21 = (f32[48,128]{1,0:T(8,128)S(1)}, f32[48,128]{1,0:T(8,128)S(1)}, u32[]{:S(2)}, u32[]{:S(2)}) collective-permute-start(f32[48,128]{1,0:T(8,128)S(1)} %pad_maximum_fusion.10), channel_id=1, source_target_pairs={{0,7},{1,6},{2,5},{3,4},{4,3},{5,2},{6,1},{7,0},{8,15},{9,14},{10,... | collective-permute-start | bytes 73736 | tf_op jit(solution)/shard_map/ppermute | solution.py:31
  54.0 3.3 %collective-permute-start.19 = (f32[48,128]{1,0:T(8,128)S(1)}, f32[48,128]{1,0:T(8,128)S(1)}, u32[]{:S(2)}, u32[]{:S(2)}) collective-permute-start(f32[48,128]{1,0:T(8,128)S(1)} %pad_maximum_fusion.10), channel_id=1, source_target_pairs={{0,3},{1,2},{2,1},{3,0},{4,7},{5,6},{6,5},{7,4},{8,11},{9,10},{10,... | collective-permute-start | bytes 73736 | tf_op jit(solution)/shard_map/ppermute | solution.py:31
  57.3 6.8 %collective-permute-start.24 = (f32[40,128]{1,0:T(8,128)S(1)}, f32[40,128]{1,0:T(8,128)S(1)}, u32[]{:S(2)}, u32[]{:S(2)}) collective-permute-start(f32[40,128]{1,0:T(8,128)S(1)} %slice_add_fusion.7), channel_id=1, source_target_pairs={{0,17},{1,16},{2,19},{3,18},{4,21},{5,20},{6,23},{7,22},{8,25},{9,... | collective-permute-start | bytes 61448 | tf_op jit(solution)/shard_map/ppermute | solution.py:31
  57.7 5.4 %collective-permute-start.22 = (f32[72,128]{1,0:T(8,128)S(1)}, f32[72,128]{1,0:T(8,128)S(1)}, u32[]{:S(2)}, u32[]{:S(2)}) collective-permute-start(f32[72,128]{1,0:T(8,128)S(1)} %get-tuple-element.104), channel_id=1, source_target_pairs={{0,25},{1,24},{2,27},{3,26},{4,29},{5,28},{6,31},{7,30},{8,17},{9,... | collective-permute-start | bytes 110600 | tf_op jit(solution)/shard_map/ppermute | solution.py:31
  59.7 4.4 %collective-permute-start.23 = (f32[72,128]{1,0:T(8,128)S(1)}, f32[72,128]{1,0:T(8,128)S(1)}, u32[]{:S(2)}, u32[]{:S(2)}) collective-permute-start(f32[72,128]{1,0:T(8,128)S(1)} %get-tuple-element.105), channel_id=1, source_target_pairs={{0,9},{1,8},{2,11},{3,10},{4,13},{5,12},{6,15},{7,14},{8,1},{9,0},... | collective-permute-start | bytes 110600 | tf_op jit(solution)/shard_map/ppermute | solution.py:31

commit v3 on v2

--- a/solution.py
+++ b/solution.py
@@ -56,38 +56,71 @@
     return stages
 
 
+def all_stages():
+    return [[(0, mask) for mask in masks] for masks in stages_of(lax.axis_size("xline"))] + [
+        [(mask, 1) for mask in masks] for masks in stages_of(lax.axis_size("inline"))
+    ]
+
+
+SPLIT_STAGES = [[(0, 1)], [(0, 3), (0, 4), (0, 7)], [(1, 1), (2, 0), (3, 1)]]
+
+
+def exchange_stage(value, stage, riders, arrived):
+    rows = value.shape[0]
+    total = value
+    for masks in stage:
+        rider = riders.get(masks)
+        if rider is None:
+            got = xor_permute(value, *masks)
+        else:
+            got = xor_permute(jnp.concatenate([value, rider], axis=0), *masks)
+            arrived[masks] = got[rows:]
+        total = total + got[:rows]
+    return total
+
+
 def all_sum(value, sides):
+    ni, nx = lax.axis_size("inline"), lax.axis_size("xline")
+    xa, xb = sides["xline"]
+    first, *others = all_stages()
+    split = isinstance(value, tuple)
+    if split:
+        halves = [part.shape[0] for part in value]
+        value = jnp.concatenate(value, axis=0)
+        if len(first) == 1 and [len(stage) for stage in others] == [3, 3] and halves[0] == halves[1]:
+            others = SPLIT_STAGES[1:]
+            two_kinds = True
+        else:
+            two_kinds = False
     arrived = {}
-    rows = value.shape[0]
-    xa, xb = sides["xline"]
-    mates = None
-    for masks in stages_of(lax.axis_size("xline")):
-        total = value
-        for mask in masks:
-            if mask == 1:
-                got = xor_permute(jnp.concatenate([value, xa, *sides["inline"]], axis=0), 0, mask)
-                lines = xa.shape[0]
-                arrived["xline", mask] = got[rows : rows + lines]
-                mates = jnp.split(got[rows + lines :], 2, axis=0)
-            elif mask in side_masks(lax.axis_size("xline")):
-                got = xor_permute(jnp.concatenate([value, xb], axis=0), 0, mask)
-                arrived["xline", mask] = got[rows:]
-            else:
-                got = xor_permute(value, 0, mask)
-            total = total + got[:rows]
-        value = total
-    for masks in stages_of(lax.axis_size("inline")):
-        total = value
-        for mask in masks:
-            if mask in side_masks(lax.axis_size("inline")):
-                face = mates[0 if mask == 1 else 1]
-                got = xor_permute(jnp.concatenate([value, face], axis=0), mask, 1)
-                arrived["inline", mask] = got[rows:]
-            else:
-                got = xor_permute(value, mask, 1)
-            total = total + got[:rows]
-        value = total
-    return value, halos(arrived)
+    riders = {(0, mask): xb for mask in side_masks(nx)}
+    riders[0, 1] = jnp.concatenate([xa, *sides["inline"]], axis=0)
+    value = exchange_stage(value, first, riders, arrived)
+    beside, mate_a, mate_b = jnp.split(
+        arrived[0, 1], [xa.shape[0], xa.shape[0] + sides["inline"][0].shape[0]], axis=0
+    )
+    arrived[0, 1] = beside
+    del riders[0, 1]
+    for mask in side_masks(ni):
+        riders[mask, 1] = mate_a if mask == 1 else mate_b
+    if split and two_kinds:
+        gi, gx = lax.axis_index("inline"), lax.axis_index("xline")
+        kind = (gx ^ (gx >> 1) ^ gi) & 1
+        value = jnp.where(kind == 0, value[: halves[0]], value[halves[0] :])
+    for stage in others:
+        value = exchange_stage(value, stage, riders, arrived)
+    if split:
+        if two_kinds:
+            swapped = xor_permute(value, 0, 1)
+            value = (jnp.where(kind == 0, value, swapped), jnp.where(kind == 0, swapped, value))
+        else:
+            value = (value[: halves[0]], value[halves[0] :])
+    return value, halos(
+        {
+            "inline": {mask: arrived[mask, 1] for mask in side_masks(ni)},
+            "xline": {mask: arrived[0, mask] for mask in side_masks(nx)},
+        }
+    )
 
 
 def beyond(index, count):
@@ -122,10 +155,10 @@
     for axis in MESH_AXES:
         index = lax.axis_index(axis)
         other = jnp.where(index % 2 == 0, index - 1, index + 1)
-        far = arrived[axis, 1]
+        far = arrived[axis][1]
         for mask in side_masks(lax.axis_size(axis))[1:]:
-            far = jnp.where((index ^ other) == mask, arrived[axis, mask], far)
-        result[axis] = ordered(axis, arrived[axis, 1], far)
+            far = jnp.where((index ^ other) == mask, arrived[axis][mask], far)
+        result[axis] = ordered(axis, arrived[axis][1], far)
     return result
 
 
@@ -250,7 +283,7 @@
 
 def perforation_kernel(
     vertical_ref, cell_ref, number_ref, index_ref,
-    cellwi_ref, storage_ref, zlow_ref, zup_ref, row_ref, col_ref, wrow_ref, wcol_ref, scaled_ref,
+    cellwi_ref, storage_ref, zlow_ref, zup_ref, row_ref, col_ref, wrow_ref, wcol_ref, scaled_ref, wscaled_ref,
 ):
     vertical = vertical_ref[...]
     below, above = layers(vertical)
@@ -264,10 +297,9 @@
         wrow_ref[:, part] = one_hot(number >> 7, wrow_ref.shape[0])
         wcol_ref[:, part] = one_hot(number & (LANES - 1), LANES)
     cellwi_ref[...] = cells_sum(index_ref, row_ref, col_ref, scaled_ref).reshape(cellwi_ref.shape)
-    total = 0.0
     for part in parts(cell_ref.shape[1]):
-        total = total + wells_sum(index_ref[:, part], wrow_ref, wcol_ref, part)
-    storage_ref[...] = total[: storage_ref.shape[0]]
+        put_wells(index_ref[:, part], wrow_ref, wscaled_ref, part)
+    storage_ref[...] = wells_sum(wscaled_ref, wcol_ref, storage_ref.shape[0])
 
 
 def put_scaled(values, col_ref, scaled_ref, part):
@@ -282,24 +314,27 @@
     return both[:, :LANES] + both[:, LANES:]
 
 
-def wells_sum(values, wrow_ref, wcol_ref, part):
-    pieces = scaled(wrow_ref[:, part], values)
-    return halves_sum(dot_nt(jnp.concatenate(pieces, axis=0), wcol_ref[:, part]))
-
-
-def perforation_sums(direction, row_ref, col_ref, wrow_ref, wcol_ref, index_ref, wells):
+def put_wells(values, wrow_ref, wscaled_ref, part):
+    rows = wrow_ref.shape[0]
+    wscaled_ref[0:rows, part], wscaled_ref[rows:, part] = scaled(wrow_ref[:, part], values)
+
+
+def wells_sum(wscaled_ref, wcol_ref, wells):
+    return halves_sum(dot_nt(wscaled_ref[...], wcol_ref[...]))[:wells]
+
+
+def perforation_sums(direction, row_ref, col_ref, wrow_ref, wcol_ref, index_ref, wscaled_ref, wells):
     fieldt = stack_split(direction.reshape(-1, LANES).T)
-    total = 0.0
     for part in parts(row_ref.shape[1]):
         values = picked_sum(col_ref[:, part], halves_sum(dot_nn(fieldt, row_ref[:, part])))
-        total = total + wells_sum(index_ref[:, part] * values, wrow_ref, wcol_ref, part)
-    return total[:wells]
+        put_wells(index_ref[:, part] * values, wrow_ref, wscaled_ref, part)
+    return wells_sum(wscaled_ref, wcol_ref, wells)
 
 
 def start_kernel(
     right_ref, lateral_ref, accumulation_ref, cellwi_ref, zlow_ref, zup_ref,
     ilow_ref, iup_ref, xlow_ref, xup_ref, row_ref, col_ref, wrow_ref, wcol_ref, index_ref,
-    til_ref, tiu_ref, txl_ref, txu_ref, diagonal_ref, inverse_ref, direction_ref, sums_ref,
+    til_ref, tiu_ref, txl_ref, txu_ref, diagonal_ref, inverse_ref, direction_ref, sums_ref, wscaled_ref,
     *, scale,
 ):
     lateral = lateral_ref[...]
@@ -325,7 +360,7 @@
     diagonal_ref[...] = diagonal
     inverse_ref[...] = inverse
     direction_ref[...] = direction
-    sums_ref[...] = perforation_sums(direction, row_ref, col_ref, wrow_ref, wcol_ref, index_ref, sums_ref.shape[0])
+    sums_ref[...] = perforation_sums(direction, row_ref, col_ref, wrow_ref, wcol_ref, index_ref, wscaled_ref, sums_ref.shape[0])
 
 
 def sweep_kernel(
@@ -339,7 +374,7 @@
     if last:
         next_pressure_ref, next_residual_ref, scaled_ref = rest
     else:
-        next_pressure_ref, next_residual_ref, next_direction_ref, next_sums_ref, scaled_ref = rest
+        next_pressure_ref, next_residual_ref, next_direction_ref, next_sums_ref, scaled_ref, wscaled_ref = rest
     wells = sums_ref.shape[0]
     bottom = sums_ref[...] / (1.0 + storage_ref[...])
     spare = wrow_ref.shape[0] - wells
@@ -367,7 +402,9 @@
     if not last:
         following = keep * direction + gain * (residual * inverse_ref[...])
         next_direction_ref[...] = following
-        next_sums_ref[...] = perforation_sums(following, row_ref, col_ref, wrow_ref, wcol_ref, index_ref, wells)
+        next_sums_ref[...] = perforation_sums(
+            following, row_ref, col_ref, wrow_ref, wcol_ref, index_ref, wscaled_ref, wells
+        )
 
 
 def body(
@@ -397,6 +434,7 @@
     rows = shape[0] * shape[1]
     hots = tuple(jax.ShapeDtypeStruct((size, n_perf), jnp.bfloat16) for size in (rows, LANES, wells_hot, LANES))
     scaled_scratch = pltpu.VMEM((2 * LANES, n_perf), jnp.bfloat16)
+    wscaled_scratch = pltpu.VMEM((2 * wells_hot, n_perf), jnp.bfloat16)
 
     row_i32 = jax.ShapeDtypeStruct((1, n_perf), jnp.int32)
     row_f32 = jax.ShapeDtypeStruct((1, n_perf), f32)
@@ -424,7 +462,7 @@
         out_shape=(grid, sums, grid, grid, *hots),
         in_specs=[VMEM] * 4,
         out_specs=(VMEM,) * 8,
-        scratch_shapes=[scaled_scratch],
+        scratch_shapes=[scaled_scratch, wscaled_scratch],
         compiler_params=PARAMS,
     )(vertical, cell, number, index)
 
@@ -437,6 +475,7 @@
         out_shape=(grid,) * 7 + (sums,),
         in_specs=[VMEM] * 15,
         out_specs=(VMEM,) * 8,
+        scratch_shapes=[wscaled_scratch],
         compiler_params=PARAMS,
     )(right_side, lateral, accumulation, cellwi, zlow, zup,
       *lateral_halo["inline"], *lateral_halo["xline"], *hot, index)
@@ -445,8 +484,7 @@
     for sweep in range(SWEEPS):
         last = sweep + 1 == SWEEPS
         if sweep == 0:
-            both, halo = all_sum(jnp.concatenate([partial, storage], axis=0), all_sides(direction))
-            total, storage = both[:wells], both[wells:]
+            (total, storage), halo = all_sum((partial, storage), all_sides(direction))
         else:
             total, halo = all_sum(partial, all_sides(direction))
         keep = gain = None
@@ -459,7 +497,7 @@
             out_shape=(grid, grid) if last else (grid, grid, grid, sums),
             in_specs=[VMEM] * 22,
             out_specs=(VMEM,) * (2 if last else 4),
-            scratch_shapes=[scaled_scratch],
+            scratch_shapes=[scaled_scratch] if last else [scaled_scratch, wscaled_scratch],
             compiler_params=PARAMS,
         )(residual, direction, pressure, diagonal, inverse, til, tiu, txl, txu, zlow, zup,
           *halo["inline"], *halo["xline"], total, storage, *hot, index)

time: 66.1 us -> 63.6 us (0.962)
  Pallas kernels: 14.3 us -> 12 us
  waiting for transfers between devices: 24.2 us -> 23.3 us
  starting transfers between devices: 25.9 us -> 26.7 us
    pallas_call x3, Pallas kernels: 9.67 us -> 7.91 us  [body(): pl.pallas_call(functools.partial(sweep_kernel, keep=keep, gain=gain, firs...]
    ppermute x25 -> x26, waiting for transfers between devices: 24.2 us -> 23.3 us  [pair_permute(): return lax.ppermute(value, MESH_AXES, pairs)]
    ppermute x25 -> x26, starting transfers between devices: 25.9 us -> 26.7 us  [pair_permute(): return lax.ppermute(value, MESH_AXES, pairs)]
  transfers between devices with their start and end apart: 25 -> 26, of which waited for: 20 -> 20; matrix products, arithmetic and copies ran while one was open for 0% -> 0% of each run, Pallas kernels for 2% -> 2%
where the time goes in v3:
time: 63.6 us; the launch traced here: 63.4 us
  starting transfers between devices  26.7 us (42%)
  waiting for transfers between devices  23.3 us (37%)
  Pallas kernels  12 us (19%)
  between operations  0.9 us (1%)
    ppermute x26, starting transfers between devices, pair_permute(): return lax.ppermute(value, MESH_AXES, pairs)  26.7 us
    ppermute x26, waiting for transfers between devices, pair_permute(): return lax.ppermute(value, MESH_AXES, pairs)  23.3 us
    pallas_call x3, Pallas kernels, body(): pl.pallas_call(functools.partial(sweep_kernel, keep=keep, gain=gain, firs...  7.91 us
    pallas_call x1, Pallas kernels, body(): pl.pallas_call(perforation_kernel, out_shape=(grid, sums, grid, grid, *ho...  1.41 us
    pallas_call x1, Pallas kernels, body(): pl.pallas_call(load_kernel, out_shape=(*faces, grid, grid, grid, grid, ro...  1.36 us
    pallas_call x1, Pallas kernels, body(): pl.pallas_call(functools.partial(start_kernel, scale=1.0 / theta), out_sh...  1.34 us
  transfers between devices with their start and end apart: 26, of which 20 were waited for; matrix products, arithmetic and copies ran while one was open for 0% of the time, Pallas kernels for 2%

profile of v3, /device:TPU:0, one launch (start us, length us, event | category | flops | bytes accessed | tf_op | source)
XLA Modules:
  0.0 63.4 jit_solution(14374616857731334655)
XLA Ops:
  0.6 1.4 %shard_map.104 = (f32[32,128]{1,0:T(8,128)S(1)}, f32[32,128]{1,0:T(8,128)S(1)}, f32[8,128]{1,0:T(8,128)S(1)}, f32[8,128]{1,0:T(8,128)S(1)}, f32[8,32,128]{2,1,0:...) custom-call(f32[2,8]{1,0:T(2,128)} %table_hbm.1, ...), custom_call_target="tpu_custom_call" | custom-call | tf_op jit(solution)/shard_map/pallas_call | solution.py:441
  2.0 3.1 %collective-permute-start.2 = (f32[8,128]{1,0:T(8,128)S(1)}, f32[8,128]{1,0:T(8,128)S(1)}, u32[]{:S(2)}, u32[]{:S(2)}) collective-permute-start(f32[8,128]{1,0:T(8,128)S(1)} %get-tuple-element.49), channel_id=1, source_target_pairs={{0,8},{1,2},{2,1},{3,4},{4,3},{5,6},{6,5},{7,15},{8,0},{9,10},{10,... | collective-permute-start | bytes 12296 | tf_op jit(solution)/shard_map/ppermute | solution.py:31
  5.1 0.0 collective-permute-start.3
  5.1 0.5 collective-permute-start
  5.6 2.7 %collective-permute-start.1 = (f32[32,128]{1,0:T(8,128)S(1)}, f32[32,128]{1,0:T(8,128)S(1)}, u32[]{:S(2)}, u32[]{:S(2)}) collective-permute-start(f32[32,128]{1,0:T(8,128)S(1)} %get-tuple-element.48), channel_id=1, source_target_pairs={{0,8},{1,9},{2,10},{3,11},{4,12},{5,13},{6,14},{7,15},{8,0},{9,1},... | collective-permute-start | bytes 49160 | tf_op jit(solution)/shard_map/ppermute | solution.py:31
  8.3 1.4 %shard_map.105 = (f32[8,32,128]{2,1,0:T(8,128)S(1)}, f32[40,128]{1,0:T(8,128)S(1)}, f32[8,32,128]{2,1,0:T(8,128)S(1)}, f32[8,32,128]{2,1,0:T(8,128)S(1)}, bf16[2...) custom-call(f32[8,32,128]{2,1,0:T(8,128)S(1)} %get-tuple-element.40., ...), custom_call_target="tpu_custom_call" | custom-call | tf_op jit(solution)/shard_map/pallas_call | solution.py:460
  9.7 0.0 collective-permute-done.2
  9.7 0.0 collective-permute-done.3
  9.7 0.0 collective-permute-done
  9.7 0.3 collective-permute-done.1
  10.0 1.3 %shard_map.106 = (f32[8,32,128]{2,1,0:T(8,128)S(1)}, f32[8,32,128]{2,1,0:T(8,128)S(1)}, f32[8,32,128]{2,1,0:T(8,128)S(1)}, f32[8,32,128]{2,1,0:T(8,128)S(1)}, f3...) custom-call(f32[8,32,128]{2,1,0:T(8,128)S(1)} %get-tuple-element.37.righ, ...), custom_call_target="tpu_custom_call" | custom-call | tf_op jit(solution)/shard_map/pallas_call | solution.py:473
  11.4 0.1 copy.11
  11.5 0.1 collective-permute-start.4
  11.6 1.2 %collective-permute-done.4 = f32[152,128]{1,0:T(8,128)S(1)} collective-permute-done((f32[152,128]{1,0:T(8,128)S(1)}, f32[152,128]{1,0:T(8,128)S(1)}, u32[]{:S(2)}, u32[]{:S(2)}) %collective-permute-start.4) | collective-permute-done | bytes 77856 | tf_op jit(solution)/shard_map/ppermute | solution.py:31
  12.9 1.6 %collective-permute-start.6 = (f32[40,128]{1,0:T(8,128)S(1)}, f32[40,128]{1,0:T(8,128)S(1)}, u32[]{:S(2)}, u32[]{:S(2)}) collective-permute-start(f32[40,128]{1,0:T(8,128)S(1)} %slice_select_fusion), channel_id=1, source_target_pairs={{0,4},{1,5},{2,6},{3,7},{4,0},{5,1},{6,2},{7,3},{8,12},{9,13},{10,... | collective-permute-start | bytes 61448 | tf_op jit(solution)/shard_map/ppermute | solution.py:31
  14.5 0.9 %collective-permute-start.7 = (f32[48,128]{1,0:T(8,128)S(1)}, f32[48,128]{1,0:T(8,128)S(1)}, u32[]{:S(2)}, u32[]{:S(2)}) collective-permute-start(f32[48,128]{1,0:T(8,128)S(1)} %pad_maximum_fusion.8), channel_id=1, source_target_pairs={{0,7},{1,6},{2,5},{3,4},{4,3},{5,2},{6,1},{7,0},{8,15},{9,14},{10,... | collective-permute-start | bytes 73736 | tf_op jit(solution)/shard_map/ppermute | solution.py:31
  15.4 0.8 %collective-permute-start.5 = (f32[48,128]{1,0:T(8,128)S(1)}, f32[48,128]{1,0:T(8,128)S(1)}, u32[]{:S(2)}, u32[]{:S(2)}) collective-permute-start(f32[48,128]{1,0:T(8,128)S(1)} %pad_maximum_fusion.8), channel_id=1, source_target_pairs={{0,3},{1,2},{2,1},{3,0},{4,7},{5,6},{6,5},{7,4},{8,11},{9,10},{10,... | collective-permute-start | bytes 73736 | tf_op jit(solution)/shard_map/ppermute | solution.py:31
  16.2 0.6 collective-permute-done.6
  16.7 2.1 %collective-permute-done.7 = f32[48,128]{1,0:T(8,128)S(1)} collective-permute-done((f32[48,128]{1,0:T(8,128)S(1)}, f32[48,128]{1,0:T(8,128)S(1)}, u32[]{:S(2)}, u32[]{:S(2)}) %collective-permute-start.7) | collective-permute-done | bytes 24608 | tf_op jit(solution)/shard_map/ppermute | solution.py:31
  18.8 0.0 collective-permute-done.5
  18.8 2.0 %collective-permute-start.10 = (f32[40,128]{1,0:T(8,128)S(1)}, f32[40,128]{1,0:T(8,128)S(1)}, u32[]{:S(2)}, u32[]{:S(2)}) collective-permute-start(f32[40,128]{1,0:T(8,128)S(1)} %slice_add_fusion.13), channel_id=1, source_target_pairs={{0,16},{1,17},{2,18},{3,19},{4,20},{5,21},{6,22},{7,23},{8,24},{9,... | collective-permute-start | bytes 61448 | tf_op jit(solution)/shard_map/ppermute | solution.py:31
  20.8 2.2 %collective-permute-start.8 = (f32[72,128]{1,0:T(8,128)S(1)}, f32[72,128]{1,0:T(8,128)S(1)}, u32[]{:S(2)}, u32[]{:S(2)}) collective-permute-start(f32[72,128]{1,0:T(8,128)S(1)} %get-tuple-element.106), channel_id=1, source_target_pairs={{0,25},{1,24},{2,27},{3,26},{4,29},{5,28},{6,31},{7,30},{8,17},{9,... | collective-permute-start | bytes 110600 | tf_op jit(solution)/shard_map/ppermute | solution.py:31
  23.1 0.0 collective-permute-start.9
  23.1 0.5 collective-permute-done.10
  23.6 2.5 %collective-permute-done.8 = f32[72,128]{1,0:T(8,128)S(1)} collective-permute-done((f32[72,128]{1,0:T(8,128)S(1)}, f32[72,128]{1,0:T(8,128)S(1)}, u32[]{:S(2)}, u32[]{:S(2)}) %collective-permute-start.8) | collective-permute-done | bytes 36896 | tf_op jit(solution)/shard_map/ppermute | solution.py:31
  26.0 0.9 %collective-permute-done.9 = f32[72,128]{1,0:T(8,128)S(1)} collective-permute-done((f32[72,128]{1,0:T(8,128)S(1)}, f32[72,128]{1,0:T(8,128)S(1)}, u32[]{:S(2)}, u32[]{:S(2)}) %collective-permute-start.9) | collective-permute-done | bytes 36896 | tf_op jit(solution)/shard_map/ppermute | solution.py:31
  26.9 0.2 collective-permute-start.11
  27.1 1.1 %collective-permute-done.11 = f32[40,128]{1,0:T(8,128)S(1)} collective-permute-done((f32[40,128]{1,0:T(8,128)S(1)}, f32[40,128]{1,0:T(8,128)S(1)}, u32[]{:S(2)}, u32[]{:S(2)}) %collective-permute-start.11) | collective-permute-done | bytes 20512 | tf_op jit(solution)/shard_map/ppermute | solution.py:31
  28.2 3.1 %shard_map.107 = (f32[8,32,128]{2,1,0:T(8,128)S(1)}, f32[8,32,128]{2,1,0:T(8,128)S(1)}, f32[8,32,128]{2,1,0:T(8,128)S(1)}, f32[40,128]{1,0:T(8,128)S(1)}) custom-call(f32[8,32,128]{2,1,0:T(8,128)S(1)} %get-tuple-element.37.right_ref.residual_ref.pressure_ref, f32[8,32,128]{2,1,0:T(8,128)S(1)} %get-tuple-element.55.direction_ref, ...), custom_call_target="tpu_custom_call" | custom-call | tf_op jit(solution)/shard_map/pallas_call | solution.py:495
  31.3 0.1 copy.13
  31.4 0.2 collective-permute-start.12
  31.6 1.1 %collective-permute-done.12 = f32[112,128]{1,0:T(8,128)S(1)} collective-permute-done((f32[112,128]{1,0:T(8,128)S(1)}, f32[112,128]{1,0:T(8,128)S(1)}, u32[]{:S(2)}, u32[]{:S(2)}) %collective-permute-start.12) | collective-permute-done | bytes 57376 | tf_op jit(solution)/shard_map/ppermute | solution.py:31
  32.7 0.8 %collective-permute-start.14 = (f32[40,128]{1,0:T(8,128)S(1)}, f32[40,128]{1,0:T(8,128)S(1)}, u32[]{:S(2)}, u32[]{:S(2)}) collective-permute-start(f32[40,128]{1,0:T(8,128)S(1)} %slice_add_fusion.10), channel_id=1, source_target_pairs={{0,5},{1,4},{2,7},{3,6},{4,1},{5,0},{6,3},{7,2},{8,13},{9,12},{10,... | collective-permute-start | bytes 61448 | tf_op jit(solution)/shard_map/ppermute | solution.py:31
  33.6 1.1 %collective-permute-start.15 = (f32[48,128]{1,0:T(8,128)S(1)}, f32[48,128]{1,0:T(8,128)S(1)}, u32[]{:S(2)}, u32[]{:S(2)}) collective-permute-start(f32[48,128]{1,0:T(8,128)S(1)} %pad_maximum_fusion.9), channel_id=1, source_target_pairs={{0,7},{1,6},{2,5},{3,4},{4,3},{5,2},{6,1},{7,0},{8,15},{9,14},{10,... | collective-permute-start | bytes 73736 | tf_op jit(solution)/shard_map/ppermute | solution.py:31
  34.7 1.0 %collective-permute-start.13 = (f32[48,128]{1,0:T(8,128)S(1)}, f32[48,128]{1,0:T(8,128)S(1)}, u32[]{:S(2)}, u32[]{:S(2)}) collective-permute-start(f32[48,128]{1,0:T(8,128)S(1)} %pad_maximum_fusion.9), channel_id=1, source_target_pairs={{0,3},{1,2},{2,1},{3,0},{4,7},{5,6},{6,5},{7,4},{8,11},{9,10},{10,... | collective-permute-start | bytes 73736 | tf_op jit(solution)/shard_map/ppermute | solution.py:31
  35.7 0.2 collective-permute-done.14
  35.9 1.8 %collective-permute-done.15 = f32[48,128]{1,0:T(8,128)S(1)} collective-permute-done((f32[48,128]{1,0:T(8,128)S(1)}, f32[48,128]{1,0:T(8,128)S(1)}, u32[]{:S(2)}, u32[]{:S(2)}) %collective-permute-start.15) | collective-permute-done | bytes 24608 | tf_op jit(solution)/shard_map/ppermute | solution.py:31
  37.7 0.3 collective-permute-done.13
  38.0 0.6 %collective-permute-start.18 = (f32[40,128]{1,0:T(8,128)S(1)}, f32[40,128]{1,0:T(8,128)S(1)}, u32[]{:S(2)}, u32[]{:S(2)}) collective-permute-start(f32[40,128]{1,0:T(8,128)S(1)} %slice_add_fusion.8), channel_id=1, source_target_pairs={{0,17},{1,16},{2,19},{3,18},{4,21},{5,20},{6,23},{7,22},{8,25},{9,... | collective-permute-start | bytes 61448 | tf_op jit(solution)/shard_map/ppermute | solution.py:31
  38.7 2.6 %collective-permute-start.16 = (f32[72,128]{1,0:T(8,128)S(1)}, f32[72,128]{1,0:T(8,128)S(1)}, u32[]{:S(2)}, u32[]{:S(2)}) collective-permute-start(f32[72,128]{1,0:T(8,128)S(1)} %get-tuple-element.104), channel_id=1, source_target_pairs={{0,25},{1,24},{2,27},{3,26},{4,29},{5,28},{6,31},{7,30},{8,17},{9,... | collective-permute-start | bytes 110600 | tf_op jit(solution)/shard_map/ppermute | solution.py:31
  41.3 0.0 collective-permute-start.17
  41.3 2.6 %collective-permute-done.16 = f32[72,128]{1,0:T(8,128)S(1)} collective-permute-done((f32[72,128]{1,0:T(8,128)S(1)}, f32[72,128]{1,0:T(8,128)S(1)}, u32[]{:S(2)}, u32[]{:S(2)}) %collective-permute-start.16) | collective-permute-done | bytes 36896 | tf_op jit(solution)/shard_map/ppermute | solution.py:31
  43.9 1.1 %collective-permute-done.17 = f32[72,128]{1,0:T(8,128)S(1)} collective-permute-done((f32[72,128]{1,0:T(8,128)S(1)}, f32[72,128]{1,0:T(8,128)S(1)}, u32[]{:S(2)}, u32[]{:S(2)}) %collective-permute-start.17) | collective-permute-done | bytes 36896 | tf_op jit(solution)/shard_map/ppermute | solution.py:31
  45.0 0.0 collective-permute-done.18
  45.0 3.1 %shard_map.108 = (f32[8,32,128]{2,1,0:T(8,128)S(1)}, f32[8,32,128]{2,1,0:T(8,128)S(1)}, f32[8,32,128]{2,1,0:T(8,128)S(1)}, f32[40,128]{1,0:T(8,128)S(1)}) custom-call(f32[8,32,128]{2,1,0:T(8,128)S(1)} %get-tuple-element.64.residual_ref, f32[8,32,128]{2,1,0:T(8,128)S(1)} %get-tuple-element.65.direction_ref, f32[8,32,128]{2,1,0:T(8,128)S(1)} %get-tuple-element.66.pressure_ref, ...), custom_call_target="tpu_custom_call" | custom-call | tf_op jit(solution)/shard_map/pallas_call | solution.py:495
  48.1 0.1 copy.15
  48.3 0.2 collective-permute-start.19
  48.4 1.1 %collective-permute-done.19 = f32[112,128]{1,0:T(8,128)S(1)} collective-permute-done((f32[112,128]{1,0:T(8,128)S(1)}, f32[112,128]{1,0:T(8,128)S(1)}, u32[]{:S(2)}, u32[]{:S(2)}) %collective-permute-start.19) | collective-permute-done | bytes 57376 | tf_op jit(solution)/shard_map/ppermute | solution.py:31
  49.6 0.7 %collective-permute-start.21 = (f32[40,128]{1,0:T(8,128)S(1)}, f32[40,128]{1,0:T(8,128)S(1)}, u32[]{:S(2)}, u32[]{:S(2)}) collective-permute-start(f32[40,128]{1,0:T(8,128)S(1)} %slice_add_fusion.5), channel_id=1, source_target_pairs={{0,5},{1,4},{2,7},{3,6},{4,1},{5,0},{6,3},{7,2},{8,13},{9,12},{10,... | collective-permute-start | bytes 61448 | tf_op jit(solution)/shard_map/ppermute | solution.py:31
  50.3 1.4 %collective-permute-start.22 = (f32[48,128]{1,0:T(8,128)S(1)}, f32[48,128]{1,0:T(8,128)S(1)}, u32[]{:S(2)}, u32[]{:S(2)}) collective-permute-start(f32[48,128]{1,0:T(8,128)S(1)} %pad_maximum_fusion.10), channel_id=1, source_target_pairs={{0,7},{1,6},{2,5},{3,4},{4,3},{5,2},{6,1},{7,0},{8,15},{9,14},{10,... | collective-permute-start | bytes 73736 | tf_op jit(solution)/shard_map/ppermute | solution.py:31
  51.6 0.9 %collective-permute-start.20 = (f32[48,128]{1,0:T(8,128)S(1)}, f32[48,128]{1,0:T(8,128)S(1)}, u32[]{:S(2)}, u32[]{:S(2)}) collective-permute-start(f32[48,128]{1,0:T(8,128)S(1)} %pad_maximum_fusion.10), channel_id=1, source_target_pairs={{0,3},{1,2},{2,1},{3,0},{4,7},{5,6},{6,5},{7,4},{8,11},{9,10},{10,... | collective-permute-start | bytes 73736 | tf_op jit(solution)/shard_map/ppermute | solution.py:31
  52.6 0.2 collective-permute-done.21
  52.8 1.6 %collective-permute-done.22 = f32[48,128]{1,0:T(8,128)S(1)} collective-permute-done((f32[48,128]{1,0:T(8,128)S(1)}, f32[48,128]{1,0:T(8,128)S(1)}, u32[]{:S(2)}, u32[]{:S(2)}) %collective-permute-start.22) | collective-permute-done | bytes 24608 | tf_op jit(solution)/shard_map/ppermute | solution.py:31
  54.4 0.5 collective-permute-done.20
  54.9 0.3 collective-permute-start.25
  55.2 2.2 %collective-permute-start.23 = (f32[72,128]{1,0:T(8,128)S(1)}, f32[72,128]{1,0:T(8,128)S(1)}, u32[]{:S(2)}, u32[]{:S(2)}) collective-permute-start(f32[72,128]{1,0:T(8,128)S(1)} %get-tuple-element.102), channel_id=1, source_target_pairs={{0,25},{1,24},{2,27},{3,26},{4,29},{5,28},{6,31},{7,30},{8,17},{9,... | collective-permute-start | bytes 110600 | tf_op jit(solution)/shard_map/ppermute | solution.py:31
  57.5 0.5 collective-permute-start.24
  57.9 2.6 %collective-permute-done.23 = f32[72,128]{1,0:T(8,128)S(1)} collective-permute-done((f32[72,128]{1,0:T(8,128)S(1)}, f32[72,128]{1,0:T(8,128)S(1)}, u32[]{:S(2)}, u32[]{:S(2)}) %collective-permute-start.23) | collective-permute-done | bytes 36896 | tf_op jit(solution)/shard_map/ppermute | solution.py:31
  60.5 1.1 %collective-permute-done.24 = f32[72,128]{1,0:T(8,128)S(1)} collective-permute-done((f32[72,128]{1,0:T(8,128)S(1)}, f32[72,128]{1,0:T(8,128)S(1)}, u32[]{:S(2)}, u32[]{:S(2)}) %collective-permute-start.24) | collective-permute-done | bytes 36896 | tf_op jit(solution)/shard_map/ppermute | solution.py:31
  61.7 0.0 collective-permute-done.25
  61.7 1.7 %shard_map.109 = (f32[8,32,128]{2,1,0:T(8,128)}, f32[8,32,128]{2,1,0:T(8,128)}) custom-call(f32[8,32,128]{2,1,0:T(8,128)S(1)} %get-tuple-element.68.residual_ref, f32[8,32,128]{2,1,0:T(8,128)S(1)} %get-tuple-element.69.direction_ref, f32[8,32,128]{2,1,0:T(8,128)S(1)} %get-tuple-element.70.pressure_ref, f32[8,32,128]{2,1,0:T(8,128)S(1)} %get-tuple-element.56.diagonal_ref, ...), custom_call_target="tpu_custom_call" | custom-call | tf_op jit(solution)/shard_map/pallas_call | solution.py:495
  (43 shorter events, 0.3 us)
Async XLA Ops:
  2.0 7.7 %collective-permute-start.2 = (f32[8,128]{1,0:T(8,128)S(1)}, f32[8,128]{1,0:T(8,128)S(1)}, u32[]{:S(2)}, u32[]{:S(2)}) collective-permute-start(f32[8,128]{1,0:T(8,128)S(1)} %get-tuple-element.49), channel_id=1, source_target_pairs={{0,8},{1,2},{2,1},{3,4},{4,3},{5,6},{6,5},{7,15},{8,0},{9,10},{10,... | collective-permute-start | bytes 12296 | tf_op jit(solution)/shard_map/ppermute | solution.py:31
  5.1 4.6 %collective-permute-start.3 = (f32[8,128]{1,0:T(8,128)S(1)}, f32[8,128]{1,0:T(8,128)S(1)}, u32[]{:S(2)}, u32[]{:S(2)}) collective-permute-start(f32[8,128]{1,0:T(8,128)S(1)} %get-tuple-element.50), channel_id=1, source_target_pairs={{0,1},{1,0},{2,3},{3,2},{4,5},{5,4},{6,7},{7,6},{8,9},{9,8},{10,11... | collective-permute-start | bytes 12296 | tf_op jit(solution)/shard_map/ppermute | solution.py:31
  5.1 4.6 %collective-permute-start = (f32[32,128]{1,0:T(8,128)S(1)}, f32[32,128]{1,0:T(8,128)S(1)}, u32[]{:S(2)}, u32[]{:S(2)}) collective-permute-start(f32[32,128]{1,0:T(8,128)S(1)} %get-tuple-element.47), channel_id=1, source_target_pairs={{0,1},{1,0},{2,3},{3,2},{4,5},{5,4},{6,7},{7,6},{8,16},{9,17},{10,... | collective-permute-start | bytes 49160 | tf_op jit(solution)/shard_map/ppermute | solution.py:31
  5.6 4.4 %collective-permute-start.1 = (f32[32,128]{1,0:T(8,128)S(1)}, f32[32,128]{1,0:T(8,128)S(1)}, u32[]{:S(2)}, u32[]{:S(2)}) collective-permute-start(f32[32,128]{1,0:T(8,128)S(1)} %get-tuple-element.48), channel_id=1, source_target_pairs={{0,8},{1,9},{2,10},{3,11},{4,12},{5,13},{6,14},{7,15},{8,0},{9,1},... | collective-permute-start | bytes 49160 | tf_op jit(solution)/shard_map/ppermute | solution.py:31
  11.5 1.3 %collective-permute-start.4 = (f32[152,128]{1,0:T(8,128)S(1)}, f32[152,128]{1,0:T(8,128)S(1)}, u32[]{:S(2)}, u32[]{:S(2)}) collective-permute-start(f32[152,128]{1,0:T(8,128)S(1)} %bitcast_dynamic-update-slice_fusion), channel_id=1, source_target_pairs={{0,1},{1,0},{2,3},{3,2},{4,5},{5,4},{6,7},{7,6},{8,9},{9,8},{10,11... | collective-permute-start | bytes 233480 | tf_op jit(solution)/shard_map/ppermute | solution.py:31
  12.9 3.8 %collective-permute-start.6 = (f32[40,128]{1,0:T(8,128)S(1)}, f32[40,128]{1,0:T(8,128)S(1)}, u32[]{:S(2)}, u32[]{:S(2)}) collective-permute-start(f32[40,128]{1,0:T(8,128)S(1)} %slice_select_fusion), channel_id=1, source_target_pairs={{0,4},{1,5},{2,6},{3,7},{4,0},{5,1},{6,2},{7,3},{8,12},{9,13},{10,... | collective-permute-start | bytes 61448 | tf_op jit(solution)/shard_map/ppermute | solution.py:31
  14.5 4.4 %collective-permute-start.7 = (f32[48,128]{1,0:T(8,128)S(1)}, f32[48,128]{1,0:T(8,128)S(1)}, u32[]{:S(2)}, u32[]{:S(2)}) collective-permute-start(f32[48,128]{1,0:T(8,128)S(1)} %pad_maximum_fusion.8), channel_id=1, source_target_pairs={{0,7},{1,6},{2,5},{3,4},{4,3},{5,2},{6,1},{7,0},{8,15},{9,14},{10,... | collective-permute-start | bytes 73736 | tf_op jit(solution)/shard_map/ppermute | solution.py:31
  15.4 3.4 %collective-permute-start.5 = (f32[48,128]{1,0:T(8,128)S(1)}, f32[48,128]{1,0:T(8,128)S(1)}, u32[]{:S(2)}, u32[]{:S(2)}) collective-permute-start(f32[48,128]{1,0:T(8,128)S(1)} %pad_maximum_fusion.8), channel_id=1, source_target_pairs={{0,3},{1,2},{2,1},{3,0},{4,7},{5,6},{6,5},{7,4},{8,11},{9,10},{10,... | collective-permute-start | bytes 73736 | tf_op jit(solution)/shard_map/ppermute | solution.py:31
  18.8 4.7 %collective-permute-start.10 = (f32[40,128]{1,0:T(8,128)S(1)}, f32[40,128]{1,0:T(8,128)S(1)}, u32[]{:S(2)}, u32[]{:S(2)}) collective-permute-start(f32[40,128]{1,0:T(8,128)S(1)} %slice_add_fusion.13), channel_id=1, source_target_pairs={{0,16},{1,17},{2,18},{3,19},{4,20},{5,21},{6,22},{7,23},{8,24},{9,... | collective-permute-start | bytes 61448 | tf_op jit(solution)/shard_map/ppermute | solution.py:31
  20.8 5.2 %collective-permute-start.8 = (f32[72,128]{1,0:T(8,128)S(1)}, f32[72,128]{1,0:T(8,128)S(1)}, u32[]{:S(2)}, u32[]{:S(2)}) collective-permute-start(f32[72,128]{1,0:T(8,128)S(1)} %get-tuple-element.106), channel_id=1, source_target_pairs={{0,25},{1,24},{2,27},{3,26},{4,29},{5,28},{6,31},{7,30},{8,17},{9,... | collective-permute-start | bytes 110600 | tf_op jit(solution)/shard_map/ppermute | solution.py:31
  23.1 3.9 %collective-permute-start.9 = (f32[72,128]{1,0:T(8,128)S(1)}, f32[72,128]{1,0:T(8,128)S(1)}, u32[]{:S(2)}, u32[]{:S(2)}) collective-permute-start(f32[72,128]{1,0:T(8,128)S(1)} %get-tuple-element.107), channel_id=1, source_target_pairs={{0,9},{1,8},{2,11},{3,10},{4,13},{5,12},{6,15},{7,14},{8,1},{9,0},... | collective-permute-start | bytes 110600 | tf_op jit(solution)/shard_map/ppermute | solution.py:31
  26.9 1.3 %collective-permute-start.11 = (f32[40,128]{1,0:T(8,128)S(1)}, f32[40,128]{1,0:T(8,128)S(1)}, u32[]{:S(2)}, u32[]{:S(2)}) collective-permute-start(f32[40,128]{1,0:T(8,128)S(1)} %slice_add_fusion.11), channel_id=1, source_target_pairs={{0,1},{1,0},{2,3},{3,2},{4,5},{5,4},{6,7},{7,6},{8,9},{9,8},{10,11... | collective-permute-start | bytes 61448 | tf_op jit(solution)/shard_map/ppermute | solution.py:31
  31.4 1.3 %collective-permute-start.12 = (f32[112,128]{1,0:T(8,128)S(1)}, f32[112,128]{1,0:T(8,128)S(1)}, u32[]{:S(2)}, u32[]{:S(2)}) collective-permute-start(f32[112,128]{1,0:T(8,128)S(1)} %pad_maximum_fusion), channel_id=1, source_target_pairs={{0,1},{1,0},{2,3},{3,2},{4,5},{5,4},{6,7},{7,6},{8,9},{9,8},{10,11... | collective-permute-start | bytes 172040 | tf_op jit(solution)/shard_map/ppermute | solution.py:31
  32.7 3.2 %collective-permute-start.14 = (f32[40,128]{1,0:T(8,128)S(1)}, f32[40,128]{1,0:T(8,128)S(1)}, u32[]{:S(2)}, u32[]{:S(2)}) collective-permute-start(f32[40,128]{1,0:T(8,128)S(1)} %slice_add_fusion.10), channel_id=1, source_target_pairs={{0,5},{1,4},{2,7},{3,6},{4,1},{5,0},{6,3},{7,2},{8,13},{9,12},{10,... | collective-permute-start | bytes 61448 | tf_op jit(solution)/shard_map/ppermute | solution.py:31
  33.6 4.2 %collective-permute-start.15 = (f32[48,128]{1,0:T(8,128)S(1)}, f32[48,128]{1,0:T(8,128)S(1)}, u32[]{:S(2)}, u32[]{:S(2)}) collective-permute-start(f32[48,128]{1,0:T(8,128)S(1)} %pad_maximum_fusion.9), channel_id=1, source_target_pairs={{0,7},{1,6},{2,5},{3,4},{4,3},{5,2},{6,1},{7,0},{8,15},{9,14},{10,... | collective-permute-start | bytes 73736 | tf_op jit(solution)/shard_map/ppermute | solution.py:31
  34.7 3.3 %collective-permute-start.13 = (f32[48,128]{1,0:T(8,128)S(1)}, f32[48,128]{1,0:T(8,128)S(1)}, u32[]{:S(2)}, u32[]{:S(2)}) collective-permute-start(f32[48,128]{1,0:T(8,128)S(1)} %pad_maximum_fusion.9), channel_id=1, source_target_pairs={{0,3},{1,2},{2,1},{3,0},{4,7},{5,6},{6,5},{7,4},{8,11},{9,10},{10,... | collective-permute-start | bytes 73736 | tf_op jit(solution)/shard_map/ppermute | solution.py:31
  38.0 7.0 %collective-permute-start.18 = (f32[40,128]{1,0:T(8,128)S(1)}, f32[40,128]{1,0:T(8,128)S(1)}, u32[]{:S(2)}, u32[]{:S(2)}) collective-permute-start(f32[40,128]{1,0:T(8,128)S(1)} %slice_add_fusion.8), channel_id=1, source_target_pairs={{0,17},{1,16},{2,19},{3,18},{4,21},{5,20},{6,23},{7,22},{8,25},{9,... | collective-permute-start | bytes 61448 | tf_op jit(solution)/shard_map/ppermute | solution.py:31
  38.7 5.2 %collective-permute-start.16 = (f32[72,128]{1,0:T(8,128)S(1)}, f32[72,128]{1,0:T(8,128)S(1)}, u32[]{:S(2)}, u32[]{:S(2)}) collective-permute-start(f32[72,128]{1,0:T(8,128)S(1)} %get-tuple-element.104), channel_id=1, source_target_pairs={{0,25},{1,24},{2,27},{3,26},{4,29},{5,28},{6,31},{7,30},{8,17},{9,... | collective-permute-start | bytes 110600 | tf_op jit(solution)/shard_map/ppermute | solution.py:31
  41.3 3.7 %collective-permute-start.17 = (f32[72,128]{1,0:T(8,128)S(1)}, f32[72,128]{1,0:T(8,128)S(1)}, u32[]{:S(2)}, u32[]{:S(2)}) collective-permute-start(f32[72,128]{1,0:T(8,128)S(1)} %get-tuple-element.105), channel_id=1, source_target_pairs={{0,9},{1,8},{2,11},{3,10},{4,13},{5,12},{6,15},{7,14},{8,1},{9,0},... | collective-permute-start | bytes 110600 | tf_op jit(solution)/shard_map/ppermute | solution.py:31
  48.3 1.3 %collective-permute-start.19 = (f32[112,128]{1,0:T(8,128)S(1)}, f32[112,128]{1,0:T(8,128)S(1)}, u32[]{:S(2)}, u32[]{:S(2)}) collective-permute-start(f32[112,128]{1,0:T(8,128)S(1)} %pad_maximum_fusion.1), channel_id=1, source_target_pairs={{0,1},{1,0},{2,3},{3,2},{4,5},{5,4},{6,7},{7,6},{8,9},{9,8},{10,11... | collective-permute-start | bytes 172040 | tf_op jit(solution)/shard_map/ppermute | solution.py:31
  49.6 3.2 %collective-permute-start.21 = (f32[40,128]{1,0:T(8,128)S(1)}, f32[40,128]{1,0:T(8,128)S(1)}, u32[]{:S(2)}, u32[]{:S(2)}) collective-permute-start(f32[40,128]{1,0:T(8,128)S(1)} %slice_add_fusion.5), channel_id=1, source_target_pairs={{0,5},{1,4},{2,7},{3,6},{4,1},{5,0},{6,3},{7,2},{8,13},{9,12},{10,... | collective-permute-start | bytes 61448 | tf_op jit(solution)/shard_map/ppermute | solution.py:31
  50.3 4.2 %collective-permute-start.22 = (f32[48,128]{1,0:T(8,128)S(1)}, f32[48,128]{1,0:T(8,128)S(1)}, u32[]{:S(2)}, u32[]{:S(2)}) collective-permute-start(f32[48,128]{1,0:T(8,128)S(1)} %pad_maximum_fusion.10), channel_id=1, source_target_pairs={{0,7},{1,6},{2,5},{3,4},{4,3},{5,2},{6,1},{7,0},{8,15},{9,14},{10,... | collective-permute-start | bytes 73736 | tf_op jit(solution)/shard_map/ppermute | solution.py:31
  51.6 3.3 %collective-permute-start.20 = (f32[48,128]{1,0:T(8,128)S(1)}, f32[48,128]{1,0:T(8,128)S(1)}, u32[]{:S(2)}, u32[]{:S(2)}) collective-permute-start(f32[48,128]{1,0:T(8,128)S(1)} %pad_maximum_fusion.10), channel_id=1, source_target_pairs={{0,3},{1,2},{2,1},{3,0},{4,7},{5,6},{6,5},{7,4},{8,11},{9,10},{10,... | collective-permute-start | bytes 73736 | tf_op jit(solution)/shard_map/ppermute | solution.py:31
  54.9 6.8 %collective-permute-start.25 = (f32[40,128]{1,0:T(8,128)S(1)}, f32[40,128]{1,0:T(8,128)S(1)}, u32[]{:S(2)}, u32[]{:S(2)}) collective-permute-start(f32[40,128]{1,0:T(8,128)S(1)} %slice_add_fusion.3), channel_id=1, source_target_pairs={{0,17},{1,16},{2,19},{3,18},{4,21},{5,20},{6,23},{7,22},{8,25},{9,... | collective-permute-start | bytes 61448 | tf_op jit(solution)/shard_map/ppermute | solution.py:31
  55.2 5.3 %collective-permute-start.23 = (f32[72,128]{1,0:T(8,128)S(1)}, f32[72,128]{1,0:T(8,128)S(1)}, u32[]{:S(2)}, u32[]{:S(2)}) collective-permute-start(f32[72,128]{1,0:T(8,128)S(1)} %get-tuple-element.102), channel_id=1, source_target_pairs={{0,25},{1,24},{2,27},{3,26},{4,29},{5,28},{6,31},{7,30},{8,17},{9,... | collective-permute-start | bytes 110600 | tf_op jit(solution)/shard_map/ppermute | solution.py:31
  57.5 4.2 %collective-permute-start.24 = (f32[72,128]{1,0:T(8,128)S(1)}, f32[72,128]{1,0:T(8,128)S(1)}, u32[]{:S(2)}, u32[]{:S(2)}) collective-permute-start(f32[72,128]{1,0:T(8,128)S(1)} %get-tuple-element.103), channel_id=1, source_target_pairs={{0,9},{1,8},{2,11},{3,10},{4,13},{5,12},{6,15},{7,14},{8,1},{9,0},... | collective-permute-start | bytes 110600 | tf_op jit(solution)/shard_map/ppermute | solution.py:31

commit v4 on v3

--- a/solution.py
+++ b/solution.py
@@ -62,7 +62,11 @@
     ]
 
 
-SPLIT_STAGES = [[(0, 1)], [(0, 3), (0, 4), (0, 7)], [(1, 1), (2, 0), (3, 1)]]
+SPLIT_STAGES = [[(0, 1)], [(0, 3), (0, 4), (0, 7)], [(1, 0), (2, 1), (3, 1)]]
+
+
+def two_kinds():
+    return [len(stage) for stage in all_stages()] == [len(stage) for stage in SPLIT_STAGES]
 
 
 def exchange_stage(value, stage, riders, arrived):
@@ -79,48 +83,50 @@
     return total
 
 
-def all_sum(value, sides):
+def all_sum(message, far, rows, kind=None):
     ni, nx = lax.axis_size("inline"), lax.axis_size("xline")
-    xa, xb = sides["xline"]
+    lines = far.shape[0]
     first, *others = all_stages()
-    split = isinstance(value, tuple)
-    if split:
-        halves = [part.shape[0] for part in value]
-        value = jnp.concatenate(value, axis=0)
-        if len(first) == 1 and [len(stage) for stage in others] == [3, 3] and halves[0] == halves[1]:
-            others = SPLIT_STAGES[1:]
-            two_kinds = True
-        else:
-            two_kinds = False
-    arrived = {}
-    riders = {(0, mask): xb for mask in side_masks(nx)}
-    riders[0, 1] = jnp.concatenate([xa, *sides["inline"]], axis=0)
-    value = exchange_stage(value, first, riders, arrived)
-    beside, mate_a, mate_b = jnp.split(
-        arrived[0, 1], [xa.shape[0], xa.shape[0] + sides["inline"][0].shape[0]], axis=0
-    )
-    arrived[0, 1] = beside
-    del riders[0, 1]
-    for mask in side_masks(ni):
-        riders[mask, 1] = mate_a if mask == 1 else mate_b
-    if split and two_kinds:
-        gi, gx = lax.axis_index("inline"), lax.axis_index("xline")
-        kind = (gx ^ (gx >> 1) ^ gi) & 1
-        value = jnp.where(kind == 0, value[: halves[0]], value[halves[0] :])
+    if kind is not None:
+        others = SPLIT_STAGES[1:]
+    got = xor_permute(message, 0, 1)
+    value = message[:rows] + got[:rows]
+    own = jnp.split(message[rows + lines :], 2, axis=0)
+    mate = jnp.split(got[rows + lines :], 2, axis=0)
+    arrived = {(0, 1): got[rows : rows + lines]}
+    riders = {(0, mask): far for mask in side_masks(nx)[1:]}
+    for stage in others:
+        for mask, flip in stage:
+            if mask in side_masks(ni):
+                riders[mask, flip] = (mate if flip else own)[0 if mask == 1 else 1]
+    value = exchange_more(value, message[:rows], first, riders, arrived)
+    if kind is not None:
+        half = rows // 2
+        value = jnp.where(kind == 0, value[:half], value[half:])
     for stage in others:
         value = exchange_stage(value, stage, riders, arrived)
-    if split:
-        if two_kinds:
-            swapped = xor_permute(value, 0, 1)
-            value = (jnp.where(kind == 0, value, swapped), jnp.where(kind == 0, swapped, value))
-        else:
-            value = (value[: halves[0]], value[halves[0] :])
-    return value, halos(
-        {
-            "inline": {mask: arrived[mask, 1] for mask in side_masks(ni)},
-            "xline": {mask: arrived[0, mask] for mask in side_masks(nx)},
-        }
+    if kind is not None:
+        swapped = xor_permute(value, 0, 1)
+        value = jnp.concatenate(
+            [jnp.where(kind == 0, value, swapped), jnp.where(kind == 0, swapped, value)], axis=0
+        )
+    beside = {masks[0] or -masks[1]: face for masks, face in arrived.items()}
+    return (
+        value,
+        [beside[mask] for mask in side_masks(ni)],
+        [beside[-mask] for mask in side_masks(nx)],
     )
+
+
+def exchange_more(value, own, first, riders, arrived):
+    rows = own.shape[0]
+    for masks in first[1:]:
+        rider = riders.get(masks)
+        got = xor_permute(own if rider is None else jnp.concatenate([own, rider], axis=0), *masks)
+        if rider is not None:
+            arrived[masks] = got[rows:]
+        value = value + got[:rows]
+    return value
 
 
 def beyond(index, count):
@@ -128,7 +134,7 @@
     return other if 0 <= other < count else None
 
 
-def side_exchange(sides):
+def side_exchange(ia, ib, xa, xb):
     ni, nx = lax.axis_size("inline"), lax.axis_size("xline")
 
     def inline_far(i, j):
@@ -139,39 +145,10 @@
         other = beyond(j, nx)
         return (i ^ 1, j) if other is None else (i, other)
 
-    return {
-        "inline": ordered("inline", xor_permute(sides["inline"][0], 1, 0), pair_permute(sides["inline"][1], inline_far)),
-        "xline": ordered("xline", xor_permute(sides["xline"][0], 0, 1), pair_permute(sides["xline"][1], xline_far)),
-    }
-
-
-def ordered(axis, beside, far):
-    even = lax.axis_index(axis) % 2 == 0
-    return jnp.where(even, far, beside), jnp.where(even, beside, far)
-
-
-def halos(arrived):
-    result = {}
-    for axis in MESH_AXES:
-        index = lax.axis_index(axis)
-        other = jnp.where(index % 2 == 0, index - 1, index + 1)
-        far = arrived[axis][1]
-        for mask in side_masks(lax.axis_size(axis))[1:]:
-            far = jnp.where((index ^ other) == mask, arrived[axis][mask], far)
-        result[axis] = ordered(axis, arrived[axis][1], far)
-    return result
-
-
-def sides_of(lower, upper, axis):
-    even = lax.axis_index(axis) % 2 == 0
-    return jnp.where(even, upper, lower), jnp.where(even, lower, upper)
-
-
-def all_sides(cells):
-    return {
-        "inline": sides_of(cells[0], cells[-1], "inline"),
-        "xline": sides_of(cells[:, 0], cells[:, -1], "xline"),
-    }
+    return (
+        xor_permute(ia, 1, 0), pair_permute(ib, inline_far),
+        xor_permute(xa, 0, 1), pair_permute(xb, xline_far),
+    )
 
 
 def harmonic_average(first, second):
@@ -245,6 +222,32 @@
 
 def layers(cells):
     return pltpu.roll(cells, 1, 2), pltpu.roll(cells, LANES - 1, 2)
+
+
+def side_faces(cells, axis):
+    lower, upper = (cells[0], cells[-1]) if axis == "inline" else (cells[:, 0], cells[:, -1])
+    odd = lax.axis_index(axis) % 2 == 1
+    return jnp.where(odd, lower, upper), jnp.where(odd, upper, lower)
+
+
+def halo(axis, faces):
+    index = lax.axis_index(axis)
+    even = index % 2 == 0
+    apart = index ^ jnp.where(even, index - 1, index + 1)
+    far = faces[-1]
+    for mask, face in list(zip(side_masks(lax.axis_size(axis)), faces))[1:-1]:
+        far = jnp.where(apart == mask, face, far)
+    return jnp.where(even, far, faces[0]), jnp.where(even, faces[0], far)
+
+
+def put_message(direction, blocks, message_ref, far_ref):
+    ia, ib = side_faces(direction, "inline")
+    xa, xb = side_faces(direction, "xline")
+    start = 0
+    for block in (*blocks, xa, ia, ib):
+        message_ref[start : start + block.shape[0], :] = block
+        start += block.shape[0]
+    far_ref[...] = xb
 
 
 def load_kernel(
@@ -271,13 +274,8 @@
     lateral = lookup(facies, table_ref, 0) * thickness
     lateral_ref[...] = lateral
     vertical_ref[...] = lookup(facies, table_ref, 1) / thickness
-    for axis, lower, upper, a_ref, b_ref in (
-        ("inline", lateral[0], lateral[-1], ia_ref, ib_ref),
-        ("xline", lateral[:, 0], lateral[:, -1], xa_ref, xb_ref),
-    ):
-        odd = lax.axis_index(axis) % 2 == 1
-        a_ref[...] = jnp.where(odd, lower, upper)
-        b_ref[...] = jnp.where(odd, upper, lower)
+    ia_ref[...], ib_ref[...] = side_faces(lateral, "inline")
+    xa_ref[...], xb_ref[...] = side_faces(lateral, "xline")
     number_ref[...] = owner_ref[...] * WELL_DEV + well_ref[...]
 
 
@@ -333,25 +331,22 @@
 
 def start_kernel(
     right_ref, lateral_ref, accumulation_ref, cellwi_ref, zlow_ref, zup_ref,
-    ilow_ref, iup_ref, xlow_ref, xup_ref, row_ref, col_ref, wrow_ref, wcol_ref, index_ref,
-    til_ref, tiu_ref, txl_ref, txu_ref, diagonal_ref, inverse_ref, direction_ref, sums_ref, wscaled_ref,
+    ia_ref, ib_ref, xa_ref, xb_ref, storage_ref, row_ref, col_ref, wrow_ref, wcol_ref, index_ref,
+    til_ref, tiu_ref, txl_ref, txu_ref, diagonal_ref, inverse_ref, direction_ref, message_ref, far_ref, kind_ref,
+    wscaled_ref,
     *, scale,
 ):
     lateral = lateral_ref[...]
     gi, gx = lax.axis_index("inline"), lax.axis_index("xline")
-    low, up = neighbours(
-        lateral,
-        jnp.where(gi == 0, 0.0, ilow_ref[...]),
-        jnp.where(gi == lax.axis_size("inline") - 1, 0.0, iup_ref[...]),
-        0,
-    )
+    low, up = halo("inline", [ia_ref[...], ib_ref[...]])
+    low = jnp.where(gi == 0, 0.0, low)
+    up = jnp.where(gi == lax.axis_size("inline") - 1, 0.0, up)
+    low, up = neighbours(lateral, low, up, 0)
     til, tiu = harmonic_average(lateral, low), harmonic_average(lateral, up)
-    low, up = neighbours(
-        lateral,
-        jnp.where(gx == 0, 0.0, xlow_ref[...]),
-        jnp.where(gx == lax.axis_size("xline") - 1, 0.0, xup_ref[...]),
-        1,
-    )
+    low, up = halo("xline", [xa_ref[...], xb_ref[...]])
+    low = jnp.where(gx == 0, 0.0, low)
+    up = jnp.where(gx == lax.axis_size("xline") - 1, 0.0, up)
+    low, up = neighbours(lateral, low, up, 1)
     txl, txu = harmonic_average(lateral, low), harmonic_average(lateral, up)
     til_ref[...], tiu_ref[...], txl_ref[...], txu_ref[...] = til, tiu, txl, txu
     diagonal = accumulation_ref[...] + til + tiu + txl + txu + zlow_ref[...] + zup_ref[...] + cellwi_ref[...]
@@ -360,21 +355,30 @@
     diagonal_ref[...] = diagonal
     inverse_ref[...] = inverse
     direction_ref[...] = direction
-    sums_ref[...] = perforation_sums(direction, row_ref, col_ref, wrow_ref, wcol_ref, index_ref, wscaled_ref, sums_ref.shape[0])
-
-
-def sweep_kernel(
-    residual_ref, direction_ref, pressure_ref, diagonal_ref, inverse_ref,
-    til_ref, tiu_ref, txl_ref, txu_ref, zlow_ref, zup_ref,
-    ilow_ref, iup_ref, xlow_ref, xup_ref, sums_ref, storage_ref,
-    row_ref, col_ref, wrow_ref, wcol_ref, index_ref,
-    *rest, keep, gain, first,
-):
+    storage = storage_ref[...]
+    sums = perforation_sums(
+        direction, row_ref, col_ref, wrow_ref, wcol_ref, index_ref, wscaled_ref, storage.shape[0]
+    )
+    put_message(direction, [sums, storage], message_ref, far_ref)
+    kind_ref[...] = jnp.full(kind_ref.shape, (gx ^ (gx >> 1) ^ (gi >> 1)) & 1, jnp.int32)
+
+
+def sweep_kernel(*refs, keep, gain, first, sides):
+    (
+        residual_ref, direction_ref, pressure_ref, diagonal_ref, inverse_ref,
+        til_ref, tiu_ref, txl_ref, txu_ref, zlow_ref, zup_ref,
+    ) = refs[:11]
+    inline_faces = [ref[...] for ref in refs[11 : 11 + sides[0]]]
+    xline_faces = [ref[...] for ref in refs[11 + sides[0] : 11 + sum(sides)]]
+    sums_ref, storage_ref, row_ref, col_ref, wrow_ref, wcol_ref, index_ref, *rest = refs[11 + sum(sides) :]
     last = keep is None
     if last:
         next_pressure_ref, next_residual_ref, scaled_ref = rest
     else:
-        next_pressure_ref, next_residual_ref, next_direction_ref, next_sums_ref, scaled_ref, wscaled_ref = rest
+        (
+            next_pressure_ref, next_residual_ref, next_direction_ref, message_ref, far_ref,
+            scaled_ref, wscaled_ref,
+        ) = rest
     wells = sums_ref.shape[0]
     bottom = sums_ref[...] / (1.0 + storage_ref[...])
     spare = wrow_ref.shape[0] - wells
@@ -385,8 +389,8 @@
         values = picked_sum(wrow_ref[:, part], halves_sum(dot_nn(table, wcol_ref[:, part])))
         put_scaled(index_ref[:, part] * values, col_ref, scaled_ref, part)
     direction = direction_ref[...]
-    ilow, iup = neighbours(direction, ilow_ref[...], iup_ref[...], 0)
-    xlow, xup = neighbours(direction, xlow_ref[...], xup_ref[...], 1)
+    ilow, iup = neighbours(direction, *halo("inline", inline_faces), 0)
+    xlow, xup = neighbours(direction, *halo("xline", xline_faces), 1)
     below, above = layers(direction)
     beside = (
         til_ref[...] * ilow + tiu_ref[...] * iup + txl_ref[...] * xlow + txu_ref[...] * xup
@@ -402,9 +406,10 @@
     if not last:
         following = keep * direction + gain * (residual * inverse_ref[...])
         next_direction_ref[...] = following
-        next_sums_ref[...] = perforation_sums(
+        next_sums = perforation_sums(
             following, row_ref, col_ref, wrow_ref, wcol_ref, index_ref, wscaled_ref, wells
         )
+        put_message(following, [next_sums], message_ref, far_ref)
 
 
 def body(
@@ -456,7 +461,7 @@
         pltpu.with_memory_space_constraint(value, pltpu.HBM)
         for value in (facies_table, facies, thickness, right_side, accumulation, cell, owner, well, index)
     ))
-    lateral_halo = side_exchange({"inline": (ia, ib), "xline": (xa, xb)})
+    lateral_faces = side_exchange(ia, ib, xa, xb)
     cellwi, storage, zlow, zup, *hot = pl.pallas_call(
         perforation_kernel,
         out_shape=(grid, sums, grid, grid, *hots),
@@ -470,41 +475,46 @@
     delta = (HIGH_BOUND - LOW_BOUND) / 2.0
     sigma = theta / delta
     rho_now = 1.0 / sigma
-    til, tiu, txl, txu, diagonal, inverse, direction, partial = pl.pallas_call(
+    face_rows = shape[0] + 2 * shape[1]
+    start_message = jax.ShapeDtypeStruct((2 * wells + face_rows, LANES), f32)
+    sweep_message = jax.ShapeDtypeStruct((wells + face_rows, LANES), f32)
+    kinds = jax.ShapeDtypeStruct((wells, LANES), jnp.int32)
+    til, tiu, txl, txu, diagonal, inverse, direction, message, far, kind = pl.pallas_call(
         functools.partial(start_kernel, scale=1.0 / theta),
-        out_shape=(grid,) * 7 + (sums,),
-        in_specs=[VMEM] * 15,
-        out_specs=(VMEM,) * 8,
+        out_shape=(grid,) * 7 + (start_message, faces[2], kinds),
+        in_specs=[VMEM] * 16,
+        out_specs=(VMEM,) * 10,
         scratch_shapes=[wscaled_scratch],
         compiler_params=PARAMS,
-    )(right_side, lateral, accumulation, cellwi, zlow, zup,
-      *lateral_halo["inline"], *lateral_halo["xline"], *hot, index)
+    )(right_side, lateral, accumulation, cellwi, zlow, zup, *lateral_faces, storage, *hot, index)
 
     residual, pressure = right_side, right_side
     for sweep in range(SWEEPS):
         last = sweep + 1 == SWEEPS
         if sweep == 0:
-            (total, storage), halo = all_sum((partial, storage), all_sides(direction))
+            both, inline_faces, xline_faces = all_sum(message, far, 2 * wells, kind if two_kinds() else None)
+            total, storage = both[:wells], both[wells:]
         else:
-            total, halo = all_sum(partial, all_sides(direction))
+            total, inline_faces, xline_faces = all_sum(message, far, wells)
         keep = gain = None
         if not last:
             rho_next = 1.0 / (2.0 * sigma - rho_now)
             keep, gain = rho_next * rho_now, 2.0 * rho_next / delta
             rho_now = rho_next
+        sides = (len(inline_faces), len(xline_faces))
         results = pl.pallas_call(
-            functools.partial(sweep_kernel, keep=keep, gain=gain, first=sweep == 0),
-            out_shape=(grid, grid) if last else (grid, grid, grid, sums),
-            in_specs=[VMEM] * 22,
-            out_specs=(VMEM,) * (2 if last else 4),
+            functools.partial(sweep_kernel, keep=keep, gain=gain, first=sweep == 0, sides=sides),
+            out_shape=(grid, grid) if last else (grid, grid, grid, sweep_message, faces[2]),
+            in_specs=[VMEM] * (18 + sum(sides)),
+            out_specs=(VMEM,) * (2 if last else 5),
             scratch_shapes=[scaled_scratch] if last else [scaled_scratch, wscaled_scratch],
             compiler_params=PARAMS,
         )(residual, direction, pressure, diagonal, inverse, til, tiu, txl, txu, zlow, zup,
-          *halo["inline"], *halo["xline"], total, storage, *hot, index)
+          *inline_faces, *xline_faces, total, storage, *hot, index)
         if last:
             pressure, residual = results
         else:
-            pressure, residual, direction, partial = results
+            pressure, residual, direction, message, far = results
     return pressure, residual
 
 

time: 63.6 us -> 61.9 us (0.973)
  waiting for transfers between devices: 23.3 us -> 20.2 us
  starting transfers between devices: 26.7 us -> 28.6 us
    ppermute x26, waiting for transfers between devices: 23.3 us -> 20.2 us  [pair_permute(): return lax.ppermute(value, MESH_AXES, pairs)]
    ppermute x26, starting transfers between devices: 26.7 us -> 28.6 us  [pair_permute(): return lax.ppermute(value, MESH_AXES, pairs)]
  transfers between devices with their start and end apart: 26 -> 26, of which waited for: 20 -> 17; matrix products, arithmetic and copies ran while one was open for 0% -> 0% of each run, Pallas kernels for 2% -> 2%
where the time goes in v4:
time: 61.9 us; the launch traced here: 61.8 us
  starting transfers between devices  28.6 us (46%)
  waiting for transfers between devices  20.2 us (33%)
  Pallas kernels  12 us (19%)
  between operations  0.78 us (1%)
    ppermute x26, starting transfers between devices, pair_permute(): return lax.ppermute(value, MESH_AXES, pairs)  28.6 us
    ppermute x26, waiting for transfers between devices, pair_permute(): return lax.ppermute(value, MESH_AXES, pairs)  20.2 us
    pallas_call x3, Pallas kernels, body(): pl.pallas_call(functools.partial(sweep_kernel, keep=keep, gain=gain, firs...  7.86 us
    pallas_call x1, Pallas kernels, body(): pl.pallas_call(perforation_kernel, out_shape=(grid, sums, grid, grid, *ho...  1.41 us
    pallas_call x1, Pallas kernels, body(): pl.pallas_call(load_kernel, out_shape=(*faces, grid, grid, grid, grid, ro...  1.36 us
    pallas_call x1, Pallas kernels, body(): pl.pallas_call(functools.partial(start_kernel, scale=1.0 / theta), out_sh...  1.36 us
  transfers between devices with their start and end apart: 26, of which 17 were waited for; matrix products, arithmetic and copies ran while one was open for 0% of the time, Pallas kernels for 2%

profile of v4, /device:TPU:0, one launch (start us, length us, event | category | flops | bytes accessed | tf_op | source)
XLA Modules:
  0.0 61.8 jit_solution(18331189724180404221)
XLA Ops:
  0.6 1.4 %shard_map.104 = (f32[32,128]{1,0:T(8,128)S(1)}, f32[32,128]{1,0:T(8,128)S(1)}, f32[8,128]{1,0:T(8,128)S(1)}, f32[8,128]{1,0:T(8,128)S(1)}, f32[8,32,128]{2,1,0:...) custom-call(f32[2,8]{1,0:T(2,128)} %table_hbm.1, ...), custom_call_target="tpu_custom_call" | custom-call | tf_op jit(solution)/shard_map/pallas_call | solution.py:446
  2.0 3.1 %collective-permute-start = (f32[32,128]{1,0:T(8,128)S(1)}, f32[32,128]{1,0:T(8,128)S(1)}, u32[]{:S(2)}, u32[]{:S(2)}) collective-permute-start(f32[32,128]{1,0:T(8,128)S(1)} %get-tuple-element.51), channel_id=1, source_target_pairs={{0,8},{1,9},{2,10},{3,11},{4,12},{5,13},{6,14},{7,15},{8,0},{9,1},... | collective-permute-start | bytes 49160 | tf_op jit(solution)/shard_map/ppermute | solution.py:31
  5.1 0.0 collective-permute-start.1
  5.1 0.5 collective-permute-start.2
  5.6 2.6 %collective-permute-start.3 = (f32[8,128]{1,0:T(8,128)S(1)}, f32[8,128]{1,0:T(8,128)S(1)}, u32[]{:S(2)}, u32[]{:S(2)}) collective-permute-start(f32[8,128]{1,0:T(8,128)S(1)} %get-tuple-element.54), channel_id=1, source_target_pairs={{0,8},{1,2},{2,1},{3,4},{4,3},{5,6},{6,5},{7,15},{8,0},{9,10},{10,... | collective-permute-start | bytes 12296 | tf_op jit(solution)/shard_map/ppermute | solution.py:31
  8.3 1.4 %shard_map.105 = (f32[8,32,128]{2,1,0:T(8,128)S(1)}, f32[40,128]{1,0:T(8,128)S(1)}, f32[8,32,128]{2,1,0:T(8,128)S(1)}, f32[8,32,128]{2,1,0:T(8,128)S(1)}, bf16[2...) custom-call(f32[8,32,128]{2,1,0:T(8,128)S(1)} %get-tuple-element.44., ...), custom_call_target="tpu_custom_call" | custom-call | tf_op jit(solution)/shard_map/pallas_call | solution.py:465
  9.7 0.0 collective-permute-done.2.xa_ref
  9.7 0.2 collective-permute-done.3.xb_ref
  9.8 0.0 collective-permute-done.ia_ref
  9.8 0.0 collective-permute-done.1.ib_ref
  9.8 1.4 %shard_map.106 = (f32[8,32,128]{2,1,0:T(8,128)S(1)}, f32[8,32,128]{2,1,0:T(8,128)S(1)}, f32[8,32,128]{2,1,0:T(8,128)S(1)}, f32[8,32,128]{2,1,0:T(8,128)S(1)}, f3...) custom-call(f32[8,32,128]{2,1,0:T(8,128)S(1)} %get-tuple-element.41., ...), custom_call_target="tpu_custom_call" | custom-call | tf_op jit(solution)/shard_map/pallas_call | solution.py:482
  11.2 0.0 collective-permute-start.4
  11.2 1.3 %collective-permute-done.4 = f32[152,128]{1,0:T(8,128)S(1)} collective-permute-done((f32[152,128]{1,0:T(8,128)S(1)}, f32[152,128]{1,0:T(8,128)S(1)}, u32[]{:S(2)}, u32[]{:S(2)}) %collective-permute-start.4) | collective-permute-done | bytes 77856 | tf_op jit(solution)/shard_map/ppermute | solution.py:31
  12.5 2.2 %collective-permute-start.7 = (f32[48,128]{1,0:T(8,128)S(1)}, f32[48,128]{1,0:T(8,128)S(1)}, u32[]{:S(2)}, u32[]{:S(2)}) collective-permute-start(f32[48,128]{1,0:T(8,128)S(1)} %pad_maximum_fusion.6), channel_id=1, source_target_pairs={{0,7},{1,6},{2,5},{3,4},{4,3},{5,2},{6,1},{7,0},{8,15},{9,14},{10,... | collective-permute-start | bytes 73736 | tf_op jit(solution)/shard_map/ppermute | solution.py:31
  14.8 0.3 collective-permute-start.5
  15.0 0.8 %collective-permute-start.6 = (f32[40,128]{1,0:T(8,128)S(1)}, f32[40,128]{1,0:T(8,128)S(1)}, u32[]{:S(2)}, u32[]{:S(2)}) collective-permute-start(f32[40,128]{1,0:T(8,128)S(1)} %get-tuple-element.80), channel_id=1, source_target_pairs={{0,4},{1,5},{2,6},{3,7},{4,0},{5,1},{6,2},{7,3},{8,12},{9,13},{10,... | collective-permute-start | bytes 61448 | tf_op jit(solution)/shard_map/ppermute | solution.py:31
  15.8 3.0 %collective-permute-done.6 = f32[40,128]{1,0:T(8,128)S(1)} collective-permute-done((f32[40,128]{1,0:T(8,128)S(1)}, f32[40,128]{1,0:T(8,128)S(1)}, u32[]{:S(2)}, u32[]{:S(2)}) %collective-permute-start.6) | collective-permute-done | bytes 20512 | tf_op jit(solution)/shard_map/ppermute | solution.py:31
  18.8 0.0 collective-permute-done.7
  18.8 0.0 collective-permute-done.5
  18.8 1.2 %collective-permute-start.9 = (f32[72,128]{1,0:T(8,128)S(1)}, f32[72,128]{1,0:T(8,128)S(1)}, u32[]{:S(2)}, u32[]{:S(2)}) collective-permute-start(f32[72,128]{1,0:T(8,128)S(1)} %get-tuple-element.92), channel_id=1, source_target_pairs={{0,25},{1,24},{2,27},{3,26},{4,29},{5,28},{6,31},{7,30},{8,17},{9,... | collective-permute-start | bytes 110600 | tf_op jit(solution)/shard_map/ppermute | solution.py:31
  20.0 1.6 %collective-permute-start.8 = (f32[72,128]{1,0:T(8,128)S(1)}, f32[72,128]{1,0:T(8,128)S(1)}, u32[]{:S(2)}, u32[]{:S(2)}) collective-permute-start(f32[72,128]{1,0:T(8,128)S(1)} %get-tuple-element.93), channel_id=1, source_target_pairs={{0,8},{1,9},{2,10},{3,11},{4,12},{5,13},{6,14},{7,15},{8,0},{9,1},... | collective-permute-start | bytes 110600 | tf_op jit(solution)/shard_map/ppermute | solution.py:31
  21.6 1.1 %collective-permute-start.10 = (f32[40,128]{1,0:T(8,128)S(1)}, f32[40,128]{1,0:T(8,128)S(1)}, u32[]{:S(2)}, u32[]{:S(2)}) collective-permute-start(f32[40,128]{1,0:T(8,128)S(1)} %slice_add_fusion.13), channel_id=1, source_target_pairs={{0,17},{1,16},{2,19},{3,18},{4,21},{5,20},{6,23},{7,22},{8,25},{9,... | collective-permute-start | bytes 61448 | tf_op jit(solution)/shard_map/ppermute | solution.py:31
  22.7 3.4 %collective-permute-done.10 = f32[40,128]{1,0:T(8,128)S(1)} collective-permute-done((f32[40,128]{1,0:T(8,128)S(1)}, f32[40,128]{1,0:T(8,128)S(1)}, u32[]{:S(2)}, u32[]{:S(2)}) %collective-permute-start.10) | collective-permute-done | bytes 20512 | tf_op jit(solution)/shard_map/ppermute | solution.py:31
  26.1 0.0 collective-permute-done.9
  26.1 0.0 collective-permute-done.8
  26.1 0.2 collective-permute-start.11
  26.4 1.1 %collective-permute-done.11 = f32[40,128]{1,0:T(8,128)S(1)} collective-permute-done((f32[40,128]{1,0:T(8,128)S(1)}, f32[40,128]{1,0:T(8,128)S(1)}, u32[]{:S(2)}, u32[]{:S(2)}) %collective-permute-start.11) | collective-permute-done | bytes 20512 | tf_op jit(solution)/shard_map/ppermute | solution.py:31
  27.4 3.0 %shard_map.107 = (f32[8,32,128]{2,1,0:T(8,128)S(1)}, f32[8,32,128]{2,1,0:T(8,128)S(1)}, f32[8,32,128]{2,1,0:T(8,128)S(1)}, f32[112,128]{1,0:T(8,128)S(1)}, f32[8,128]{1,0:T(8,128)S(1)}) custom-call(f32[8,32,128]{2,1,0:T(8,128)S(1)} %get-tuple-element.41.right_ref.refs_0_.refs_2_, f32[8,32,128]{2,1,0:T(8,128)S(1)} %get-tuple-element.60.refs_1_, ...), custom_call_target="tpu_custom_call" | custom-call | tf_op jit(solution)/shard_map/pallas_call | solution.py:505
  30.5 0.2 collective-permute-start.12
  30.7 1.1 %collective-permute-done.12 = f32[112,128]{1,0:T(8,128)S(1)} collective-permute-done((f32[112,128]{1,0:T(8,128)S(1)}, f32[112,128]{1,0:T(8,128)S(1)}, u32[]{:S(2)}, u32[]{:S(2)}) %collective-permute-start.12) | collective-permute-done | bytes 57376 | tf_op jit(solution)/shard_map/ppermute | solution.py:31
  31.7 0.1 collective-permute-start.14
  31.9 1.4 %collective-permute-start.15 = (f32[48,128]{1,0:T(8,128)S(1)}, f32[48,128]{1,0:T(8,128)S(1)}, u32[]{:S(2)}, u32[]{:S(2)}) collective-permute-start(f32[48,128]{1,0:T(8,128)S(1)} %pad_maximum_fusion.7), channel_id=1, source_target_pairs={{0,7},{1,6},{2,5},{3,4},{4,3},{5,2},{6,1},{7,0},{8,15},{9,14},{10,... | collective-permute-start | bytes 73736 | tf_op jit(solution)/shard_map/ppermute | solution.py:31
  33.2 1.5 %collective-permute-start.13 = (f32[48,128]{1,0:T(8,128)S(1)}, f32[48,128]{1,0:T(8,128)S(1)}, u32[]{:S(2)}, u32[]{:S(2)}) collective-permute-start(f32[48,128]{1,0:T(8,128)S(1)} %pad_maximum_fusion.7), channel_id=1, source_target_pairs={{0,3},{1,2},{2,1},{3,0},{4,7},{5,6},{6,5},{7,4},{8,11},{9,10},{10,... | collective-permute-start | bytes 73736 | tf_op jit(solution)/shard_map/ppermute | solution.py:31
  34.7 0.2 collective-permute-done.14
  34.9 1.1 %collective-permute-done.15 = f32[48,128]{1,0:T(8,128)S(1)} collective-permute-done((f32[48,128]{1,0:T(8,128)S(1)}, f32[48,128]{1,0:T(8,128)S(1)}, u32[]{:S(2)}, u32[]{:S(2)}) %collective-permute-start.15) | collective-permute-done | bytes 24608 | tf_op jit(solution)/shard_map/ppermute | solution.py:31
  36.0 0.5 collective-permute-done.13
  36.5 2.2 %collective-permute-start.17 = (f32[72,128]{1,0:T(8,128)S(1)}, f32[72,128]{1,0:T(8,128)S(1)}, u32[]{:S(2)}, u32[]{:S(2)}) collective-permute-start(f32[72,128]{1,0:T(8,128)S(1)} %get-tuple-element.90), channel_id=1, source_target_pairs={{0,25},{1,24},{2,27},{3,26},{4,29},{5,28},{6,31},{7,30},{8,17},{9,... | collective-permute-start | bytes 110600 | tf_op jit(solution)/shard_map/ppermute | solution.py:31
  38.8 0.1 collective-permute-start.16
  38.8 1.8 %collective-permute-start.18 = (f32[40,128]{1,0:T(8,128)S(1)}, f32[40,128]{1,0:T(8,128)S(1)}, u32[]{:S(2)}, u32[]{:S(2)}) collective-permute-start(f32[40,128]{1,0:T(8,128)S(1)} %slice_add_fusion.8), channel_id=1, source_target_pairs={{0,17},{1,16},{2,19},{3,18},{4,21},{5,20},{6,23},{7,22},{8,25},{9,... | collective-permute-start | bytes 61448 | tf_op jit(solution)/shard_map/ppermute | solution.py:31
  40.6 1.1 %collective-permute-done.17 = f32[72,128]{1,0:T(8,128)S(1)} collective-permute-done((f32[72,128]{1,0:T(8,128)S(1)}, f32[72,128]{1,0:T(8,128)S(1)}, u32[]{:S(2)}, u32[]{:S(2)}) %collective-permute-start.17) | collective-permute-done | bytes 36896 | tf_op jit(solution)/shard_map/ppermute | solution.py:31
  41.8 0.8 %collective-permute-done.16 = f32[72,128]{1,0:T(8,128)S(1)} collective-permute-done((f32[72,128]{1,0:T(8,128)S(1)}, f32[72,128]{1,0:T(8,128)S(1)}, u32[]{:S(2)}, u32[]{:S(2)}) %collective-permute-start.16) | collective-permute-done | bytes 36896 | tf_op jit(solution)/shard_map/ppermute | solution.py:31
  42.6 0.4 collective-permute-done.18
  43.0 3.1 %shard_map.108 = (f32[8,32,128]{2,1,0:T(8,128)S(1)}, f32[8,32,128]{2,1,0:T(8,128)S(1)}, f32[8,32,128]{2,1,0:T(8,128)S(1)}, f32[112,128]{1,0:T(8,128)S(1)}, f32[8,128]{1,0:T(8,128)S(1)}) custom-call(f32[8,32,128]{2,1,0:T(8,128)S(1)} %get-tuple-element.70.refs_0_, f32[8,32,128]{2,1,0:T(8,128)S(1)} %get-tuple-element.71.refs_1_, ...), custom_call_target="tpu_custom_call" | custom-call | tf_op jit(solution)/shard_map/pallas_call | solution.py:505
  46.0 0.3 collective-permute-start.19
  46.4 0.9 %collective-permute-done.19 = f32[112,128]{1,0:T(8,128)S(1)} collective-permute-done((f32[112,128]{1,0:T(8,128)S(1)}, f32[112,128]{1,0:T(8,128)S(1)}, u32[]{:S(2)}, u32[]{:S(2)}) %collective-permute-start.19) | collective-permute-done | bytes 57376 | tf_op jit(solution)/shard_map/ppermute | solution.py:31
  47.3 2.0 %collective-permute-start.21 = (f32[40,128]{1,0:T(8,128)S(1)}, f32[40,128]{1,0:T(8,128)S(1)}, u32[]{:S(2)}, u32[]{:S(2)}) collective-permute-start(f32[40,128]{1,0:T(8,128)S(1)} %slice_add_fusion.5), channel_id=1, source_target_pairs={{0,5},{1,4},{2,7},{3,6},{4,1},{5,0},{6,3},{7,2},{8,13},{9,12},{10,... | collective-permute-start | bytes 61448 | tf_op jit(solution)/shard_map/ppermute | solution.py:31
  49.3 1.3 %collective-permute-start.22 = (f32[48,128]{1,0:T(8,128)S(1)}, f32[48,128]{1,0:T(8,128)S(1)}, u32[]{:S(2)}, u32[]{:S(2)}) collective-permute-start(f32[48,128]{1,0:T(8,128)S(1)} %pad_maximum_fusion.8), channel_id=1, source_target_pairs={{0,7},{1,6},{2,5},{3,4},{4,3},{5,2},{6,1},{7,0},{8,15},{9,14},{10,... | collective-permute-start | bytes 73736 | tf_op jit(solution)/shard_map/ppermute | solution.py:31
  50.6 0.2 collective-permute-start.20
  50.8 0.0 collective-permute-done.21
  50.8 2.6 %collective-permute-done.22 = f32[48,128]{1,0:T(8,128)S(1)} collective-permute-done((f32[48,128]{1,0:T(8,128)S(1)}, f32[48,128]{1,0:T(8,128)S(1)}, u32[]{:S(2)}, u32[]{:S(2)}) %collective-permute-start.22) | collective-permute-done | bytes 24608 | tf_op jit(solution)/shard_map/ppermute | solution.py:31
  53.4 0.4 collective-permute-done.20
  53.9 1.4 %collective-permute-start.24 = (f32[72,128]{1,0:T(8,128)S(1)}, f32[72,128]{1,0:T(8,128)S(1)}, u32[]{:S(2)}, u32[]{:S(2)}) collective-permute-start(f32[72,128]{1,0:T(8,128)S(1)} %get-tuple-element.88), channel_id=1, source_target_pairs={{0,25},{1,24},{2,27},{3,26},{4,29},{5,28},{6,31},{7,30},{8,17},{9,... | collective-permute-start | bytes 110600 | tf_op jit(solution)/shard_map/ppermute | solution.py:31
  55.3 0.4 collective-permute-start.23
  55.7 2.2 %collective-permute-start.25 = (f32[40,128]{1,0:T(8,128)S(1)}, f32[40,128]{1,0:T(8,128)S(1)}, u32[]{:S(2)}, u32[]{:S(2)}) collective-permute-start(f32[40,128]{1,0:T(8,128)S(1)} %slice_add_fusion.3), channel_id=1, source_target_pairs={{0,17},{1,16},{2,19},{3,18},{4,21},{5,20},{6,23},{7,22},{8,25},{9,... | collective-permute-start | bytes 61448 | tf_op jit(solution)/shard_map/ppermute | solution.py:31
  57.8 1.4 %collective-permute-done.24 = f32[72,128]{1,0:T(8,128)S(1)} collective-permute-done((f32[72,128]{1,0:T(8,128)S(1)}, f32[72,128]{1,0:T(8,128)S(1)}, u32[]{:S(2)}, u32[]{:S(2)}) %collective-permute-start.24) | collective-permute-done | bytes 36896 | tf_op jit(solution)/shard_map/ppermute | solution.py:31
  59.2 0.0 collective-permute-done.23
  59.2 0.8 %collective-permute-done.25 = f32[40,128]{1,0:T(8,128)S(1)} collective-permute-done((f32[40,128]{1,0:T(8,128)S(1)}, f32[40,128]{1,0:T(8,128)S(1)}, u32[]{:S(2)}, u32[]{:S(2)}) %collective-permute-start.25) | collective-permute-done | bytes 20512 | tf_op jit(solution)/shard_map/ppermute | solution.py:31
  60.0 1.8 %shard_map.109 = (f32[8,32,128]{2,1,0:T(8,128)}, f32[8,32,128]{2,1,0:T(8,128)}) custom-call(f32[8,32,128]{2,1,0:T(8,128)S(1)} %get-tuple-element.75.refs_0_, f32[8,32,128]{2,1,0:T(8,128)S(1)} %get-tuple-element.76.refs_1_, f32[8,32,128]{2,1,0:T(8,128)S(1)} %get-tuple-element.77.refs_2_, f32[8,32,128]{2,1,0:T(8,128)S(1)} %get-tuple-element.61.refs_3_, ...), custom_call_target="tpu_custom_call" | custom-call | tf_op jit(solution)/shard_map/pallas_call | solution.py:505
  (36 shorter events, 0.2 us)
Async XLA Ops:
  2.0 7.8 %collective-permute-start = (f32[32,128]{1,0:T(8,128)S(1)}, f32[32,128]{1,0:T(8,128)S(1)}, u32[]{:S(2)}, u32[]{:S(2)}) collective-permute-start(f32[32,128]{1,0:T(8,128)S(1)} %get-tuple-element.51), channel_id=1, source_target_pairs={{0,8},{1,9},{2,10},{3,11},{4,12},{5,13},{6,14},{7,15},{8,0},{9,1},... | collective-permute-start | bytes 49160 | tf_op jit(solution)/shard_map/ppermute | solution.py:31
  5.1 4.7 %collective-permute-start.1 = (f32[32,128]{1,0:T(8,128)S(1)}, f32[32,128]{1,0:T(8,128)S(1)}, u32[]{:S(2)}, u32[]{:S(2)}) collective-permute-start(f32[32,128]{1,0:T(8,128)S(1)} %get-tuple-element.52), channel_id=1, source_target_pairs={{0,1},{1,0},{2,3},{3,2},{4,5},{5,4},{6,7},{7,6},{8,16},{9,17},{10,... | collective-permute-start | bytes 49160 | tf_op jit(solution)/shard_map/ppermute | solution.py:31
  5.1 4.6 %collective-permute-start.2 = (f32[8,128]{1,0:T(8,128)S(1)}, f32[8,128]{1,0:T(8,128)S(1)}, u32[]{:S(2)}, u32[]{:S(2)}) collective-permute-start(f32[8,128]{1,0:T(8,128)S(1)} %get-tuple-element.53), channel_id=1, source_target_pairs={{0,1},{1,0},{2,3},{3,2},{4,5},{5,4},{6,7},{7,6},{8,9},{9,8},{10,11... | collective-permute-start | bytes 12296 | tf_op jit(solution)/shard_map/ppermute | solution.py:31
  5.6 4.2 %collective-permute-start.3 = (f32[8,128]{1,0:T(8,128)S(1)}, f32[8,128]{1,0:T(8,128)S(1)}, u32[]{:S(2)}, u32[]{:S(2)}) collective-permute-start(f32[8,128]{1,0:T(8,128)S(1)} %get-tuple-element.54), channel_id=1, source_target_pairs={{0,8},{1,2},{2,1},{3,4},{4,3},{5,6},{6,5},{7,15},{8,0},{9,10},{10,... | collective-permute-start | bytes 12296 | tf_op jit(solution)/shard_map/ppermute | solution.py:31
  11.2 1.3 %collective-permute-start.4 = (f32[152,128]{1,0:T(8,128)S(1)}, f32[152,128]{1,0:T(8,128)S(1)}, u32[]{:S(2)}, u32[]{:S(2)}) collective-permute-start(f32[152,128]{1,0:T(8,128)S(1)} %get-tuple-element.68), channel_id=1, source_target_pairs={{0,1},{1,0},{2,3},{3,2},{4,5},{5,4},{6,7},{7,6},{8,9},{9,8},{10,11... | collective-permute-start | bytes 233480 | tf_op jit(solution)/shard_map/ppermute | solution.py:31
  12.5 6.3 %collective-permute-start.7 = (f32[48,128]{1,0:T(8,128)S(1)}, f32[48,128]{1,0:T(8,128)S(1)}, u32[]{:S(2)}, u32[]{:S(2)}) collective-permute-start(f32[48,128]{1,0:T(8,128)S(1)} %pad_maximum_fusion.6), channel_id=1, source_target_pairs={{0,7},{1,6},{2,5},{3,4},{4,3},{5,2},{6,1},{7,0},{8,15},{9,14},{10,... | collective-permute-start | bytes 73736 | tf_op jit(solution)/shard_map/ppermute | solution.py:31
  14.8 4.0 %collective-permute-start.5 = (f32[48,128]{1,0:T(8,128)S(1)}, f32[48,128]{1,0:T(8,128)S(1)}, u32[]{:S(2)}, u32[]{:S(2)}) collective-permute-start(f32[48,128]{1,0:T(8,128)S(1)} %pad_maximum_fusion.6), channel_id=1, source_target_pairs={{0,3},{1,2},{2,1},{3,0},{4,7},{5,6},{6,5},{7,4},{8,11},{9,10},{10,... | collective-permute-start | bytes 73736 | tf_op jit(solution)/shard_map/ppermute | solution.py:31
  15.0 3.8 %collective-permute-start.6 = (f32[40,128]{1,0:T(8,128)S(1)}, f32[40,128]{1,0:T(8,128)S(1)}, u32[]{:S(2)}, u32[]{:S(2)}) collective-permute-start(f32[40,128]{1,0:T(8,128)S(1)} %get-tuple-element.80), channel_id=1, source_target_pairs={{0,4},{1,5},{2,6},{3,7},{4,0},{5,1},{6,2},{7,3},{8,12},{9,13},{10,... | collective-permute-start | bytes 61448 | tf_op jit(solution)/shard_map/ppermute | solution.py:31
  18.8 7.3 %collective-permute-start.9 = (f32[72,128]{1,0:T(8,128)S(1)}, f32[72,128]{1,0:T(8,128)S(1)}, u32[]{:S(2)}, u32[]{:S(2)}) collective-permute-start(f32[72,128]{1,0:T(8,128)S(1)} %get-tuple-element.92), channel_id=1, source_target_pairs={{0,25},{1,24},{2,27},{3,26},{4,29},{5,28},{6,31},{7,30},{8,17},{9,... | collective-permute-start | bytes 110600 | tf_op jit(solution)/shard_map/ppermute | solution.py:31
  20.0 6.2 %collective-permute-start.8 = (f32[72,128]{1,0:T(8,128)S(1)}, f32[72,128]{1,0:T(8,128)S(1)}, u32[]{:S(2)}, u32[]{:S(2)}) collective-permute-start(f32[72,128]{1,0:T(8,128)S(1)} %get-tuple-element.93), channel_id=1, source_target_pairs={{0,8},{1,9},{2,10},{3,11},{4,12},{5,13},{6,14},{7,15},{8,0},{9,1},... | collective-permute-start | bytes 110600 | tf_op jit(solution)/shard_map/ppermute | solution.py:31
  21.6 4.5 %collective-permute-start.10 = (f32[40,128]{1,0:T(8,128)S(1)}, f32[40,128]{1,0:T(8,128)S(1)}, u32[]{:S(2)}, u32[]{:S(2)}) collective-permute-start(f32[40,128]{1,0:T(8,128)S(1)} %slice_add_fusion.13), channel_id=1, source_target_pairs={{0,17},{1,16},{2,19},{3,18},{4,21},{5,20},{6,23},{7,22},{8,25},{9,... | collective-permute-start | bytes 61448 | tf_op jit(solution)/shard_map/ppermute | solution.py:31
  26.1 1.3 %collective-permute-start.11 = (f32[40,128]{1,0:T(8,128)S(1)}, f32[40,128]{1,0:T(8,128)S(1)}, u32[]{:S(2)}, u32[]{:S(2)}) collective-permute-start(f32[40,128]{1,0:T(8,128)S(1)} %slice_add_fusion.11), channel_id=1, source_target_pairs={{0,1},{1,0},{2,3},{3,2},{4,5},{5,4},{6,7},{7,6},{8,9},{9,8},{10,11... | collective-permute-start | bytes 61448 | tf_op jit(solution)/shard_map/ppermute | solution.py:31
  30.5 1.3 %collective-permute-start.12 = (f32[112,128]{1,0:T(8,128)S(1)}, f32[112,128]{1,0:T(8,128)S(1)}, u32[]{:S(2)}, u32[]{:S(2)}) collective-permute-start(f32[112,128]{1,0:T(8,128)S(1)} %get-tuple-element.73), channel_id=1, source_target_pairs={{0,1},{1,0},{2,3},{3,2},{4,5},{5,4},{6,7},{7,6},{8,9},{9,8},{10,11... | collective-permute-start | bytes 172040 | tf_op jit(solution)/shard_map/ppermute | solution.py:31
  31.7 3.2 %collective-permute-start.14 = (f32[40,128]{1,0:T(8,128)S(1)}, f32[40,128]{1,0:T(8,128)S(1)}, u32[]{:S(2)}, u32[]{:S(2)}) collective-permute-start(f32[40,128]{1,0:T(8,128)S(1)} %slice_add_fusion.10), channel_id=1, source_target_pairs={{0,5},{1,4},{2,7},{3,6},{4,1},{5,0},{6,3},{7,2},{8,13},{9,12},{10,... | collective-permute-start | bytes 61448 | tf_op jit(solution)/shard_map/ppermute | solution.py:31
  31.9 4.2 %collective-permute-start.15 = (f32[48,128]{1,0:T(8,128)S(1)}, f32[48,128]{1,0:T(8,128)S(1)}, u32[]{:S(2)}, u32[]{:S(2)}) collective-permute-start(f32[48,128]{1,0:T(8,128)S(1)} %pad_maximum_fusion.7), channel_id=1, source_target_pairs={{0,7},{1,6},{2,5},{3,4},{4,3},{5,2},{6,1},{7,0},{8,15},{9,14},{10,... | collective-permute-start | bytes 73736 | tf_op jit(solution)/shard_map/ppermute | solution.py:31
  33.2 3.3 %collective-permute-start.13 = (f32[48,128]{1,0:T(8,128)S(1)}, f32[48,128]{1,0:T(8,128)S(1)}, u32[]{:S(2)}, u32[]{:S(2)}) collective-permute-start(f32[48,128]{1,0:T(8,128)S(1)} %pad_maximum_fusion.7), channel_id=1, source_target_pairs={{0,3},{1,2},{2,1},{3,0},{4,7},{5,6},{6,5},{7,4},{8,11},{9,10},{10,... | collective-permute-start | bytes 73736 | tf_op jit(solution)/shard_map/ppermute | solution.py:31
  36.5 5.2 %collective-permute-start.17 = (f32[72,128]{1,0:T(8,128)S(1)}, f32[72,128]{1,0:T(8,128)S(1)}, u32[]{:S(2)}, u32[]{:S(2)}) collective-permute-start(f32[72,128]{1,0:T(8,128)S(1)} %get-tuple-element.90), channel_id=1, source_target_pairs={{0,25},{1,24},{2,27},{3,26},{4,29},{5,28},{6,31},{7,30},{8,17},{9,... | collective-permute-start | bytes 110600 | tf_op jit(solution)/shard_map/ppermute | solution.py:31
  38.8 3.8 %collective-permute-start.16 = (f32[72,128]{1,0:T(8,128)S(1)}, f32[72,128]{1,0:T(8,128)S(1)}, u32[]{:S(2)}, u32[]{:S(2)}) collective-permute-start(f32[72,128]{1,0:T(8,128)S(1)} %get-tuple-element.91), channel_id=1, source_target_pairs={{0,9},{1,8},{2,11},{3,10},{4,13},{5,12},{6,15},{7,14},{8,1},{9,0},... | collective-permute-start | bytes 110600 | tf_op jit(solution)/shard_map/ppermute | solution.py:31
  38.8 4.1 %collective-permute-start.18 = (f32[40,128]{1,0:T(8,128)S(1)}, f32[40,128]{1,0:T(8,128)S(1)}, u32[]{:S(2)}, u32[]{:S(2)}) collective-permute-start(f32[40,128]{1,0:T(8,128)S(1)} %slice_add_fusion.8), channel_id=1, source_target_pairs={{0,17},{1,16},{2,19},{3,18},{4,21},{5,20},{6,23},{7,22},{8,25},{9,... | collective-permute-start | bytes 61448 | tf_op jit(solution)/shard_map/ppermute | solution.py:31
  46.0 1.3 %collective-permute-start.19 = (f32[112,128]{1,0:T(8,128)S(1)}, f32[112,128]{1,0:T(8,128)S(1)}, u32[]{:S(2)}, u32[]{:S(2)}) collective-permute-start(f32[112,128]{1,0:T(8,128)S(1)} %get-tuple-element.78), channel_id=1, source_target_pairs={{0,1},{1,0},{2,3},{3,2},{4,5},{5,4},{6,7},{7,6},{8,9},{9,8},{10,11... | collective-permute-start | bytes 172040 | tf_op jit(solution)/shard_map/ppermute | solution.py:31
  47.3 3.5 %collective-permute-start.21 = (f32[40,128]{1,0:T(8,128)S(1)}, f32[40,128]{1,0:T(8,128)S(1)}, u32[]{:S(2)}, u32[]{:S(2)}) collective-permute-start(f32[40,128]{1,0:T(8,128)S(1)} %slice_add_fusion.5), channel_id=1, source_target_pairs={{0,5},{1,4},{2,7},{3,6},{4,1},{5,0},{6,3},{7,2},{8,13},{9,12},{10,... | collective-permute-start | bytes 61448 | tf_op jit(solution)/shard_map/ppermute | solution.py:31
  49.3 4.2 %collective-permute-start.22 = (f32[48,128]{1,0:T(8,128)S(1)}, f32[48,128]{1,0:T(8,128)S(1)}, u32[]{:S(2)}, u32[]{:S(2)}) collective-permute-start(f32[48,128]{1,0:T(8,128)S(1)} %pad_maximum_fusion.8), channel_id=1, source_target_pairs={{0,7},{1,6},{2,5},{3,4},{4,3},{5,2},{6,1},{7,0},{8,15},{9,14},{10,... | collective-permute-start | bytes 73736 | tf_op jit(solution)/shard_map/ppermute | solution.py:31
  50.6 3.3 %collective-permute-start.20 = (f32[48,128]{1,0:T(8,128)S(1)}, f32[48,128]{1,0:T(8,128)S(1)}, u32[]{:S(2)}, u32[]{:S(2)}) collective-permute-start(f32[48,128]{1,0:T(8,128)S(1)} %pad_maximum_fusion.8), channel_id=1, source_target_pairs={{0,3},{1,2},{2,1},{3,0},{4,7},{5,6},{6,5},{7,4},{8,11},{9,10},{10,... | collective-permute-start | bytes 73736 | tf_op jit(solution)/shard_map/ppermute | solution.py:31
  53.9 5.3 %collective-permute-start.24 = (f32[72,128]{1,0:T(8,128)S(1)}, f32[72,128]{1,0:T(8,128)S(1)}, u32[]{:S(2)}, u32[]{:S(2)}) collective-permute-start(f32[72,128]{1,0:T(8,128)S(1)} %get-tuple-element.88), channel_id=1, source_target_pairs={{0,25},{1,24},{2,27},{3,26},{4,29},{5,28},{6,31},{7,30},{8,17},{9,... | collective-permute-start | bytes 110600 | tf_op jit(solution)/shard_map/ppermute | solution.py:31
  55.3 3.9 %collective-permute-start.23 = (f32[72,128]{1,0:T(8,128)S(1)}, f32[72,128]{1,0:T(8,128)S(1)}, u32[]{:S(2)}, u32[]{:S(2)}) collective-permute-start(f32[72,128]{1,0:T(8,128)S(1)} %get-tuple-element.89), channel_id=1, source_target_pairs={{0,9},{1,8},{2,11},{3,10},{4,13},{5,12},{6,15},{7,14},{8,1},{9,0},... | collective-permute-start | bytes 110600 | tf_op jit(solution)/shard_map/ppermute | solution.py:31
  55.7 4.3 %collective-permute-start.25 = (f32[40,128]{1,0:T(8,128)S(1)}, f32[40,128]{1,0:T(8,128)S(1)}, u32[]{:S(2)}, u32[]{:S(2)}) collective-permute-start(f32[40,128]{1,0:T(8,128)S(1)} %slice_add_fusion.3), channel_id=1, source_target_pairs={{0,17},{1,16},{2,19},{3,18},{4,21},{5,20},{6,23},{7,22},{8,25},{9,... | collective-permute-start | bytes 61448 | tf_op jit(solution)/shard_map/ppermute | solution.py:31

commit v5 on v4

--- a/solution.py
+++ b/solution.py
@@ -94,7 +94,7 @@
     own = jnp.split(message[rows + lines :], 2, axis=0)
     mate = jnp.split(got[rows + lines :], 2, axis=0)
     arrived = {(0, 1): got[rows : rows + lines]}
-    riders = {(0, mask): far for mask in side_masks(nx)[1:]}
+    riders = {(0, mask): far for mask in range(2, nx)}
     for stage in others:
         for mask, flip in stage:
             if mask in side_masks(ni):
@@ -280,9 +280,11 @@
 
 
 def perforation_kernel(
-    vertical_ref, cell_ref, number_ref, index_ref,
-    cellwi_ref, storage_ref, zlow_ref, zup_ref, row_ref, col_ref, wrow_ref, wcol_ref, scaled_ref, wscaled_ref,
+    vertical_ref, cell_ref, number_ref, index_ref, face_ref,
+    cellwi_ref, storage_ref, zlow_ref, zup_ref, row_ref, col_ref, wrow_ref, wcol_ref, face_out_ref,
+    scaled_ref, wscaled_ref,
 ):
+    face_out_ref[...] = face_ref[...]
     vertical = vertical_ref[...]
     below, above = layers(vertical)
     place = lax.broadcasted_iota(jnp.int32, vertical.shape, 2)
@@ -380,6 +382,19 @@
             scaled_ref, wscaled_ref,
         ) = rest
     wells = sums_ref.shape[0]
+    direction = direction_ref[...]
+    ilow, iup = neighbours(direction, *halo("inline", inline_faces), 0)
+    xlow, xup = neighbours(direction, *halo("xline", xline_faces), 1)
+    below, above = layers(direction)
+    beside = (
+        til_ref[...] * ilow + tiu_ref[...] * iup + txl_ref[...] * xlow + txu_ref[...] * xup
+        + zlow_ref[...] * below + zup_ref[...] * above
+    )
+    if first:
+        next_pressure_ref[...] = direction
+    else:
+        next_pressure_ref[...] = pressure_ref[...] + direction
+    next_residual_ref[...] = residual_ref[...] - (diagonal_ref[...] * direction - beside)
     bottom = sums_ref[...] / (1.0 + storage_ref[...])
     spare = wrow_ref.shape[0] - wells
     if spare:
@@ -388,23 +403,11 @@
     for part in parts(row_ref.shape[1]):
         values = picked_sum(wrow_ref[:, part], halves_sum(dot_nn(table, wcol_ref[:, part])))
         put_scaled(index_ref[:, part] * values, col_ref, scaled_ref, part)
-    direction = direction_ref[...]
-    ilow, iup = neighbours(direction, *halo("inline", inline_faces), 0)
-    xlow, xup = neighbours(direction, *halo("xline", xline_faces), 1)
-    below, above = layers(direction)
-    beside = (
-        til_ref[...] * ilow + tiu_ref[...] * iup + txl_ref[...] * xlow + txu_ref[...] * xup
-        + zlow_ref[...] * below + zup_ref[...] * above
-    )
-    wells_term = cells_sum(None, row_ref, col_ref, scaled_ref).reshape(direction.shape)
-    residual = residual_ref[...] - (diagonal_ref[...] * direction - beside - wells_term)
+    wells_term = cells_sum(None, row_ref, col_ref, scaled_ref).reshape(direction_ref.shape)
+    residual = next_residual_ref[...] + wells_term
     next_residual_ref[...] = residual
-    if first:
-        next_pressure_ref[...] = direction
-    else:
-        next_pressure_ref[...] = pressure_ref[...] + direction
     if not last:
-        following = keep * direction + gain * (residual * inverse_ref[...])
+        following = keep * direction_ref[...] + gain * (residual * inverse_ref[...])
         next_direction_ref[...] = following
         next_sums = perforation_sums(
             following, row_ref, col_ref, wrow_ref, wcol_ref, index_ref, wscaled_ref, wells
@@ -461,15 +464,15 @@
         pltpu.with_memory_space_constraint(value, pltpu.HBM)
         for value in (facies_table, facies, thickness, right_side, accumulation, cell, owner, well, index)
     ))
-    lateral_faces = side_exchange(ia, ib, xa, xb)
-    cellwi, storage, zlow, zup, *hot = pl.pallas_call(
+    cellwi, storage, zlow, zup, *hot, xa = pl.pallas_call(
         perforation_kernel,
-        out_shape=(grid, sums, grid, grid, *hots),
-        in_specs=[VMEM] * 4,
-        out_specs=(VMEM,) * 8,
+        out_shape=(grid, sums, grid, grid, *hots, faces[2]),
+        in_specs=[VMEM] * 5,
+        out_specs=(VMEM,) * 9,
         scratch_shapes=[scaled_scratch, wscaled_scratch],
         compiler_params=PARAMS,
-    )(vertical, cell, number, index)
+    )(vertical, cell, number, index, xa)
+    lateral_faces = side_exchange(ia, ib, xa, xb)
 
     theta = (HIGH_BOUND + LOW_BOUND) / 2.0
     delta = (HIGH_BOUND - LOW_BOUND) / 2.0

time: 61.9 us -> 61.7 us (level)
  transfers between devices with their start and end apart: 26 -> 26, of which waited for: 17 -> 20; matrix products, arithmetic and copies ran while one was open for 0% -> 0% of each run, Pallas kernels for 2% -> 2%
where the time goes in v5:
time: 61.7 us; the launch traced here: 61.5 us
  starting transfers between devices  28.2 us (46%)
  waiting for transfers between devices  20.4 us (33%)
  Pallas kernels  12 us (19%)
  between operations  0.76 us (1%)
    ppermute x26, starting transfers between devices, pair_permute(): return lax.ppermute(value, MESH_AXES, pairs)  28.2 us
    ppermute x26, waiting for transfers between devices, pair_permute(): return lax.ppermute(value, MESH_AXES, pairs)  20.4 us
    pallas_call x3, Pallas kernels, body(): pl.pallas_call(functools.partial(sweep_kernel, keep=keep, gain=gain, firs...  7.83 us
    pallas_call x1, Pallas kernels, body(): pl.pallas_call(perforation_kernel, out_shape=(grid, sums, grid, grid, *ho...  1.4 us
    pallas_call x1, Pallas kernels, body(): pl.pallas_call(load_kernel, out_shape=(*faces, grid, grid, grid, grid, ro...  1.36 us
    pallas_call x1, Pallas kernels, body(): pl.pallas_call(functools.partial(start_kernel, scale=1.0 / theta), out_sh...  1.36 us
  transfers between devices with their start and end apart: 26, of which 20 were waited for; matrix products, arithmetic and copies ran while one was open for 0% of the time, Pallas kernels for 2%

profile of v5, /device:TPU:0, one launch (start us, length us, event | category | flops | bytes accessed | tf_op | source)
XLA Modules:
  0.0 61.5 jit_solution(14149486350398709227)
XLA Ops:
  0.6 1.4 %shard_map.104 = (f32[32,128]{1,0:T(8,128)S(1)}, f32[32,128]{1,0:T(8,128)S(1)}, f32[8,128]{1,0:T(8,128)S(1)}, f32[8,128]{1,0:T(8,128)S(1)}, f32[8,32,128]{2,1,0:...) custom-call(f32[2,8]{1,0:T(2,128)} %table_hbm.1, ...), custom_call_target="tpu_custom_call" | custom-call | tf_op jit(solution)/shard_map/pallas_call | solution.py:449
  2.0 3.1 %collective-permute-start = (f32[32,128]{1,0:T(8,128)S(1)}, f32[32,128]{1,0:T(8,128)S(1)}, u32[]{:S(2)}, u32[]{:S(2)}) collective-permute-start(f32[32,128]{1,0:T(8,128)S(1)} %get-tuple-element.53), channel_id=1, source_target_pairs={{0,8},{1,9},{2,10},{3,11},{4,12},{5,13},{6,14},{7,15},{8,0},{9,1},... | collective-permute-start | bytes 49160 | tf_op jit(solution)/shard_map/ppermute | solution.py:31
  5.1 0.0 collective-permute-start.1
  5.1 3.1 %collective-permute-start.3 = (f32[8,128]{1,0:T(8,128)S(1)}, f32[8,128]{1,0:T(8,128)S(1)}, u32[]{:S(2)}, u32[]{:S(2)}) collective-permute-start(f32[8,128]{1,0:T(8,128)S(1)} %get-tuple-element.56), channel_id=1, source_target_pairs={{0,8},{1,2},{2,1},{3,4},{4,3},{5,6},{6,5},{7,15},{8,0},{9,10},{10,... | collective-permute-start | bytes 12296 | tf_op jit(solution)/shard_map/ppermute | solution.py:31
  8.2 1.4 %shard_map.105 = (f32[8,32,128]{2,1,0:T(8,128)S(1)}, f32[40,128]{1,0:T(8,128)S(1)}, f32[8,32,128]{2,1,0:T(8,128)S(1)}, f32[8,32,128]{2,1,0:T(8,128)S(1)}, bf16[2...) custom-call(f32[8,32,128]{2,1,0:T(8,128)S(1)} %get-tuple-element.45., ...), custom_call_target="tpu_custom_call" | custom-call | tf_op jit(solution)/shard_map/pallas_call | solution.py:467
  9.7 0.1 collective-permute-start.2
  9.7 0.1 collective-permute-done.3.xb_ref
  9.8 1.1 %collective-permute-done.2.xa_ref = f32[8,128]{1,0:T(8,128)S(1)} collective-permute-done((f32[8,128]{1,0:T(8,128)S(1)}, f32[8,128]{1,0:T(8,128)S(1)}, u32[]{:S(2)}, u32[]{:S(2)}) %collective-permute-start.2) | collective-permute-done | bytes 4128 | tf_op jit(solution)/shard_map/ppermute | solution.py:31
  10.9 0.0 collective-permute-done.ia_ref
  10.9 0.0 collective-permute-done.1.ib_ref
  10.9 1.4 %shard_map.106 = (f32[8,32,128]{2,1,0:T(8,128)S(1)}, f32[8,32,128]{2,1,0:T(8,128)S(1)}, f32[8,32,128]{2,1,0:T(8,128)S(1)}, f32[8,32,128]{2,1,0:T(8,128)S(1)}, f3...) custom-call(f32[8,32,128]{2,1,0:T(8,128)S(1)} %get-tuple-element.42., ...), custom_call_target="tpu_custom_call" | custom-call | tf_op jit(solution)/shard_map/pallas_call | solution.py:485
  12.3 0.2 collective-permute-start.4
  12.5 1.1 %collective-permute-done.4 = f32[152,128]{1,0:T(8,128)S(1)} collective-permute-done((f32[152,128]{1,0:T(8,128)S(1)}, f32[152,128]{1,0:T(8,128)S(1)}, u32[]{:S(2)}, u32[]{:S(2)}) %collective-permute-start.4) | collective-permute-done | bytes 77856 | tf_op jit(solution)/shard_map/ppermute | solution.py:31
  13.6 1.1 %collective-permute-start.7 = (f32[48,128]{1,0:T(8,128)S(1)}, f32[48,128]{1,0:T(8,128)S(1)}, u32[]{:S(2)}, u32[]{:S(2)}) collective-permute-start(f32[48,128]{1,0:T(8,128)S(1)} %pad_maximum_fusion.6), channel_id=1, source_target_pairs={{0,7},{1,6},{2,5},{3,4},{4,3},{5,2},{6,1},{7,0},{8,15},{9,14},{10,... | collective-permute-start | bytes 73736 | tf_op jit(solution)/shard_map/ppermute | solution.py:31
  14.7 0.2 collective-permute-start.6
  14.9 1.7 %collective-permute-start.5 = (f32[48,128]{1,0:T(8,128)S(1)}, f32[48,128]{1,0:T(8,128)S(1)}, u32[]{:S(2)}, u32[]{:S(2)}) collective-permute-start(f32[48,128]{1,0:T(8,128)S(1)} %pad_maximum_fusion.6), channel_id=1, source_target_pairs={{0,3},{1,2},{2,1},{3,0},{4,7},{5,6},{6,5},{7,4},{8,11},{9,10},{10,... | collective-permute-start | bytes 73736 | tf_op jit(solution)/shard_map/ppermute | solution.py:31
  16.6 1.3 %collective-permute-done.7 = f32[48,128]{1,0:T(8,128)S(1)} collective-permute-done((f32[48,128]{1,0:T(8,128)S(1)}, f32[48,128]{1,0:T(8,128)S(1)}, u32[]{:S(2)}, u32[]{:S(2)}) %collective-permute-start.7) | collective-permute-done | bytes 24608 | tf_op jit(solution)/shard_map/ppermute | solution.py:31
  17.9 0.6 %collective-permute-done.6 = f32[48,128]{1,0:T(8,128)S(1)} collective-permute-done((f32[48,128]{1,0:T(8,128)S(1)}, f32[48,128]{1,0:T(8,128)S(1)}, u32[]{:S(2)}, u32[]{:S(2)}) %collective-permute-start.6) | collective-permute-done | bytes 24608 | tf_op jit(solution)/shard_map/ppermute | solution.py:31
  18.5 0.0 collective-permute-done.5
  18.6 2.1 %collective-permute-start.9 = (f32[72,128]{1,0:T(8,128)S(1)}, f32[72,128]{1,0:T(8,128)S(1)}, u32[]{:S(2)}, u32[]{:S(2)}) collective-permute-start(f32[72,128]{1,0:T(8,128)S(1)} %get-tuple-element.94), channel_id=1, source_target_pairs={{0,25},{1,24},{2,27},{3,26},{4,29},{5,28},{6,31},{7,30},{8,17},{9,... | collective-permute-start | bytes 110600 | tf_op jit(solution)/shard_map/ppermute | solution.py:31
  20.6 0.8 %collective-permute-start.8 = (f32[72,128]{1,0:T(8,128)S(1)}, f32[72,128]{1,0:T(8,128)S(1)}, u32[]{:S(2)}, u32[]{:S(2)}) collective-permute-start(f32[72,128]{1,0:T(8,128)S(1)} %get-tuple-element.95), channel_id=1, source_target_pairs={{0,8},{1,9},{2,10},{3,11},{4,12},{5,13},{6,14},{7,15},{8,0},{9,1},... | collective-permute-start | bytes 110600 | tf_op jit(solution)/shard_map/ppermute | solution.py:31
  21.4 1.1 %collective-permute-start.10 = (f32[40,128]{1,0:T(8,128)S(1)}, f32[40,128]{1,0:T(8,128)S(1)}, u32[]{:S(2)}, u32[]{:S(2)}) collective-permute-start(f32[40,128]{1,0:T(8,128)S(1)} %slice_add_fusion.15), channel_id=1, source_target_pairs={{0,17},{1,16},{2,19},{3,18},{4,21},{5,20},{6,23},{7,22},{8,25},{9,... | collective-permute-start | bytes 61448 | tf_op jit(solution)/shard_map/ppermute | solution.py:31
  22.5 3.2 %collective-permute-done.10 = f32[40,128]{1,0:T(8,128)S(1)} collective-permute-done((f32[40,128]{1,0:T(8,128)S(1)}, f32[40,128]{1,0:T(8,128)S(1)}, u32[]{:S(2)}, u32[]{:S(2)}) %collective-permute-start.10) | collective-permute-done | bytes 20512 | tf_op jit(solution)/shard_map/ppermute | solution.py:31
  25.8 0.0 collective-permute-done.9
  25.8 0.0 collective-permute-done.8
  25.8 0.2 collective-permute-start.11
  26.0 1.1 %collective-permute-done.11 = f32[40,128]{1,0:T(8,128)S(1)} collective-permute-done((f32[40,128]{1,0:T(8,128)S(1)}, f32[40,128]{1,0:T(8,128)S(1)}, u32[]{:S(2)}, u32[]{:S(2)}) %collective-permute-start.11) | collective-permute-done | bytes 20512 | tf_op jit(solution)/shard_map/ppermute | solution.py:31
  27.0 3.0 %shard_map.107 = (f32[8,32,128]{2,1,0:T(8,128)S(1)}, f32[8,32,128]{2,1,0:T(8,128)S(1)}, f32[8,32,128]{2,1,0:T(8,128)S(1)}, f32[112,128]{1,0:T(8,128)S(1)}, f32[8,128]{1,0:T(8,128)S(1)}) custom-call(f32[8,32,128]{2,1,0:T(8,128)S(1)} %get-tuple-element.42.right_ref.refs_0_.refs_2_, f32[8,32,128]{2,1,0:T(8,128)S(1)} %get-tuple-element.62.refs_1_, ...), custom_call_target="tpu_custom_call" | custom-call | tf_op jit(solution)/shard_map/pallas_call | solution.py:508
  30.1 0.2 collective-permute-start.12
  30.3 1.1 %collective-permute-done.12 = f32[112,128]{1,0:T(8,128)S(1)} collective-permute-done((f32[112,128]{1,0:T(8,128)S(1)}, f32[112,128]{1,0:T(8,128)S(1)}, u32[]{:S(2)}, u32[]{:S(2)}) %collective-permute-start.12) | collective-permute-done | bytes 57376 | tf_op jit(solution)/shard_map/ppermute | solution.py:31
  31.4 1.3 %collective-permute-start.15 = (f32[48,128]{1,0:T(8,128)S(1)}, f32[48,128]{1,0:T(8,128)S(1)}, u32[]{:S(2)}, u32[]{:S(2)}) collective-permute-start(f32[48,128]{1,0:T(8,128)S(1)} %pad_maximum_fusion.7), channel_id=1, source_target_pairs={{0,7},{1,6},{2,5},{3,4},{4,3},{5,2},{6,1},{7,0},{8,15},{9,14},{10,... | collective-permute-start | bytes 73736 | tf_op jit(solution)/shard_map/ppermute | solution.py:31
  32.7 0.7 %collective-permute-start.14 = (f32[48,128]{1,0:T(8,128)S(1)}, f32[48,128]{1,0:T(8,128)S(1)}, u32[]{:S(2)}, u32[]{:S(2)}) collective-permute-start(f32[48,128]{1,0:T(8,128)S(1)} %pad_maximum_fusion.7), channel_id=1, source_target_pairs={{0,5},{1,4},{2,7},{3,6},{4,1},{5,0},{6,3},{7,2},{8,13},{9,12},{10,... | collective-permute-start | bytes 73736 | tf_op jit(solution)/shard_map/ppermute | solution.py:31
  33.3 1.1 %collective-permute-start.13 = (f32[48,128]{1,0:T(8,128)S(1)}, f32[48,128]{1,0:T(8,128)S(1)}, u32[]{:S(2)}, u32[]{:S(2)}) collective-permute-start(f32[48,128]{1,0:T(8,128)S(1)} %pad_maximum_fusion.7), channel_id=1, source_target_pairs={{0,3},{1,2},{2,1},{3,0},{4,7},{5,6},{6,5},{7,4},{8,11},{9,10},{10,... | collective-permute-start | bytes 73736 | tf_op jit(solution)/shard_map/ppermute | solution.py:31
  34.4 1.2 %collective-permute-done.15 = f32[48,128]{1,0:T(8,128)S(1)} collective-permute-done((f32[48,128]{1,0:T(8,128)S(1)}, f32[48,128]{1,0:T(8,128)S(1)}, u32[]{:S(2)}, u32[]{:S(2)}) %collective-permute-start.15) | collective-permute-done | bytes 24608 | tf_op jit(solution)/shard_map/ppermute | solution.py:31
  35.6 0.6 collective-permute-done.14
  36.2 0.4 collective-permute-done.13
  36.6 2.2 %collective-permute-start.17 = (f32[72,128]{1,0:T(8,128)S(1)}, f32[72,128]{1,0:T(8,128)S(1)}, u32[]{:S(2)}, u32[]{:S(2)}) collective-permute-start(f32[72,128]{1,0:T(8,128)S(1)} %get-tuple-element.92), channel_id=1, source_target_pairs={{0,25},{1,24},{2,27},{3,26},{4,29},{5,28},{6,31},{7,30},{8,17},{9,... | collective-permute-start | bytes 110600 | tf_op jit(solution)/shard_map/ppermute | solution.py:31
  38.8 0.2 collective-permute-start.16
  39.0 1.6 %collective-permute-start.18 = (f32[40,128]{1,0:T(8,128)S(1)}, f32[40,128]{1,0:T(8,128)S(1)}, u32[]{:S(2)}, u32[]{:S(2)}) collective-permute-start(f32[40,128]{1,0:T(8,128)S(1)} %slice_add_fusion.9), channel_id=1, source_target_pairs={{0,17},{1,16},{2,19},{3,18},{4,21},{5,20},{6,23},{7,22},{8,25},{9,... | collective-permute-start | bytes 61448 | tf_op jit(solution)/shard_map/ppermute | solution.py:31
  40.6 1.4 %collective-permute-done.17 = f32[72,128]{1,0:T(8,128)S(1)} collective-permute-done((f32[72,128]{1,0:T(8,128)S(1)}, f32[72,128]{1,0:T(8,128)S(1)}, u32[]{:S(2)}, u32[]{:S(2)}) %collective-permute-start.17) | collective-permute-done | bytes 36896 | tf_op jit(solution)/shard_map/ppermute | solution.py:31
  41.9 0.9 %collective-permute-done.16 = f32[72,128]{1,0:T(8,128)S(1)} collective-permute-done((f32[72,128]{1,0:T(8,128)S(1)}, f32[72,128]{1,0:T(8,128)S(1)}, u32[]{:S(2)}, u32[]{:S(2)}) %collective-permute-start.16) | collective-permute-done | bytes 36896 | tf_op jit(solution)/shard_map/ppermute | solution.py:31
  42.8 0.3 collective-permute-done.18
  43.1 3.0 %shard_map.108 = (f32[8,32,128]{2,1,0:T(8,128)S(1)}, f32[8,32,128]{2,1,0:T(8,128)S(1)}, f32[8,32,128]{2,1,0:T(8,128)S(1)}, f32[112,128]{1,0:T(8,128)S(1)}, f32[8,128]{1,0:T(8,128)S(1)}) custom-call(f32[8,32,128]{2,1,0:T(8,128)S(1)} %get-tuple-element.72.refs_0_, f32[8,32,128]{2,1,0:T(8,128)S(1)} %get-tuple-element.73.refs_1_, ...), custom_call_target="tpu_custom_call" | custom-call | tf_op jit(solution)/shard_map/pallas_call | solution.py:508
  46.2 0.2 collective-permute-start.19
  46.4 1.0 %collective-permute-done.19 = f32[112,128]{1,0:T(8,128)S(1)} collective-permute-done((f32[112,128]{1,0:T(8,128)S(1)}, f32[112,128]{1,0:T(8,128)S(1)}, u32[]{:S(2)}, u32[]{:S(2)}) %collective-permute-start.19) | collective-permute-done | bytes 57376 | tf_op jit(solution)/shard_map/ppermute | solution.py:31
  47.5 1.3 %collective-permute-start.22 = (f32[48,128]{1,0:T(8,128)S(1)}, f32[48,128]{1,0:T(8,128)S(1)}, u32[]{:S(2)}, u32[]{:S(2)}) collective-permute-start(f32[48,128]{1,0:T(8,128)S(1)} %pad_maximum_fusion.8), channel_id=1, source_target_pairs={{0,7},{1,6},{2,5},{3,4},{4,3},{5,2},{6,1},{7,0},{8,15},{9,14},{10,... | collective-permute-start | bytes 73736 | tf_op jit(solution)/shard_map/ppermute | solution.py:31
  48.7 1.5 %collective-permute-start.21 = (f32[48,128]{1,0:T(8,128)S(1)}, f32[48,128]{1,0:T(8,128)S(1)}, u32[]{:S(2)}, u32[]{:S(2)}) collective-permute-start(f32[48,128]{1,0:T(8,128)S(1)} %pad_maximum_fusion.8), channel_id=1, source_target_pairs={{0,5},{1,4},{2,7},{3,6},{4,1},{5,0},{6,3},{7,2},{8,13},{9,12},{10,... | collective-permute-start | bytes 73736 | tf_op jit(solution)/shard_map/ppermute | solution.py:31
  50.2 0.3 collective-permute-start.20
  50.6 1.1 %collective-permute-done.22 = f32[48,128]{1,0:T(8,128)S(1)} collective-permute-done((f32[48,128]{1,0:T(8,128)S(1)}, f32[48,128]{1,0:T(8,128)S(1)}, u32[]{:S(2)}, u32[]{:S(2)}) %collective-permute-start.22) | collective-permute-done | bytes 24608 | tf_op jit(solution)/shard_map/ppermute | solution.py:31
  51.7 0.6 collective-permute-done.21
  52.2 1.3 %collective-permute-done.20 = f32[48,128]{1,0:T(8,128)S(1)} collective-permute-done((f32[48,128]{1,0:T(8,128)S(1)}, f32[48,128]{1,0:T(8,128)S(1)}, u32[]{:S(2)}, u32[]{:S(2)}) %collective-permute-start.20) | collective-permute-done | bytes 24608 | tf_op jit(solution)/shard_map/ppermute | solution.py:31
  53.5 1.6 %collective-permute-start.24 = (f32[72,128]{1,0:T(8,128)S(1)}, f32[72,128]{1,0:T(8,128)S(1)}, u32[]{:S(2)}, u32[]{:S(2)}) collective-permute-start(f32[72,128]{1,0:T(8,128)S(1)} %get-tuple-element.90), channel_id=1, source_target_pairs={{0,25},{1,24},{2,27},{3,26},{4,29},{5,28},{6,31},{7,30},{8,17},{9,... | collective-permute-start | bytes 110600 | tf_op jit(solution)/shard_map/ppermute | solution.py:31
  55.1 0.5 collective-permute-start.23
  55.6 1.9 %collective-permute-start.25 = (f32[40,128]{1,0:T(8,128)S(1)}, f32[40,128]{1,0:T(8,128)S(1)}, u32[]{:S(2)}, u32[]{:S(2)}) collective-permute-start(f32[40,128]{1,0:T(8,128)S(1)} %slice_add_fusion.3), channel_id=1, source_target_pairs={{0,17},{1,16},{2,19},{3,18},{4,21},{5,20},{6,23},{7,22},{8,25},{9,... | collective-permute-start | bytes 61448 | tf_op jit(solution)/shard_map/ppermute | solution.py:31
  57.6 1.4 %collective-permute-done.24 = f32[72,128]{1,0:T(8,128)S(1)} collective-permute-done((f32[72,128]{1,0:T(8,128)S(1)}, f32[72,128]{1,0:T(8,128)S(1)}, u32[]{:S(2)}, u32[]{:S(2)}) %collective-permute-start.24) | collective-permute-done | bytes 36896 | tf_op jit(solution)/shard_map/ppermute | solution.py:31
  58.9 0.0 collective-permute-done.23
  58.9 0.8 %collective-permute-done.25 = f32[40,128]{1,0:T(8,128)S(1)} collective-permute-done((f32[40,128]{1,0:T(8,128)S(1)}, f32[40,128]{1,0:T(8,128)S(1)}, u32[]{:S(2)}, u32[]{:S(2)}) %collective-permute-start.25) | collective-permute-done | bytes 20512 | tf_op jit(solution)/shard_map/ppermute | solution.py:31
  59.7 1.7 %shard_map.109 = (f32[8,32,128]{2,1,0:T(8,128)}, f32[8,32,128]{2,1,0:T(8,128)}) custom-call(f32[8,32,128]{2,1,0:T(8,128)S(1)} %get-tuple-element.77.refs_0_, f32[8,32,128]{2,1,0:T(8,128)S(1)} %get-tuple-element.78.refs_1_, f32[8,32,128]{2,1,0:T(8,128)S(1)} %get-tuple-element.79.refs_2_, f32[8,32,128]{2,1,0:T(8,128)S(1)} %get-tuple-element.63.refs_3_, ...), custom_call_target="tpu_custom_call" | custom-call | tf_op jit(solution)/shard_map/pallas_call | solution.py:508
  (36 shorter events, 0.2 us)
Async XLA Ops:
  2.0 8.9 %collective-permute-start = (f32[32,128]{1,0:T(8,128)S(1)}, f32[32,128]{1,0:T(8,128)S(1)}, u32[]{:S(2)}, u32[]{:S(2)}) collective-permute-start(f32[32,128]{1,0:T(8,128)S(1)} %get-tuple-element.53), channel_id=1, source_target_pairs={{0,8},{1,9},{2,10},{3,11},{4,12},{5,13},{6,14},{7,15},{8,0},{9,1},... | collective-permute-start | bytes 49160 | tf_op jit(solution)/shard_map/ppermute | solution.py:31
  5.1 5.8 %collective-permute-start.1 = (f32[32,128]{1,0:T(8,128)S(1)}, f32[32,128]{1,0:T(8,128)S(1)}, u32[]{:S(2)}, u32[]{:S(2)}) collective-permute-start(f32[32,128]{1,0:T(8,128)S(1)} %get-tuple-element.54), channel_id=1, source_target_pairs={{0,1},{1,0},{2,3},{3,2},{4,5},{5,4},{6,7},{7,6},{8,16},{9,17},{10,... | collective-permute-start | bytes 49160 | tf_op jit(solution)/shard_map/ppermute | solution.py:31
  5.1 4.7 %collective-permute-start.3 = (f32[8,128]{1,0:T(8,128)S(1)}, f32[8,128]{1,0:T(8,128)S(1)}, u32[]{:S(2)}, u32[]{:S(2)}) collective-permute-start(f32[8,128]{1,0:T(8,128)S(1)} %get-tuple-element.56), channel_id=1, source_target_pairs={{0,8},{1,2},{2,1},{3,4},{4,3},{5,6},{6,5},{7,15},{8,0},{9,10},{10,... | collective-permute-start | bytes 12296 | tf_op jit(solution)/shard_map/ppermute | solution.py:31
  9.7 1.2 %collective-permute-start.2 = (f32[8,128]{1,0:T(8,128)S(1)}, f32[8,128]{1,0:T(8,128)S(1)}, u32[]{:S(2)}, u32[]{:S(2)}) collective-permute-start(f32[8,128]{1,0:T(8,128)S(1)} %get-tuple-element.55), channel_id=1, source_target_pairs={{0,1},{1,0},{2,3},{3,2},{4,5},{5,4},{6,7},{7,6},{8,9},{9,8},{10,11... | collective-permute-start | bytes 12296 | tf_op jit(solution)/shard_map/ppermute | solution.py:31
  12.3 1.3 %collective-permute-start.4 = (f32[152,128]{1,0:T(8,128)S(1)}, f32[152,128]{1,0:T(8,128)S(1)}, u32[]{:S(2)}, u32[]{:S(2)}) collective-permute-start(f32[152,128]{1,0:T(8,128)S(1)} %get-tuple-element.70), channel_id=1, source_target_pairs={{0,1},{1,0},{2,3},{3,2},{4,5},{5,4},{6,7},{7,6},{8,9},{9,8},{10,11... | collective-permute-start | bytes 233480 | tf_op jit(solution)/shard_map/ppermute | solution.py:31
  13.6 4.3 %collective-permute-start.7 = (f32[48,128]{1,0:T(8,128)S(1)}, f32[48,128]{1,0:T(8,128)S(1)}, u32[]{:S(2)}, u32[]{:S(2)}) collective-permute-start(f32[48,128]{1,0:T(8,128)S(1)} %pad_maximum_fusion.6), channel_id=1, source_target_pairs={{0,7},{1,6},{2,5},{3,4},{4,3},{5,2},{6,1},{7,0},{8,15},{9,14},{10,... | collective-permute-start | bytes 73736 | tf_op jit(solution)/shard_map/ppermute | solution.py:31
  14.7 3.8 %collective-permute-start.6 = (f32[48,128]{1,0:T(8,128)S(1)}, f32[48,128]{1,0:T(8,128)S(1)}, u32[]{:S(2)}, u32[]{:S(2)}) collective-permute-start(f32[48,128]{1,0:T(8,128)S(1)} %pad_maximum_fusion.6), channel_id=1, source_target_pairs={{0,4},{1,5},{2,6},{3,7},{4,0},{5,1},{6,2},{7,3},{8,12},{9,13},{10,... | collective-permute-start | bytes 73736 | tf_op jit(solution)/shard_map/ppermute | solution.py:31
  14.9 3.7 %collective-permute-start.5 = (f32[48,128]{1,0:T(8,128)S(1)}, f32[48,128]{1,0:T(8,128)S(1)}, u32[]{:S(2)}, u32[]{:S(2)}) collective-permute-start(f32[48,128]{1,0:T(8,128)S(1)} %pad_maximum_fusion.6), channel_id=1, source_target_pairs={{0,3},{1,2},{2,1},{3,0},{4,7},{5,6},{6,5},{7,4},{8,11},{9,10},{10,... | collective-permute-start | bytes 73736 | tf_op jit(solution)/shard_map/ppermute | solution.py:31
  18.6 7.2 %collective-permute-start.9 = (f32[72,128]{1,0:T(8,128)S(1)}, f32[72,128]{1,0:T(8,128)S(1)}, u32[]{:S(2)}, u32[]{:S(2)}) collective-permute-start(f32[72,128]{1,0:T(8,128)S(1)} %get-tuple-element.94), channel_id=1, source_target_pairs={{0,25},{1,24},{2,27},{3,26},{4,29},{5,28},{6,31},{7,30},{8,17},{9,... | collective-permute-start | bytes 110600 | tf_op jit(solution)/shard_map/ppermute | solution.py:31
  20.6 5.1 %collective-permute-start.8 = (f32[72,128]{1,0:T(8,128)S(1)}, f32[72,128]{1,0:T(8,128)S(1)}, u32[]{:S(2)}, u32[]{:S(2)}) collective-permute-start(f32[72,128]{1,0:T(8,128)S(1)} %get-tuple-element.95), channel_id=1, source_target_pairs={{0,8},{1,9},{2,10},{3,11},{4,12},{5,13},{6,14},{7,15},{8,0},{9,1},... | collective-permute-start | bytes 110600 | tf_op jit(solution)/shard_map/ppermute | solution.py:31
  21.4 4.3 %collective-permute-start.10 = (f32[40,128]{1,0:T(8,128)S(1)}, f32[40,128]{1,0:T(8,128)S(1)}, u32[]{:S(2)}, u32[]{:S(2)}) collective-permute-start(f32[40,128]{1,0:T(8,128)S(1)} %slice_add_fusion.15), channel_id=1, source_target_pairs={{0,17},{1,16},{2,19},{3,18},{4,21},{5,20},{6,23},{7,22},{8,25},{9,... | collective-permute-start | bytes 61448 | tf_op jit(solution)/shard_map/ppermute | solution.py:31
  25.8 1.3 %collective-permute-start.11 = (f32[40,128]{1,0:T(8,128)S(1)}, f32[40,128]{1,0:T(8,128)S(1)}, u32[]{:S(2)}, u32[]{:S(2)}) collective-permute-start(f32[40,128]{1,0:T(8,128)S(1)} %slice_add_fusion.13), channel_id=1, source_target_pairs={{0,1},{1,0},{2,3},{3,2},{4,5},{5,4},{6,7},{7,6},{8,9},{9,8},{10,11... | collective-permute-start | bytes 61448 | tf_op jit(solution)/shard_map/ppermute | solution.py:31
  30.1 1.3 %collective-permute-start.12 = (f32[112,128]{1,0:T(8,128)S(1)}, f32[112,128]{1,0:T(8,128)S(1)}, u32[]{:S(2)}, u32[]{:S(2)}) collective-permute-start(f32[112,128]{1,0:T(8,128)S(1)} %get-tuple-element.75), channel_id=1, source_target_pairs={{0,1},{1,0},{2,3},{3,2},{4,5},{5,4},{6,7},{7,6},{8,9},{9,8},{10,11... | collective-permute-start | bytes 172040 | tf_op jit(solution)/shard_map/ppermute | solution.py:31
  31.4 4.2 %collective-permute-start.15 = (f32[48,128]{1,0:T(8,128)S(1)}, f32[48,128]{1,0:T(8,128)S(1)}, u32[]{:S(2)}, u32[]{:S(2)}) collective-permute-start(f32[48,128]{1,0:T(8,128)S(1)} %pad_maximum_fusion.7), channel_id=1, source_target_pairs={{0,7},{1,6},{2,5},{3,4},{4,3},{5,2},{6,1},{7,0},{8,15},{9,14},{10,... | collective-permute-start | bytes 73736 | tf_op jit(solution)/shard_map/ppermute | solution.py:31
  32.7 3.5 %collective-permute-start.14 = (f32[48,128]{1,0:T(8,128)S(1)}, f32[48,128]{1,0:T(8,128)S(1)}, u32[]{:S(2)}, u32[]{:S(2)}) collective-permute-start(f32[48,128]{1,0:T(8,128)S(1)} %pad_maximum_fusion.7), channel_id=1, source_target_pairs={{0,5},{1,4},{2,7},{3,6},{4,1},{5,0},{6,3},{7,2},{8,13},{9,12},{10,... | collective-permute-start | bytes 73736 | tf_op jit(solution)/shard_map/ppermute | solution.py:31
  33.3 3.3 %collective-permute-start.13 = (f32[48,128]{1,0:T(8,128)S(1)}, f32[48,128]{1,0:T(8,128)S(1)}, u32[]{:S(2)}, u32[]{:S(2)}) collective-permute-start(f32[48,128]{1,0:T(8,128)S(1)} %pad_maximum_fusion.7), channel_id=1, source_target_pairs={{0,3},{1,2},{2,1},{3,0},{4,7},{5,6},{6,5},{7,4},{8,11},{9,10},{10,... | collective-permute-start | bytes 73736 | tf_op jit(solution)/shard_map/ppermute | solution.py:31
  36.6 5.3 %collective-permute-start.17 = (f32[72,128]{1,0:T(8,128)S(1)}, f32[72,128]{1,0:T(8,128)S(1)}, u32[]{:S(2)}, u32[]{:S(2)}) collective-permute-start(f32[72,128]{1,0:T(8,128)S(1)} %get-tuple-element.92), channel_id=1, source_target_pairs={{0,25},{1,24},{2,27},{3,26},{4,29},{5,28},{6,31},{7,30},{8,17},{9,... | collective-permute-start | bytes 110600 | tf_op jit(solution)/shard_map/ppermute | solution.py:31
  38.8 4.1 %collective-permute-start.16 = (f32[72,128]{1,0:T(8,128)S(1)}, f32[72,128]{1,0:T(8,128)S(1)}, u32[]{:S(2)}, u32[]{:S(2)}) collective-permute-start(f32[72,128]{1,0:T(8,128)S(1)} %get-tuple-element.93), channel_id=1, source_target_pairs={{0,9},{1,8},{2,11},{3,10},{4,13},{5,12},{6,15},{7,14},{8,1},{9,0},... | collective-permute-start | bytes 110600 | tf_op jit(solution)/shard_map/ppermute | solution.py:31
  39.0 4.1 %collective-permute-start.18 = (f32[40,128]{1,0:T(8,128)S(1)}, f32[40,128]{1,0:T(8,128)S(1)}, u32[]{:S(2)}, u32[]{:S(2)}) collective-permute-start(f32[40,128]{1,0:T(8,128)S(1)} %slice_add_fusion.9), channel_id=1, source_target_pairs={{0,17},{1,16},{2,19},{3,18},{4,21},{5,20},{6,23},{7,22},{8,25},{9,... | collective-permute-start | bytes 61448 | tf_op jit(solution)/shard_map/ppermute | solution.py:31
  46.2 1.3 %collective-permute-start.19 = (f32[112,128]{1,0:T(8,128)S(1)}, f32[112,128]{1,0:T(8,128)S(1)}, u32[]{:S(2)}, u32[]{:S(2)}) collective-permute-start(f32[112,128]{1,0:T(8,128)S(1)} %get-tuple-element.80), channel_id=1, source_target_pairs={{0,1},{1,0},{2,3},{3,2},{4,5},{5,4},{6,7},{7,6},{8,9},{9,8},{10,11... | collective-permute-start | bytes 172040 | tf_op jit(solution)/shard_map/ppermute | solution.py:31
  47.5 4.2 %collective-permute-start.22 = (f32[48,128]{1,0:T(8,128)S(1)}, f32[48,128]{1,0:T(8,128)S(1)}, u32[]{:S(2)}, u32[]{:S(2)}) collective-permute-start(f32[48,128]{1,0:T(8,128)S(1)} %pad_maximum_fusion.8), channel_id=1, source_target_pairs={{0,7},{1,6},{2,5},{3,4},{4,3},{5,2},{6,1},{7,0},{8,15},{9,14},{10,... | collective-permute-start | bytes 73736 | tf_op jit(solution)/shard_map/ppermute | solution.py:31
  48.7 3.5 %collective-permute-start.21 = (f32[48,128]{1,0:T(8,128)S(1)}, f32[48,128]{1,0:T(8,128)S(1)}, u32[]{:S(2)}, u32[]{:S(2)}) collective-permute-start(f32[48,128]{1,0:T(8,128)S(1)} %pad_maximum_fusion.8), channel_id=1, source_target_pairs={{0,5},{1,4},{2,7},{3,6},{4,1},{5,0},{6,3},{7,2},{8,13},{9,12},{10,... | collective-permute-start | bytes 73736 | tf_op jit(solution)/shard_map/ppermute | solution.py:31
  50.2 3.3 %collective-permute-start.20 = (f32[48,128]{1,0:T(8,128)S(1)}, f32[48,128]{1,0:T(8,128)S(1)}, u32[]{:S(2)}, u32[]{:S(2)}) collective-permute-start(f32[48,128]{1,0:T(8,128)S(1)} %pad_maximum_fusion.8), channel_id=1, source_target_pairs={{0,3},{1,2},{2,1},{3,0},{4,7},{5,6},{6,5},{7,4},{8,11},{9,10},{10,... | collective-permute-start | bytes 73736 | tf_op jit(solution)/shard_map/ppermute | solution.py:31
  53.5 5.4 %collective-permute-start.24 = (f32[72,128]{1,0:T(8,128)S(1)}, f32[72,128]{1,0:T(8,128)S(1)}, u32[]{:S(2)}, u32[]{:S(2)}) collective-permute-start(f32[72,128]{1,0:T(8,128)S(1)} %get-tuple-element.90), channel_id=1, source_target_pairs={{0,25},{1,24},{2,27},{3,26},{4,29},{5,28},{6,31},{7,30},{8,17},{9,... | collective-permute-start | bytes 110600 | tf_op jit(solution)/shard_map/ppermute | solution.py:31
  55.1 3.8 %collective-permute-start.23 = (f32[72,128]{1,0:T(8,128)S(1)}, f32[72,128]{1,0:T(8,128)S(1)}, u32[]{:S(2)}, u32[]{:S(2)}) collective-permute-start(f32[72,128]{1,0:T(8,128)S(1)} %get-tuple-element.91), channel_id=1, source_target_pairs={{0,9},{1,8},{2,11},{3,10},{4,13},{5,12},{6,15},{7,14},{8,1},{9,0},... | collective-permute-start | bytes 110600 | tf_op jit(solution)/shard_map/ppermute | solution.py:31
  55.6 4.1 %collective-permute-start.25 = (f32[40,128]{1,0:T(8,128)S(1)}, f32[40,128]{1,0:T(8,128)S(1)}, u32[]{:S(2)}, u32[]{:S(2)}) collective-permute-start(f32[40,128]{1,0:T(8,128)S(1)} %slice_add_fusion.3), channel_id=1, source_target_pairs={{0,17},{1,16},{2,19},{3,18},{4,21},{5,20},{6,23},{7,22},{8,25},{9,... | collective-permute-start | bytes 61448 | tf_op jit(solution)/shard_map/ppermute | solution.py:31

commit v6 on v5

--- a/solution.py
+++ b/solution.py
@@ -268,7 +268,7 @@
     ]
     for copy in copies:
         copy.start()
-    for copy in copies:
+    for copy in copies[:3]:
         copy.wait()
     facies, thickness = facies_ref[...], thickness_ref[...]
     lateral = lookup(facies, table_ref, 0) * thickness
@@ -276,6 +276,8 @@
     vertical_ref[...] = lookup(facies, table_ref, 1) / thickness
     ia_ref[...], ib_ref[...] = side_faces(lateral, "inline")
     xa_ref[...], xb_ref[...] = side_faces(lateral, "xline")
+    for copy in copies[3:]:
+        copy.wait()
     number_ref[...] = owner_ref[...] * WELL_DEV + well_ref[...]
 
 

time: 61.7 us -> 61.5 us (level)
  no operation moved by 1% of the time
where the time goes in v6:
time: 61.5 us; the launch traced here: 61.4 us
  starting transfers between devices  28.2 us (46%)
  waiting for transfers between devices  20.4 us (33%)
  Pallas kernels  11.8 us (19%)
  between operations  0.76 us (1%)
    ppermute x26, starting transfers between devices, pair_permute(): return lax.ppermute(value, MESH_AXES, pairs)  28.2 us
    ppermute x26, waiting for transfers between devices, pair_permute(): return lax.ppermute(value, MESH_AXES, pairs)  20.4 us
    pallas_call x3, Pallas kernels, body(): pl.pallas_call(functools.partial(sweep_kernel, keep=keep, gain=gain, firs...  7.83 us
    pallas_call x1, Pallas kernels, body(): pl.pallas_call(perforation_kernel, out_shape=(grid, sums, grid, grid, *ho...  1.4 us
    pallas_call x1, Pallas kernels, body(): pl.pallas_call(functools.partial(start_kernel, scale=1.0 / theta), out_sh...  1.36 us
  transfers between devices with their start and end apart: 26, of which 20 were waited for; matrix products, arithmetic and copies ran while one was open for 0% of the time, Pallas kernels for 2%

profile of v6, /device:TPU:0, one launch (start us, length us, event | category | flops | bytes accessed | tf_op | source)
XLA Modules:
  0.0 61.4 jit_solution(7661018530911062137)
XLA Ops:
  0.6 1.2 %shard_map.104 = (f32[32,128]{1,0:T(8,128)S(1)}, f32[32,128]{1,0:T(8,128)S(1)}, f32[8,128]{1,0:T(8,128)S(1)}, f32[8,128]{1,0:T(8,128)S(1)}, f32[8,32,128]{2,1,0:...) custom-call(f32[2,8]{1,0:T(2,128)} %table_hbm.1, ...), custom_call_target="tpu_custom_call" | custom-call | tf_op jit(solution)/shard_map/pallas_call | solution.py:451
  1.9 3.1 %collective-permute-start = (f32[32,128]{1,0:T(8,128)S(1)}, f32[32,128]{1,0:T(8,128)S(1)}, u32[]{:S(2)}, u32[]{:S(2)}) collective-permute-start(f32[32,128]{1,0:T(8,128)S(1)} %get-tuple-element.53), channel_id=1, source_target_pairs={{0,8},{1,9},{2,10},{3,11},{4,12},{5,13},{6,14},{7,15},{8,0},{9,1},... | collective-permute-start | bytes 49160 | tf_op jit(solution)/shard_map/ppermute | solution.py:31
  5.0 0.0 collective-permute-start.1
  5.0 3.1 %collective-permute-start.3 = (f32[8,128]{1,0:T(8,128)S(1)}, f32[8,128]{1,0:T(8,128)S(1)}, u32[]{:S(2)}, u32[]{:S(2)}) collective-permute-start(f32[8,128]{1,0:T(8,128)S(1)} %get-tuple-element.56), channel_id=1, source_target_pairs={{0,8},{1,2},{2,1},{3,4},{4,3},{5,6},{6,5},{7,15},{8,0},{9,10},{10,... | collective-permute-start | bytes 12296 | tf_op jit(solution)/shard_map/ppermute | solution.py:31
  8.1 1.4 %shard_map.105 = (f32[8,32,128]{2,1,0:T(8,128)S(1)}, f32[40,128]{1,0:T(8,128)S(1)}, f32[8,32,128]{2,1,0:T(8,128)S(1)}, f32[8,32,128]{2,1,0:T(8,128)S(1)}, bf16[2...) custom-call(f32[8,32,128]{2,1,0:T(8,128)S(1)} %get-tuple-element.45., ...), custom_call_target="tpu_custom_call" | custom-call | tf_op jit(solution)/shard_map/pallas_call | solution.py:469
  9.5 0.1 collective-permute-start.2
  9.6 0.1 collective-permute-done.3.xb_ref
  9.7 1.1 %collective-permute-done.2.xa_ref = f32[8,128]{1,0:T(8,128)S(1)} collective-permute-done((f32[8,128]{1,0:T(8,128)S(1)}, f32[8,128]{1,0:T(8,128)S(1)}, u32[]{:S(2)}, u32[]{:S(2)}) %collective-permute-start.2) | collective-permute-done | bytes 4128 | tf_op jit(solution)/shard_map/ppermute | solution.py:31
  10.7 0.0 collective-permute-done.ia_ref
  10.7 0.0 collective-permute-done.1.ib_ref
  10.8 1.4 %shard_map.106 = (f32[8,32,128]{2,1,0:T(8,128)S(1)}, f32[8,32,128]{2,1,0:T(8,128)S(1)}, f32[8,32,128]{2,1,0:T(8,128)S(1)}, f32[8,32,128]{2,1,0:T(8,128)S(1)}, f3...) custom-call(f32[8,32,128]{2,1,0:T(8,128)S(1)} %get-tuple-element.42., ...), custom_call_target="tpu_custom_call" | custom-call | tf_op jit(solution)/shard_map/pallas_call | solution.py:487
  12.1 0.2 collective-permute-start.4
  12.3 1.1 %collective-permute-done.4 = f32[152,128]{1,0:T(8,128)S(1)} collective-permute-done((f32[152,128]{1,0:T(8,128)S(1)}, f32[152,128]{1,0:T(8,128)S(1)}, u32[]{:S(2)}, u32[]{:S(2)}) %collective-permute-start.4) | collective-permute-done | bytes 77856 | tf_op jit(solution)/shard_map/ppermute | solution.py:31
  13.5 1.1 %collective-permute-start.7 = (f32[48,128]{1,0:T(8,128)S(1)}, f32[48,128]{1,0:T(8,128)S(1)}, u32[]{:S(2)}, u32[]{:S(2)}) collective-permute-start(f32[48,128]{1,0:T(8,128)S(1)} %pad_maximum_fusion.6), channel_id=1, source_target_pairs={{0,7},{1,6},{2,5},{3,4},{4,3},{5,2},{6,1},{7,0},{8,15},{9,14},{10,... | collective-permute-start | bytes 73736 | tf_op jit(solution)/shard_map/ppermute | solution.py:31
  14.6 0.2 collective-permute-start.6
  14.7 1.7 %collective-permute-start.5 = (f32[48,128]{1,0:T(8,128)S(1)}, f32[48,128]{1,0:T(8,128)S(1)}, u32[]{:S(2)}, u32[]{:S(2)}) collective-permute-start(f32[48,128]{1,0:T(8,128)S(1)} %pad_maximum_fusion.6), channel_id=1, source_target_pairs={{0,3},{1,2},{2,1},{3,0},{4,7},{5,6},{6,5},{7,4},{8,11},{9,10},{10,... | collective-permute-start | bytes 73736 | tf_op jit(solution)/shard_map/ppermute | solution.py:31
  16.5 1.3 %collective-permute-done.7 = f32[48,128]{1,0:T(8,128)S(1)} collective-permute-done((f32[48,128]{1,0:T(8,128)S(1)}, f32[48,128]{1,0:T(8,128)S(1)}, u32[]{:S(2)}, u32[]{:S(2)}) %collective-permute-start.7) | collective-permute-done | bytes 24608 | tf_op jit(solution)/shard_map/ppermute | solution.py:31
  17.8 0.6 %collective-permute-done.6 = f32[48,128]{1,0:T(8,128)S(1)} collective-permute-done((f32[48,128]{1,0:T(8,128)S(1)}, f32[48,128]{1,0:T(8,128)S(1)}, u32[]{:S(2)}, u32[]{:S(2)}) %collective-permute-start.6) | collective-permute-done | bytes 24608 | tf_op jit(solution)/shard_map/ppermute | solution.py:31
  18.4 0.0 collective-permute-done.5
  18.4 2.1 %collective-permute-start.9 = (f32[72,128]{1,0:T(8,128)S(1)}, f32[72,128]{1,0:T(8,128)S(1)}, u32[]{:S(2)}, u32[]{:S(2)}) collective-permute-start(f32[72,128]{1,0:T(8,128)S(1)} %get-tuple-element.94), channel_id=1, source_target_pairs={{0,25},{1,24},{2,27},{3,26},{4,29},{5,28},{6,31},{7,30},{8,17},{9,... | collective-permute-start | bytes 110600 | tf_op jit(solution)/shard_map/ppermute | solution.py:31
  20.5 0.8 %collective-permute-start.8 = (f32[72,128]{1,0:T(8,128)S(1)}, f32[72,128]{1,0:T(8,128)S(1)}, u32[]{:S(2)}, u32[]{:S(2)}) collective-permute-start(f32[72,128]{1,0:T(8,128)S(1)} %get-tuple-element.95), channel_id=1, source_target_pairs={{0,8},{1,9},{2,10},{3,11},{4,12},{5,13},{6,14},{7,15},{8,0},{9,1},... | collective-permute-start | bytes 110600 | tf_op jit(solution)/shard_map/ppermute | solution.py:31
  21.3 1.1 %collective-permute-start.10 = (f32[40,128]{1,0:T(8,128)S(1)}, f32[40,128]{1,0:T(8,128)S(1)}, u32[]{:S(2)}, u32[]{:S(2)}) collective-permute-start(f32[40,128]{1,0:T(8,128)S(1)} %slice_add_fusion.15), channel_id=1, source_target_pairs={{0,17},{1,16},{2,19},{3,18},{4,21},{5,20},{6,23},{7,22},{8,25},{9,... | collective-permute-start | bytes 61448 | tf_op jit(solution)/shard_map/ppermute | solution.py:31
  22.4 3.2 %collective-permute-done.10 = f32[40,128]{1,0:T(8,128)S(1)} collective-permute-done((f32[40,128]{1,0:T(8,128)S(1)}, f32[40,128]{1,0:T(8,128)S(1)}, u32[]{:S(2)}, u32[]{:S(2)}) %collective-permute-start.10) | collective-permute-done | bytes 20512 | tf_op jit(solution)/shard_map/ppermute | solution.py:31
  25.6 0.0 collective-permute-done.9
  25.6 0.0 collective-permute-done.8
  25.6 0.2 collective-permute-start.11
  25.8 1.1 %collective-permute-done.11 = f32[40,128]{1,0:T(8,128)S(1)} collective-permute-done((f32[40,128]{1,0:T(8,128)S(1)}, f32[40,128]{1,0:T(8,128)S(1)}, u32[]{:S(2)}, u32[]{:S(2)}) %collective-permute-start.11) | collective-permute-done | bytes 20512 | tf_op jit(solution)/shard_map/ppermute | solution.py:31
  26.9 3.0 %shard_map.107 = (f32[8,32,128]{2,1,0:T(8,128)S(1)}, f32[8,32,128]{2,1,0:T(8,128)S(1)}, f32[8,32,128]{2,1,0:T(8,128)S(1)}, f32[112,128]{1,0:T(8,128)S(1)}, f32[8,128]{1,0:T(8,128)S(1)}) custom-call(f32[8,32,128]{2,1,0:T(8,128)S(1)} %get-tuple-element.42.right_ref.refs_0_.refs_2_, f32[8,32,128]{2,1,0:T(8,128)S(1)} %get-tuple-element.62.refs_1_, ...), custom_call_target="tpu_custom_call" | custom-call | tf_op jit(solution)/shard_map/pallas_call | solution.py:510
  29.9 0.2 collective-permute-start.12
  30.1 1.1 %collective-permute-done.12 = f32[112,128]{1,0:T(8,128)S(1)} collective-permute-done((f32[112,128]{1,0:T(8,128)S(1)}, f32[112,128]{1,0:T(8,128)S(1)}, u32[]{:S(2)}, u32[]{:S(2)}) %collective-permute-start.12) | collective-permute-done | bytes 57376 | tf_op jit(solution)/shard_map/ppermute | solution.py:31
  31.2 1.3 %collective-permute-start.15 = (f32[48,128]{1,0:T(8,128)S(1)}, f32[48,128]{1,0:T(8,128)S(1)}, u32[]{:S(2)}, u32[]{:S(2)}) collective-permute-start(f32[48,128]{1,0:T(8,128)S(1)} %pad_maximum_fusion.7), channel_id=1, source_target_pairs={{0,7},{1,6},{2,5},{3,4},{4,3},{5,2},{6,1},{7,0},{8,15},{9,14},{10,... | collective-permute-start | bytes 73736 | tf_op jit(solution)/shard_map/ppermute | solution.py:31
  32.5 0.7 %collective-permute-start.14 = (f32[48,128]{1,0:T(8,128)S(1)}, f32[48,128]{1,0:T(8,128)S(1)}, u32[]{:S(2)}, u32[]{:S(2)}) collective-permute-start(f32[48,128]{1,0:T(8,128)S(1)} %pad_maximum_fusion.7), channel_id=1, source_target_pairs={{0,5},{1,4},{2,7},{3,6},{4,1},{5,0},{6,3},{7,2},{8,13},{9,12},{10,... | collective-permute-start | bytes 73736 | tf_op jit(solution)/shard_map/ppermute | solution.py:31
  33.2 1.1 %collective-permute-start.13 = (f32[48,128]{1,0:T(8,128)S(1)}, f32[48,128]{1,0:T(8,128)S(1)}, u32[]{:S(2)}, u32[]{:S(2)}) collective-permute-start(f32[48,128]{1,0:T(8,128)S(1)} %pad_maximum_fusion.7), channel_id=1, source_target_pairs={{0,3},{1,2},{2,1},{3,0},{4,7},{5,6},{6,5},{7,4},{8,11},{9,10},{10,... | collective-permute-start | bytes 73736 | tf_op jit(solution)/shard_map/ppermute | solution.py:31
  34.3 1.2 %collective-permute-done.15 = f32[48,128]{1,0:T(8,128)S(1)} collective-permute-done((f32[48,128]{1,0:T(8,128)S(1)}, f32[48,128]{1,0:T(8,128)S(1)}, u32[]{:S(2)}, u32[]{:S(2)}) %collective-permute-start.15) | collective-permute-done | bytes 24608 | tf_op jit(solution)/shard_map/ppermute | solution.py:31
  35.4 0.6 collective-permute-done.14
  36.0 0.4 collective-permute-done.13
  36.5 2.2 %collective-permute-start.17 = (f32[72,128]{1,0:T(8,128)S(1)}, f32[72,128]{1,0:T(8,128)S(1)}, u32[]{:S(2)}, u32[]{:S(2)}) collective-permute-start(f32[72,128]{1,0:T(8,128)S(1)} %get-tuple-element.92), channel_id=1, source_target_pairs={{0,25},{1,24},{2,27},{3,26},{4,29},{5,28},{6,31},{7,30},{8,17},{9,... | collective-permute-start | bytes 110600 | tf_op jit(solution)/shard_map/ppermute | solution.py:31
  38.6 0.2 collective-permute-start.16
  38.8 1.6 %collective-permute-start.18 = (f32[40,128]{1,0:T(8,128)S(1)}, f32[40,128]{1,0:T(8,128)S(1)}, u32[]{:S(2)}, u32[]{:S(2)}) collective-permute-start(f32[40,128]{1,0:T(8,128)S(1)} %slice_add_fusion.9), channel_id=1, source_target_pairs={{0,17},{1,16},{2,19},{3,18},{4,21},{5,20},{6,23},{7,22},{8,25},{9,... | collective-permute-start | bytes 61448 | tf_op jit(solution)/shard_map/ppermute | solution.py:31
  40.4 1.4 %collective-permute-done.17 = f32[72,128]{1,0:T(8,128)S(1)} collective-permute-done((f32[72,128]{1,0:T(8,128)S(1)}, f32[72,128]{1,0:T(8,128)S(1)}, u32[]{:S(2)}, u32[]{:S(2)}) %collective-permute-start.17) | collective-permute-done | bytes 36896 | tf_op jit(solution)/shard_map/ppermute | solution.py:31
  41.8 0.9 %collective-permute-done.16 = f32[72,128]{1,0:T(8,128)S(1)} collective-permute-done((f32[72,128]{1,0:T(8,128)S(1)}, f32[72,128]{1,0:T(8,128)S(1)}, u32[]{:S(2)}, u32[]{:S(2)}) %collective-permute-start.16) | collective-permute-done | bytes 36896 | tf_op jit(solution)/shard_map/ppermute | solution.py:31
  42.7 0.3 collective-permute-done.18
  43.0 3.0 %shard_map.108 = (f32[8,32,128]{2,1,0:T(8,128)S(1)}, f32[8,32,128]{2,1,0:T(8,128)S(1)}, f32[8,32,128]{2,1,0:T(8,128)S(1)}, f32[112,128]{1,0:T(8,128)S(1)}, f32[8,128]{1,0:T(8,128)S(1)}) custom-call(f32[8,32,128]{2,1,0:T(8,128)S(1)} %get-tuple-element.72.refs_0_, f32[8,32,128]{2,1,0:T(8,128)S(1)} %get-tuple-element.73.refs_1_, ...), custom_call_target="tpu_custom_call" | custom-call | tf_op jit(solution)/shard_map/pallas_call | solution.py:510
  46.0 0.2 collective-permute-start.19
  46.3 1.0 %collective-permute-done.19 = f32[112,128]{1,0:T(8,128)S(1)} collective-permute-done((f32[112,128]{1,0:T(8,128)S(1)}, f32[112,128]{1,0:T(8,128)S(1)}, u32[]{:S(2)}, u32[]{:S(2)}) %collective-permute-start.19) | collective-permute-done | bytes 57376 | tf_op jit(solution)/shard_map/ppermute | solution.py:31
  47.3 1.3 %collective-permute-start.22 = (f32[48,128]{1,0:T(8,128)S(1)}, f32[48,128]{1,0:T(8,128)S(1)}, u32[]{:S(2)}, u32[]{:S(2)}) collective-permute-start(f32[48,128]{1,0:T(8,128)S(1)} %pad_maximum_fusion.8), channel_id=1, source_target_pairs={{0,7},{1,6},{2,5},{3,4},{4,3},{5,2},{6,1},{7,0},{8,15},{9,14},{10,... | collective-permute-start | bytes 73736 | tf_op jit(solution)/shard_map/ppermute | solution.py:31
  48.6 1.5 %collective-permute-start.21 = (f32[48,128]{1,0:T(8,128)S(1)}, f32[48,128]{1,0:T(8,128)S(1)}, u32[]{:S(2)}, u32[]{:S(2)}) collective-permute-start(f32[48,128]{1,0:T(8,128)S(1)} %pad_maximum_fusion.8), channel_id=1, source_target_pairs={{0,5},{1,4},{2,7},{3,6},{4,1},{5,0},{6,3},{7,2},{8,13},{9,12},{10,... | collective-permute-start | bytes 73736 | tf_op jit(solution)/shard_map/ppermute | solution.py:31
  50.1 0.3 collective-permute-start.20
  50.4 1.1 %collective-permute-done.22 = f32[48,128]{1,0:T(8,128)S(1)} collective-permute-done((f32[48,128]{1,0:T(8,128)S(1)}, f32[48,128]{1,0:T(8,128)S(1)}, u32[]{:S(2)}, u32[]{:S(2)}) %collective-permute-start.22) | collective-permute-done | bytes 24608 | tf_op jit(solution)/shard_map/ppermute | solution.py:31
  51.5 0.6 collective-permute-done.21
  52.1 1.3 %collective-permute-done.20 = f32[48,128]{1,0:T(8,128)S(1)} collective-permute-done((f32[48,128]{1,0:T(8,128)S(1)}, f32[48,128]{1,0:T(8,128)S(1)}, u32[]{:S(2)}, u32[]{:S(2)}) %collective-permute-start.20) | collective-permute-done | bytes 24608 | tf_op jit(solution)/shard_map/ppermute | solution.py:31
  53.4 1.6 %collective-permute-start.24 = (f32[72,128]{1,0:T(8,128)S(1)}, f32[72,128]{1,0:T(8,128)S(1)}, u32[]{:S(2)}, u32[]{:S(2)}) collective-permute-start(f32[72,128]{1,0:T(8,128)S(1)} %get-tuple-element.90), channel_id=1, source_target_pairs={{0,25},{1,24},{2,27},{3,26},{4,29},{5,28},{6,31},{7,30},{8,17},{9,... | collective-permute-start | bytes 110600 | tf_op jit(solution)/shard_map/ppermute | solution.py:31
  55.0 0.5 collective-permute-start.23
  55.5 1.9 %collective-permute-start.25 = (f32[40,128]{1,0:T(8,128)S(1)}, f32[40,128]{1,0:T(8,128)S(1)}, u32[]{:S(2)}, u32[]{:S(2)}) collective-permute-start(f32[40,128]{1,0:T(8,128)S(1)} %slice_add_fusion.3), channel_id=1, source_target_pairs={{0,17},{1,16},{2,19},{3,18},{4,21},{5,20},{6,23},{7,22},{8,25},{9,... | collective-permute-start | bytes 61448 | tf_op jit(solution)/shard_map/ppermute | solution.py:31
  57.4 1.4 %collective-permute-done.24 = f32[72,128]{1,0:T(8,128)S(1)} collective-permute-done((f32[72,128]{1,0:T(8,128)S(1)}, f32[72,128]{1,0:T(8,128)S(1)}, u32[]{:S(2)}, u32[]{:S(2)}) %collective-permute-start.24) | collective-permute-done | bytes 36896 | tf_op jit(solution)/shard_map/ppermute | solution.py:31
  58.8 0.0 collective-permute-done.23
  58.8 0.8 %collective-permute-done.25 = f32[40,128]{1,0:T(8,128)S(1)} collective-permute-done((f32[40,128]{1,0:T(8,128)S(1)}, f32[40,128]{1,0:T(8,128)S(1)}, u32[]{:S(2)}, u32[]{:S(2)}) %collective-permute-start.25) | collective-permute-done | bytes 20512 | tf_op jit(solution)/shard_map/ppermute | solution.py:31
  59.6 1.7 %shard_map.109 = (f32[8,32,128]{2,1,0:T(8,128)}, f32[8,32,128]{2,1,0:T(8,128)}) custom-call(f32[8,32,128]{2,1,0:T(8,128)S(1)} %get-tuple-element.77.refs_0_, f32[8,32,128]{2,1,0:T(8,128)S(1)} %get-tuple-element.78.refs_1_, f32[8,32,128]{2,1,0:T(8,128)S(1)} %get-tuple-element.79.refs_2_, f32[8,32,128]{2,1,0:T(8,128)S(1)} %get-tuple-element.63.refs_3_, ...), custom_call_target="tpu_custom_call" | custom-call | tf_op jit(solution)/shard_map/pallas_call | solution.py:510
  (36 shorter events, 0.2 us)
Async XLA Ops:
  1.9 8.9 %collective-permute-start = (f32[32,128]{1,0:T(8,128)S(1)}, f32[32,128]{1,0:T(8,128)S(1)}, u32[]{:S(2)}, u32[]{:S(2)}) collective-permute-start(f32[32,128]{1,0:T(8,128)S(1)} %get-tuple-element.53), channel_id=1, source_target_pairs={{0,8},{1,9},{2,10},{3,11},{4,12},{5,13},{6,14},{7,15},{8,0},{9,1},... | collective-permute-start | bytes 49160 | tf_op jit(solution)/shard_map/ppermute | solution.py:31
  5.0 5.8 %collective-permute-start.1 = (f32[32,128]{1,0:T(8,128)S(1)}, f32[32,128]{1,0:T(8,128)S(1)}, u32[]{:S(2)}, u32[]{:S(2)}) collective-permute-start(f32[32,128]{1,0:T(8,128)S(1)} %get-tuple-element.54), channel_id=1, source_target_pairs={{0,1},{1,0},{2,3},{3,2},{4,5},{5,4},{6,7},{7,6},{8,16},{9,17},{10,... | collective-permute-start | bytes 49160 | tf_op jit(solution)/shard_map/ppermute | solution.py:31
  5.0 4.7 %collective-permute-start.3 = (f32[8,128]{1,0:T(8,128)S(1)}, f32[8,128]{1,0:T(8,128)S(1)}, u32[]{:S(2)}, u32[]{:S(2)}) collective-permute-start(f32[8,128]{1,0:T(8,128)S(1)} %get-tuple-element.56), channel_id=1, source_target_pairs={{0,8},{1,2},{2,1},{3,4},{4,3},{5,6},{6,5},{7,15},{8,0},{9,10},{10,... | collective-permute-start | bytes 12296 | tf_op jit(solution)/shard_map/ppermute | solution.py:31
  9.5 1.2 %collective-permute-start.2 = (f32[8,128]{1,0:T(8,128)S(1)}, f32[8,128]{1,0:T(8,128)S(1)}, u32[]{:S(2)}, u32[]{:S(2)}) collective-permute-start(f32[8,128]{1,0:T(8,128)S(1)} %get-tuple-element.55), channel_id=1, source_target_pairs={{0,1},{1,0},{2,3},{3,2},{4,5},{5,4},{6,7},{7,6},{8,9},{9,8},{10,11... | collective-permute-start | bytes 12296 | tf_op jit(solution)/shard_map/ppermute | solution.py:31
  12.1 1.3 %collective-permute-start.4 = (f32[152,128]{1,0:T(8,128)S(1)}, f32[152,128]{1,0:T(8,128)S(1)}, u32[]{:S(2)}, u32[]{:S(2)}) collective-permute-start(f32[152,128]{1,0:T(8,128)S(1)} %get-tuple-element.70), channel_id=1, source_target_pairs={{0,1},{1,0},{2,3},{3,2},{4,5},{5,4},{6,7},{7,6},{8,9},{9,8},{10,11... | collective-permute-start | bytes 233480 | tf_op jit(solution)/shard_map/ppermute | solution.py:31
  13.5 4.3 %collective-permute-start.7 = (f32[48,128]{1,0:T(8,128)S(1)}, f32[48,128]{1,0:T(8,128)S(1)}, u32[]{:S(2)}, u32[]{:S(2)}) collective-permute-start(f32[48,128]{1,0:T(8,128)S(1)} %pad_maximum_fusion.6), channel_id=1, source_target_pairs={{0,7},{1,6},{2,5},{3,4},{4,3},{5,2},{6,1},{7,0},{8,15},{9,14},{10,... | collective-permute-start | bytes 73736 | tf_op jit(solution)/shard_map/ppermute | solution.py:31
  14.6 3.8 %collective-permute-start.6 = (f32[48,128]{1,0:T(8,128)S(1)}, f32[48,128]{1,0:T(8,128)S(1)}, u32[]{:S(2)}, u32[]{:S(2)}) collective-permute-start(f32[48,128]{1,0:T(8,128)S(1)} %pad_maximum_fusion.6), channel_id=1, source_target_pairs={{0,4},{1,5},{2,6},{3,7},{4,0},{5,1},{6,2},{7,3},{8,12},{9,13},{10,... | collective-permute-start | bytes 73736 | tf_op jit(solution)/shard_map/ppermute | solution.py:31
  14.7 3.7 %collective-permute-start.5 = (f32[48,128]{1,0:T(8,128)S(1)}, f32[48,128]{1,0:T(8,128)S(1)}, u32[]{:S(2)}, u32[]{:S(2)}) collective-permute-start(f32[48,128]{1,0:T(8,128)S(1)} %pad_maximum_fusion.6), channel_id=1, source_target_pairs={{0,3},{1,2},{2,1},{3,0},{4,7},{5,6},{6,5},{7,4},{8,11},{9,10},{10,... | collective-permute-start | bytes 73736 | tf_op jit(solution)/shard_map/ppermute | solution.py:31
  18.4 7.2 %collective-permute-start.9 = (f32[72,128]{1,0:T(8,128)S(1)}, f32[72,128]{1,0:T(8,128)S(1)}, u32[]{:S(2)}, u32[]{:S(2)}) collective-permute-start(f32[72,128]{1,0:T(8,128)S(1)} %get-tuple-element.94), channel_id=1, source_target_pairs={{0,25},{1,24},{2,27},{3,26},{4,29},{5,28},{6,31},{7,30},{8,17},{9,... | collective-permute-start | bytes 110600 | tf_op jit(solution)/shard_map/ppermute | solution.py:31
  20.5 5.1 %collective-permute-start.8 = (f32[72,128]{1,0:T(8,128)S(1)}, f32[72,128]{1,0:T(8,128)S(1)}, u32[]{:S(2)}, u32[]{:S(2)}) collective-permute-start(f32[72,128]{1,0:T(8,128)S(1)} %get-tuple-element.95), channel_id=1, source_target_pairs={{0,8},{1,9},{2,10},{3,11},{4,12},{5,13},{6,14},{7,15},{8,0},{9,1},... | collective-permute-start | bytes 110600 | tf_op jit(solution)/shard_map/ppermute | solution.py:31
  21.3 4.3 %collective-permute-start.10 = (f32[40,128]{1,0:T(8,128)S(1)}, f32[40,128]{1,0:T(8,128)S(1)}, u32[]{:S(2)}, u32[]{:S(2)}) collective-permute-start(f32[40,128]{1,0:T(8,128)S(1)} %slice_add_fusion.15), channel_id=1, source_target_pairs={{0,17},{1,16},{2,19},{3,18},{4,21},{5,20},{6,23},{7,22},{8,25},{9,... | collective-permute-start | bytes 61448 | tf_op jit(solution)/shard_map/ppermute | solution.py:31
  25.6 1.3 %collective-permute-start.11 = (f32[40,128]{1,0:T(8,128)S(1)}, f32[40,128]{1,0:T(8,128)S(1)}, u32[]{:S(2)}, u32[]{:S(2)}) collective-permute-start(f32[40,128]{1,0:T(8,128)S(1)} %slice_add_fusion.13), channel_id=1, source_target_pairs={{0,1},{1,0},{2,3},{3,2},{4,5},{5,4},{6,7},{7,6},{8,9},{9,8},{10,11... | collective-permute-start | bytes 61448 | tf_op jit(solution)/shard_map/ppermute | solution.py:31
  29.9 1.3 %collective-permute-start.12 = (f32[112,128]{1,0:T(8,128)S(1)}, f32[112,128]{1,0:T(8,128)S(1)}, u32[]{:S(2)}, u32[]{:S(2)}) collective-permute-start(f32[112,128]{1,0:T(8,128)S(1)} %get-tuple-element.75), channel_id=1, source_target_pairs={{0,1},{1,0},{2,3},{3,2},{4,5},{5,4},{6,7},{7,6},{8,9},{9,8},{10,11... | collective-permute-start | bytes 172040 | tf_op jit(solution)/shard_map/ppermute | solution.py:31
  31.2 4.2 %collective-permute-start.15 = (f32[48,128]{1,0:T(8,128)S(1)}, f32[48,128]{1,0:T(8,128)S(1)}, u32[]{:S(2)}, u32[]{:S(2)}) collective-permute-start(f32[48,128]{1,0:T(8,128)S(1)} %pad_maximum_fusion.7), channel_id=1, source_target_pairs={{0,7},{1,6},{2,5},{3,4},{4,3},{5,2},{6,1},{7,0},{8,15},{9,14},{10,... | collective-permute-start | bytes 73736 | tf_op jit(solution)/shard_map/ppermute | solution.py:31
  32.5 3.5 %collective-permute-start.14 = (f32[48,128]{1,0:T(8,128)S(1)}, f32[48,128]{1,0:T(8,128)S(1)}, u32[]{:S(2)}, u32[]{:S(2)}) collective-permute-start(f32[48,128]{1,0:T(8,128)S(1)} %pad_maximum_fusion.7), channel_id=1, source_target_pairs={{0,5},{1,4},{2,7},{3,6},{4,1},{5,0},{6,3},{7,2},{8,13},{9,12},{10,... | collective-permute-start | bytes 73736 | tf_op jit(solution)/shard_map/ppermute | solution.py:31
  33.2 3.3 %collective-permute-start.13 = (f32[48,128]{1,0:T(8,128)S(1)}, f32[48,128]{1,0:T(8,128)S(1)}, u32[]{:S(2)}, u32[]{:S(2)}) collective-permute-start(f32[48,128]{1,0:T(8,128)S(1)} %pad_maximum_fusion.7), channel_id=1, source_target_pairs={{0,3},{1,2},{2,1},{3,0},{4,7},{5,6},{6,5},{7,4},{8,11},{9,10},{10,... | collective-permute-start | bytes 73736 | tf_op jit(solution)/shard_map/ppermute | solution.py:31
  36.5 5.3 %collective-permute-start.17 = (f32[72,128]{1,0:T(8,128)S(1)}, f32[72,128]{1,0:T(8,128)S(1)}, u32[]{:S(2)}, u32[]{:S(2)}) collective-permute-start(f32[72,128]{1,0:T(8,128)S(1)} %get-tuple-element.92), channel_id=1, source_target_pairs={{0,25},{1,24},{2,27},{3,26},{4,29},{5,28},{6,31},{7,30},{8,17},{9,... | collective-permute-start | bytes 110600 | tf_op jit(solution)/shard_map/ppermute | solution.py:31
  38.6 4.1 %collective-permute-start.16 = (f32[72,128]{1,0:T(8,128)S(1)}, f32[72,128]{1,0:T(8,128)S(1)}, u32[]{:S(2)}, u32[]{:S(2)}) collective-permute-start(f32[72,128]{1,0:T(8,128)S(1)} %get-tuple-element.93), channel_id=1, source_target_pairs={{0,9},{1,8},{2,11},{3,10},{4,13},{5,12},{6,15},{7,14},{8,1},{9,0},... | collective-permute-start | bytes 110600 | tf_op jit(solution)/shard_map/ppermute | solution.py:31
  38.8 4.1 %collective-permute-start.18 = (f32[40,128]{1,0:T(8,128)S(1)}, f32[40,128]{1,0:T(8,128)S(1)}, u32[]{:S(2)}, u32[]{:S(2)}) collective-permute-start(f32[40,128]{1,0:T(8,128)S(1)} %slice_add_fusion.9), channel_id=1, source_target_pairs={{0,17},{1,16},{2,19},{3,18},{4,21},{5,20},{6,23},{7,22},{8,25},{9,... | collective-permute-start | bytes 61448 | tf_op jit(solution)/shard_map/ppermute | solution.py:31
  46.0 1.3 %collective-permute-start.19 = (f32[112,128]{1,0:T(8,128)S(1)}, f32[112,128]{1,0:T(8,128)S(1)}, u32[]{:S(2)}, u32[]{:S(2)}) collective-permute-start(f32[112,128]{1,0:T(8,128)S(1)} %get-tuple-element.80), channel_id=1, source_target_pairs={{0,1},{1,0},{2,3},{3,2},{4,5},{5,4},{6,7},{7,6},{8,9},{9,8},{10,11... | collective-permute-start | bytes 172040 | tf_op jit(solution)/shard_map/ppermute | solution.py:31
  47.3 4.2 %collective-permute-start.22 = (f32[48,128]{1,0:T(8,128)S(1)}, f32[48,128]{1,0:T(8,128)S(1)}, u32[]{:S(2)}, u32[]{:S(2)}) collective-permute-start(f32[48,128]{1,0:T(8,128)S(1)} %pad_maximum_fusion.8), channel_id=1, source_target_pairs={{0,7},{1,6},{2,5},{3,4},{4,3},{5,2},{6,1},{7,0},{8,15},{9,14},{10,... | collective-permute-start | bytes 73736 | tf_op jit(solution)/shard_map/ppermute | solution.py:31
  48.6 3.5 %collective-permute-start.21 = (f32[48,128]{1,0:T(8,128)S(1)}, f32[48,128]{1,0:T(8,128)S(1)}, u32[]{:S(2)}, u32[]{:S(2)}) collective-permute-start(f32[48,128]{1,0:T(8,128)S(1)} %pad_maximum_fusion.8), channel_id=1, source_target_pairs={{0,5},{1,4},{2,7},{3,6},{4,1},{5,0},{6,3},{7,2},{8,13},{9,12},{10,... | collective-permute-start | bytes 73736 | tf_op jit(solution)/shard_map/ppermute | solution.py:31
  50.1 3.3 %collective-permute-start.20 = (f32[48,128]{1,0:T(8,128)S(1)}, f32[48,128]{1,0:T(8,128)S(1)}, u32[]{:S(2)}, u32[]{:S(2)}) collective-permute-start(f32[48,128]{1,0:T(8,128)S(1)} %pad_maximum_fusion.8), channel_id=1, source_target_pairs={{0,3},{1,2},{2,1},{3,0},{4,7},{5,6},{6,5},{7,4},{8,11},{9,10},{10,... | collective-permute-start | bytes 73736 | tf_op jit(solution)/shard_map/ppermute | solution.py:31
  53.4 5.4 %collective-permute-start.24 = (f32[72,128]{1,0:T(8,128)S(1)}, f32[72,128]{1,0:T(8,128)S(1)}, u32[]{:S(2)}, u32[]{:S(2)}) collective-permute-start(f32[72,128]{1,0:T(8,128)S(1)} %get-tuple-element.90), channel_id=1, source_target_pairs={{0,25},{1,24},{2,27},{3,26},{4,29},{5,28},{6,31},{7,30},{8,17},{9,... | collective-permute-start | bytes 110600 | tf_op jit(solution)/shard_map/ppermute | solution.py:31
  55.0 3.8 %collective-permute-start.23 = (f32[72,128]{1,0:T(8,128)S(1)}, f32[72,128]{1,0:T(8,128)S(1)}, u32[]{:S(2)}, u32[]{:S(2)}) collective-permute-start(f32[72,128]{1,0:T(8,128)S(1)} %get-tuple-element.91), channel_id=1, source_target_pairs={{0,9},{1,8},{2,11},{3,10},{4,13},{5,12},{6,15},{7,14},{8,1},{9,0},... | collective-permute-start | bytes 110600 | tf_op jit(solution)/shard_map/ppermute | solution.py:31
  55.5 4.1 %collective-permute-start.25 = (f32[40,128]{1,0:T(8,128)S(1)}, f32[40,128]{1,0:T(8,128)S(1)}, u32[]{:S(2)}, u32[]{:S(2)}) collective-permute-start(f32[40,128]{1,0:T(8,128)S(1)} %slice_add_fusion.3), channel_id=1, source_target_pairs={{0,17},{1,16},{2,19},{3,18},{4,21},{5,20},{6,23},{7,22},{8,25},{9,... | collective-permute-start | bytes 61448 | tf_op jit(solution)/shard_map/ppermute | solution.py:31

commit v7 on v6

--- a/solution.py
+++ b/solution.py
@@ -58,11 +58,11 @@
 
 def all_stages():
     return [[(0, mask) for mask in masks] for masks in stages_of(lax.axis_size("xline"))] + [
-        [(mask, 1) for mask in masks] for masks in stages_of(lax.axis_size("inline"))
+        [(mask, 1) for mask in reversed(masks)] for masks in stages_of(lax.axis_size("inline"))
     ]
 
 
-SPLIT_STAGES = [[(0, 1)], [(0, 3), (0, 4), (0, 7)], [(1, 0), (2, 1), (3, 1)]]
+SPLIT_STAGES = [[(0, 1)], [(0, 3), (0, 4), (0, 7)], [(3, 1), (2, 1), (1, 0)]]
 
 
 def two_kinds():

time: 61.5 us -> 61.5 us (level)
  no operation moved by 1% of the time
where the time goes in v7:
time: 61.5 us; the launch traced here: 61.4 us
  starting transfers between devices  28.2 us (46%)
  waiting for transfers between devices  20.4 us (33%)
  Pallas kernels  11.8 us (19%)
  between operations  0.76 us (1%)
    ppermute x26, starting transfers between devices, pair_permute(): return lax.ppermute(value, MESH_AXES, pairs)  28.2 us
    ppermute x26, waiting for transfers between devices, pair_permute(): return lax.ppermute(value, MESH_AXES, pairs)  20.4 us
    pallas_call x3, Pallas kernels, body(): pl.pallas_call(functools.partial(sweep_kernel, keep=keep, gain=gain, firs...  7.83 us
    pallas_call x1, Pallas kernels, body(): pl.pallas_call(perforation_kernel, out_shape=(grid, sums, grid, grid, *ho...  1.4 us
    pallas_call x1, Pallas kernels, body(): pl.pallas_call(functools.partial(start_kernel, scale=1.0 / theta), out_sh...  1.36 us
  transfers between devices with their start and end apart: 26, of which 20 were waited for; matrix products, arithmetic and copies ran while one was open for 0% of the time, Pallas kernels for 2%

profile of v7, /device:TPU:0, one launch (start us, length us, event | category | flops | bytes accessed | tf_op | source)
XLA Modules:
  0.0 61.4 jit_solution(4628956889824067553)
XLA Ops:
  0.6 1.2 %shard_map.104 = (f32[32,128]{1,0:T(8,128)S(1)}, f32[32,128]{1,0:T(8,128)S(1)}, f32[8,128]{1,0:T(8,128)S(1)}, f32[8,128]{1,0:T(8,128)S(1)}, f32[8,32,128]{2,1,0:...) custom-call(f32[2,8]{1,0:T(2,128)} %table_hbm.1, ...), custom_call_target="tpu_custom_call" | custom-call | tf_op jit(solution)/shard_map/pallas_call | solution.py:451
  1.9 3.1 %collective-permute-start = (f32[32,128]{1,0:T(8,128)S(1)}, f32[32,128]{1,0:T(8,128)S(1)}, u32[]{:S(2)}, u32[]{:S(2)}) collective-permute-start(f32[32,128]{1,0:T(8,128)S(1)} %get-tuple-element.53), channel_id=1, source_target_pairs={{0,8},{1,9},{2,10},{3,11},{4,12},{5,13},{6,14},{7,15},{8,0},{9,1},... | collective-permute-start | bytes 49160 | tf_op jit(solution)/shard_map/ppermute | solution.py:31
  5.0 0.0 collective-permute-start.1
  5.0 3.1 %collective-permute-start.3 = (f32[8,128]{1,0:T(8,128)S(1)}, f32[8,128]{1,0:T(8,128)S(1)}, u32[]{:S(2)}, u32[]{:S(2)}) collective-permute-start(f32[8,128]{1,0:T(8,128)S(1)} %get-tuple-element.56), channel_id=1, source_target_pairs={{0,8},{1,2},{2,1},{3,4},{4,3},{5,6},{6,5},{7,15},{8,0},{9,10},{10,... | collective-permute-start | bytes 12296 | tf_op jit(solution)/shard_map/ppermute | solution.py:31
  8.1 1.4 %shard_map.105 = (f32[8,32,128]{2,1,0:T(8,128)S(1)}, f32[40,128]{1,0:T(8,128)S(1)}, f32[8,32,128]{2,1,0:T(8,128)S(1)}, f32[8,32,128]{2,1,0:T(8,128)S(1)}, bf16[2...) custom-call(f32[8,32,128]{2,1,0:T(8,128)S(1)} %get-tuple-element.45., ...), custom_call_target="tpu_custom_call" | custom-call | tf_op jit(solution)/shard_map/pallas_call | solution.py:469
  9.5 0.1 collective-permute-start.2
  9.6 0.1 collective-permute-done.3.xb_ref
  9.7 1.1 %collective-permute-done.2.xa_ref = f32[8,128]{1,0:T(8,128)S(1)} collective-permute-done((f32[8,128]{1,0:T(8,128)S(1)}, f32[8,128]{1,0:T(8,128)S(1)}, u32[]{:S(2)}, u32[]{:S(2)}) %collective-permute-start.2) | collective-permute-done | bytes 4128 | tf_op jit(solution)/shard_map/ppermute | solution.py:31
  10.7 0.0 collective-permute-done.ia_ref
  10.7 0.0 collective-permute-done.1.ib_ref
  10.8 1.4 %shard_map.106 = (f32[8,32,128]{2,1,0:T(8,128)S(1)}, f32[8,32,128]{2,1,0:T(8,128)S(1)}, f32[8,32,128]{2,1,0:T(8,128)S(1)}, f32[8,32,128]{2,1,0:T(8,128)S(1)}, f3...) custom-call(f32[8,32,128]{2,1,0:T(8,128)S(1)} %get-tuple-element.42., ...), custom_call_target="tpu_custom_call" | custom-call | tf_op jit(solution)/shard_map/pallas_call | solution.py:487
  12.1 0.2 collective-permute-start.4
  12.3 1.1 %collective-permute-done.4 = f32[152,128]{1,0:T(8,128)S(1)} collective-permute-done((f32[152,128]{1,0:T(8,128)S(1)}, f32[152,128]{1,0:T(8,128)S(1)}, u32[]{:S(2)}, u32[]{:S(2)}) %collective-permute-start.4) | collective-permute-done | bytes 77856 | tf_op jit(solution)/shard_map/ppermute | solution.py:31
  13.5 1.1 %collective-permute-start.7 = (f32[48,128]{1,0:T(8,128)S(1)}, f32[48,128]{1,0:T(8,128)S(1)}, u32[]{:S(2)}, u32[]{:S(2)}) collective-permute-start(f32[48,128]{1,0:T(8,128)S(1)} %pad_maximum_fusion.6), channel_id=1, source_target_pairs={{0,7},{1,6},{2,5},{3,4},{4,3},{5,2},{6,1},{7,0},{8,15},{9,14},{10,... | collective-permute-start | bytes 73736 | tf_op jit(solution)/shard_map/ppermute | solution.py:31
  14.6 0.2 collective-permute-start.6
  14.7 1.7 %collective-permute-start.5 = (f32[48,128]{1,0:T(8,128)S(1)}, f32[48,128]{1,0:T(8,128)S(1)}, u32[]{:S(2)}, u32[]{:S(2)}) collective-permute-start(f32[48,128]{1,0:T(8,128)S(1)} %pad_maximum_fusion.6), channel_id=1, source_target_pairs={{0,3},{1,2},{2,1},{3,0},{4,7},{5,6},{6,5},{7,4},{8,11},{9,10},{10,... | collective-permute-start | bytes 73736 | tf_op jit(solution)/shard_map/ppermute | solution.py:31
  16.5 1.3 %collective-permute-done.7 = f32[48,128]{1,0:T(8,128)S(1)} collective-permute-done((f32[48,128]{1,0:T(8,128)S(1)}, f32[48,128]{1,0:T(8,128)S(1)}, u32[]{:S(2)}, u32[]{:S(2)}) %collective-permute-start.7) | collective-permute-done | bytes 24608 | tf_op jit(solution)/shard_map/ppermute | solution.py:31
  17.8 0.6 %collective-permute-done.6 = f32[48,128]{1,0:T(8,128)S(1)} collective-permute-done((f32[48,128]{1,0:T(8,128)S(1)}, f32[48,128]{1,0:T(8,128)S(1)}, u32[]{:S(2)}, u32[]{:S(2)}) %collective-permute-start.6) | collective-permute-done | bytes 24608 | tf_op jit(solution)/shard_map/ppermute | solution.py:31
  18.4 0.0 collective-permute-done.5
  18.4 2.1 %collective-permute-start.9 = (f32[72,128]{1,0:T(8,128)S(1)}, f32[72,128]{1,0:T(8,128)S(1)}, u32[]{:S(2)}, u32[]{:S(2)}) collective-permute-start(f32[72,128]{1,0:T(8,128)S(1)} %get-tuple-element.94), channel_id=1, source_target_pairs={{0,25},{1,24},{2,27},{3,26},{4,29},{5,28},{6,31},{7,30},{8,17},{9,... | collective-permute-start | bytes 110600 | tf_op jit(solution)/shard_map/ppermute | solution.py:31
  20.5 0.8 %collective-permute-start.8 = (f32[72,128]{1,0:T(8,128)S(1)}, f32[72,128]{1,0:T(8,128)S(1)}, u32[]{:S(2)}, u32[]{:S(2)}) collective-permute-start(f32[72,128]{1,0:T(8,128)S(1)} %get-tuple-element.95), channel_id=1, source_target_pairs={{0,8},{1,9},{2,10},{3,11},{4,12},{5,13},{6,14},{7,15},{8,0},{9,1},... | collective-permute-start | bytes 110600 | tf_op jit(solution)/shard_map/ppermute | solution.py:31
  21.3 1.1 %collective-permute-start.10 = (f32[40,128]{1,0:T(8,128)S(1)}, f32[40,128]{1,0:T(8,128)S(1)}, u32[]{:S(2)}, u32[]{:S(2)}) collective-permute-start(f32[40,128]{1,0:T(8,128)S(1)} %slice_add_fusion.15), channel_id=1, source_target_pairs={{0,17},{1,16},{2,19},{3,18},{4,21},{5,20},{6,23},{7,22},{8,25},{9,... | collective-permute-start | bytes 61448 | tf_op jit(solution)/shard_map/ppermute | solution.py:31
  22.4 3.2 %collective-permute-done.10 = f32[40,128]{1,0:T(8,128)S(1)} collective-permute-done((f32[40,128]{1,0:T(8,128)S(1)}, f32[40,128]{1,0:T(8,128)S(1)}, u32[]{:S(2)}, u32[]{:S(2)}) %collective-permute-start.10) | collective-permute-done | bytes 20512 | tf_op jit(solution)/shard_map/ppermute | solution.py:31
  25.6 0.0 collective-permute-done.9
  25.6 0.0 collective-permute-done.8
  25.6 0.2 collective-permute-start.11
  25.8 1.1 %collective-permute-done.11 = f32[40,128]{1,0:T(8,128)S(1)} collective-permute-done((f32[40,128]{1,0:T(8,128)S(1)}, f32[40,128]{1,0:T(8,128)S(1)}, u32[]{:S(2)}, u32[]{:S(2)}) %collective-permute-start.11) | collective-permute-done | bytes 20512 | tf_op jit(solution)/shard_map/ppermute | solution.py:31
  26.9 3.0 %shard_map.107 = (f32[8,32,128]{2,1,0:T(8,128)S(1)}, f32[8,32,128]{2,1,0:T(8,128)S(1)}, f32[8,32,128]{2,1,0:T(8,128)S(1)}, f32[112,128]{1,0:T(8,128)S(1)}, f32[8,128]{1,0:T(8,128)S(1)}) custom-call(f32[8,32,128]{2,1,0:T(8,128)S(1)} %get-tuple-element.42.right_ref.refs_0_.refs_2_, f32[8,32,128]{2,1,0:T(8,128)S(1)} %get-tuple-element.62.refs_1_, ...), custom_call_target="tpu_custom_call" | custom-call | tf_op jit(solution)/shard_map/pallas_call | solution.py:510
  29.9 0.2 collective-permute-start.12
  30.1 1.1 %collective-permute-done.12 = f32[112,128]{1,0:T(8,128)S(1)} collective-permute-done((f32[112,128]{1,0:T(8,128)S(1)}, f32[112,128]{1,0:T(8,128)S(1)}, u32[]{:S(2)}, u32[]{:S(2)}) %collective-permute-start.12) | collective-permute-done | bytes 57376 | tf_op jit(solution)/shard_map/ppermute | solution.py:31
  31.2 1.3 %collective-permute-start.15 = (f32[48,128]{1,0:T(8,128)S(1)}, f32[48,128]{1,0:T(8,128)S(1)}, u32[]{:S(2)}, u32[]{:S(2)}) collective-permute-start(f32[48,128]{1,0:T(8,128)S(1)} %pad_maximum_fusion.7), channel_id=1, source_target_pairs={{0,7},{1,6},{2,5},{3,4},{4,3},{5,2},{6,1},{7,0},{8,15},{9,14},{10,... | collective-permute-start | bytes 73736 | tf_op jit(solution)/shard_map/ppermute | solution.py:31
  32.5 0.7 %collective-permute-start.14 = (f32[48,128]{1,0:T(8,128)S(1)}, f32[48,128]{1,0:T(8,128)S(1)}, u32[]{:S(2)}, u32[]{:S(2)}) collective-permute-start(f32[48,128]{1,0:T(8,128)S(1)} %pad_maximum_fusion.7), channel_id=1, source_target_pairs={{0,5},{1,4},{2,7},{3,6},{4,1},{5,0},{6,3},{7,2},{8,13},{9,12},{10,... | collective-permute-start | bytes 73736 | tf_op jit(solution)/shard_map/ppermute | solution.py:31
  33.2 1.1 %collective-permute-start.13 = (f32[48,128]{1,0:T(8,128)S(1)}, f32[48,128]{1,0:T(8,128)S(1)}, u32[]{:S(2)}, u32[]{:S(2)}) collective-permute-start(f32[48,128]{1,0:T(8,128)S(1)} %pad_maximum_fusion.7), channel_id=1, source_target_pairs={{0,3},{1,2},{2,1},{3,0},{4,7},{5,6},{6,5},{7,4},{8,11},{9,10},{10,... | collective-permute-start | bytes 73736 | tf_op jit(solution)/shard_map/ppermute | solution.py:31
  34.3 1.2 %collective-permute-done.15 = f32[48,128]{1,0:T(8,128)S(1)} collective-permute-done((f32[48,128]{1,0:T(8,128)S(1)}, f32[48,128]{1,0:T(8,128)S(1)}, u32[]{:S(2)}, u32[]{:S(2)}) %collective-permute-start.15) | collective-permute-done | bytes 24608 | tf_op jit(solution)/shard_map/ppermute | solution.py:31
  35.4 0.6 collective-permute-done.14
  36.0 0.4 collective-permute-done.13
  36.5 2.2 %collective-permute-start.17 = (f32[72,128]{1,0:T(8,128)S(1)}, f32[72,128]{1,0:T(8,128)S(1)}, u32[]{:S(2)}, u32[]{:S(2)}) collective-permute-start(f32[72,128]{1,0:T(8,128)S(1)} %get-tuple-element.92), channel_id=1, source_target_pairs={{0,25},{1,24},{2,27},{3,26},{4,29},{5,28},{6,31},{7,30},{8,17},{9,... | collective-permute-start | bytes 110600 | tf_op jit(solution)/shard_map/ppermute | solution.py:31
  38.6 0.2 collective-permute-start.16
  38.8 1.6 %collective-permute-start.18 = (f32[40,128]{1,0:T(8,128)S(1)}, f32[40,128]{1,0:T(8,128)S(1)}, u32[]{:S(2)}, u32[]{:S(2)}) collective-permute-start(f32[40,128]{1,0:T(8,128)S(1)} %slice_add_fusion.9), channel_id=1, source_target_pairs={{0,17},{1,16},{2,19},{3,18},{4,21},{5,20},{6,23},{7,22},{8,25},{9,... | collective-permute-start | bytes 61448 | tf_op jit(solution)/shard_map/ppermute | solution.py:31
  40.4 1.4 %collective-permute-done.17 = f32[72,128]{1,0:T(8,128)S(1)} collective-permute-done((f32[72,128]{1,0:T(8,128)S(1)}, f32[72,128]{1,0:T(8,128)S(1)}, u32[]{:S(2)}, u32[]{:S(2)}) %collective-permute-start.17) | collective-permute-done | bytes 36896 | tf_op jit(solution)/shard_map/ppermute | solution.py:31
  41.8 0.9 %collective-permute-done.16 = f32[72,128]{1,0:T(8,128)S(1)} collective-permute-done((f32[72,128]{1,0:T(8,128)S(1)}, f32[72,128]{1,0:T(8,128)S(1)}, u32[]{:S(2)}, u32[]{:S(2)}) %collective-permute-start.16) | collective-permute-done | bytes 36896 | tf_op jit(solution)/shard_map/ppermute | solution.py:31
  42.7 0.3 collective-permute-done.18
  43.0 3.0 %shard_map.108 = (f32[8,32,128]{2,1,0:T(8,128)S(1)}, f32[8,32,128]{2,1,0:T(8,128)S(1)}, f32[8,32,128]{2,1,0:T(8,128)S(1)}, f32[112,128]{1,0:T(8,128)S(1)}, f32[8,128]{1,0:T(8,128)S(1)}) custom-call(f32[8,32,128]{2,1,0:T(8,128)S(1)} %get-tuple-element.72.refs_0_, f32[8,32,128]{2,1,0:T(8,128)S(1)} %get-tuple-element.73.refs_1_, ...), custom_call_target="tpu_custom_call" | custom-call | tf_op jit(solution)/shard_map/pallas_call | solution.py:510
  46.0 0.2 collective-permute-start.19
  46.3 1.0 %collective-permute-done.19 = f32[112,128]{1,0:T(8,128)S(1)} collective-permute-done((f32[112,128]{1,0:T(8,128)S(1)}, f32[112,128]{1,0:T(8,128)S(1)}, u32[]{:S(2)}, u32[]{:S(2)}) %collective-permute-start.19) | collective-permute-done | bytes 57376 | tf_op jit(solution)/shard_map/ppermute | solution.py:31
  47.3 1.3 %collective-permute-start.22 = (f32[48,128]{1,0:T(8,128)S(1)}, f32[48,128]{1,0:T(8,128)S(1)}, u32[]{:S(2)}, u32[]{:S(2)}) collective-permute-start(f32[48,128]{1,0:T(8,128)S(1)} %pad_maximum_fusion.8), channel_id=1, source_target_pairs={{0,7},{1,6},{2,5},{3,4},{4,3},{5,2},{6,1},{7,0},{8,15},{9,14},{10,... | collective-permute-start | bytes 73736 | tf_op jit(solution)/shard_map/ppermute | solution.py:31
  48.6 1.5 %collective-permute-start.21 = (f32[48,128]{1,0:T(8,128)S(1)}, f32[48,128]{1,0:T(8,128)S(1)}, u32[]{:S(2)}, u32[]{:S(2)}) collective-permute-start(f32[48,128]{1,0:T(8,128)S(1)} %pad_maximum_fusion.8), channel_id=1, source_target_pairs={{0,5},{1,4},{2,7},{3,6},{4,1},{5,0},{6,3},{7,2},{8,13},{9,12},{10,... | collective-permute-start | bytes 73736 | tf_op jit(solution)/shard_map/ppermute | solution.py:31
  50.1 0.3 collective-permute-start.20
  50.4 1.1 %collective-permute-done.22 = f32[48,128]{1,0:T(8,128)S(1)} collective-permute-done((f32[48,128]{1,0:T(8,128)S(1)}, f32[48,128]{1,0:T(8,128)S(1)}, u32[]{:S(2)}, u32[]{:S(2)}) %collective-permute-start.22) | collective-permute-done | bytes 24608 | tf_op jit(solution)/shard_map/ppermute | solution.py:31
  51.5 0.6 collective-permute-done.21
  52.1 1.3 %collective-permute-done.20 = f32[48,128]{1,0:T(8,128)S(1)} collective-permute-done((f32[48,128]{1,0:T(8,128)S(1)}, f32[48,128]{1,0:T(8,128)S(1)}, u32[]{:S(2)}, u32[]{:S(2)}) %collective-permute-start.20) | collective-permute-done | bytes 24608 | tf_op jit(solution)/shard_map/ppermute | solution.py:31
  53.4 1.6 %collective-permute-start.24 = (f32[72,128]{1,0:T(8,128)S(1)}, f32[72,128]{1,0:T(8,128)S(1)}, u32[]{:S(2)}, u32[]{:S(2)}) collective-permute-start(f32[72,128]{1,0:T(8,128)S(1)} %get-tuple-element.90), channel_id=1, source_target_pairs={{0,25},{1,24},{2,27},{3,26},{4,29},{5,28},{6,31},{7,30},{8,17},{9,... | collective-permute-start | bytes 110600 | tf_op jit(solution)/shard_map/ppermute | solution.py:31
  55.0 0.5 collective-permute-start.23
  55.5 1.9 %collective-permute-start.25 = (f32[40,128]{1,0:T(8,128)S(1)}, f32[40,128]{1,0:T(8,128)S(1)}, u32[]{:S(2)}, u32[]{:S(2)}) collective-permute-start(f32[40,128]{1,0:T(8,128)S(1)} %slice_add_fusion.3), channel_id=1, source_target_pairs={{0,17},{1,16},{2,19},{3,18},{4,21},{5,20},{6,23},{7,22},{8,25},{9,... | collective-permute-start | bytes 61448 | tf_op jit(solution)/shard_map/ppermute | solution.py:31
  57.4 1.4 %collective-permute-done.24 = f32[72,128]{1,0:T(8,128)S(1)} collective-permute-done((f32[72,128]{1,0:T(8,128)S(1)}, f32[72,128]{1,0:T(8,128)S(1)}, u32[]{:S(2)}, u32[]{:S(2)}) %collective-permute-start.24) | collective-permute-done | bytes 36896 | tf_op jit(solution)/shard_map/ppermute | solution.py:31
  58.8 0.0 collective-permute-done.23
  58.8 0.8 %collective-permute-done.25 = f32[40,128]{1,0:T(8,128)S(1)} collective-permute-done((f32[40,128]{1,0:T(8,128)S(1)}, f32[40,128]{1,0:T(8,128)S(1)}, u32[]{:S(2)}, u32[]{:S(2)}) %collective-permute-start.25) | collective-permute-done | bytes 20512 | tf_op jit(solution)/shard_map/ppermute | solution.py:31
  59.6 1.7 %shard_map.109 = (f32[8,32,128]{2,1,0:T(8,128)}, f32[8,32,128]{2,1,0:T(8,128)}) custom-call(f32[8,32,128]{2,1,0:T(8,128)S(1)} %get-tuple-element.77.refs_0_, f32[8,32,128]{2,1,0:T(8,128)S(1)} %get-tuple-element.78.refs_1_, f32[8,32,128]{2,1,0:T(8,128)S(1)} %get-tuple-element.79.refs_2_, f32[8,32,128]{2,1,0:T(8,128)S(1)} %get-tuple-element.63.refs_3_, ...), custom_call_target="tpu_custom_call" | custom-call | tf_op jit(solution)/shard_map/pallas_call | solution.py:510
  (36 shorter events, 0.2 us)
Async XLA Ops:
  1.9 8.9 %collective-permute-start = (f32[32,128]{1,0:T(8,128)S(1)}, f32[32,128]{1,0:T(8,128)S(1)}, u32[]{:S(2)}, u32[]{:S(2)}) collective-permute-start(f32[32,128]{1,0:T(8,128)S(1)} %get-tuple-element.53), channel_id=1, source_target_pairs={{0,8},{1,9},{2,10},{3,11},{4,12},{5,13},{6,14},{7,15},{8,0},{9,1},... | collective-permute-start | bytes 49160 | tf_op jit(solution)/shard_map/ppermute | solution.py:31
  5.0 5.8 %collective-permute-start.1 = (f32[32,128]{1,0:T(8,128)S(1)}, f32[32,128]{1,0:T(8,128)S(1)}, u32[]{:S(2)}, u32[]{:S(2)}) collective-permute-start(f32[32,128]{1,0:T(8,128)S(1)} %get-tuple-element.54), channel_id=1, source_target_pairs={{0,1},{1,0},{2,3},{3,2},{4,5},{5,4},{6,7},{7,6},{8,16},{9,17},{10,... | collective-permute-start | bytes 49160 | tf_op jit(solution)/shard_map/ppermute | solution.py:31
  5.0 4.7 %collective-permute-start.3 = (f32[8,128]{1,0:T(8,128)S(1)}, f32[8,128]{1,0:T(8,128)S(1)}, u32[]{:S(2)}, u32[]{:S(2)}) collective-permute-start(f32[8,128]{1,0:T(8,128)S(1)} %get-tuple-element.56), channel_id=1, source_target_pairs={{0,8},{1,2},{2,1},{3,4},{4,3},{5,6},{6,5},{7,15},{8,0},{9,10},{10,... | collective-permute-start | bytes 12296 | tf_op jit(solution)/shard_map/ppermute | solution.py:31
  9.5 1.2 %collective-permute-start.2 = (f32[8,128]{1,0:T(8,128)S(1)}, f32[8,128]{1,0:T(8,128)S(1)}, u32[]{:S(2)}, u32[]{:S(2)}) collective-permute-start(f32[8,128]{1,0:T(8,128)S(1)} %get-tuple-element.55), channel_id=1, source_target_pairs={{0,1},{1,0},{2,3},{3,2},{4,5},{5,4},{6,7},{7,6},{8,9},{9,8},{10,11... | collective-permute-start | bytes 12296 | tf_op jit(solution)/shard_map/ppermute | solution.py:31
  12.1 1.3 %collective-permute-start.4 = (f32[152,128]{1,0:T(8,128)S(1)}, f32[152,128]{1,0:T(8,128)S(1)}, u32[]{:S(2)}, u32[]{:S(2)}) collective-permute-start(f32[152,128]{1,0:T(8,128)S(1)} %get-tuple-element.70), channel_id=1, source_target_pairs={{0,1},{1,0},{2,3},{3,2},{4,5},{5,4},{6,7},{7,6},{8,9},{9,8},{10,11... | collective-permute-start | bytes 233480 | tf_op jit(solution)/shard_map/ppermute | solution.py:31
  13.5 4.3 %collective-permute-start.7 = (f32[48,128]{1,0:T(8,128)S(1)}, f32[48,128]{1,0:T(8,128)S(1)}, u32[]{:S(2)}, u32[]{:S(2)}) collective-permute-start(f32[48,128]{1,0:T(8,128)S(1)} %pad_maximum_fusion.6), channel_id=1, source_target_pairs={{0,7},{1,6},{2,5},{3,4},{4,3},{5,2},{6,1},{7,0},{8,15},{9,14},{10,... | collective-permute-start | bytes 73736 | tf_op jit(solution)/shard_map/ppermute | solution.py:31
  14.6 3.8 %collective-permute-start.6 = (f32[48,128]{1,0:T(8,128)S(1)}, f32[48,128]{1,0:T(8,128)S(1)}, u32[]{:S(2)}, u32[]{:S(2)}) collective-permute-start(f32[48,128]{1,0:T(8,128)S(1)} %pad_maximum_fusion.6), channel_id=1, source_target_pairs={{0,4},{1,5},{2,6},{3,7},{4,0},{5,1},{6,2},{7,3},{8,12},{9,13},{10,... | collective-permute-start | bytes 73736 | tf_op jit(solution)/shard_map/ppermute | solution.py:31
  14.7 3.7 %collective-permute-start.5 = (f32[48,128]{1,0:T(8,128)S(1)}, f32[48,128]{1,0:T(8,128)S(1)}, u32[]{:S(2)}, u32[]{:S(2)}) collective-permute-start(f32[48,128]{1,0:T(8,128)S(1)} %pad_maximum_fusion.6), channel_id=1, source_target_pairs={{0,3},{1,2},{2,1},{3,0},{4,7},{5,6},{6,5},{7,4},{8,11},{9,10},{10,... | collective-permute-start | bytes 73736 | tf_op jit(solution)/shard_map/ppermute | solution.py:31
  18.4 7.2 %collective-permute-start.9 = (f32[72,128]{1,0:T(8,128)S(1)}, f32[72,128]{1,0:T(8,128)S(1)}, u32[]{:S(2)}, u32[]{:S(2)}) collective-permute-start(f32[72,128]{1,0:T(8,128)S(1)} %get-tuple-element.94), channel_id=1, source_target_pairs={{0,25},{1,24},{2,27},{3,26},{4,29},{5,28},{6,31},{7,30},{8,17},{9,... | collective-permute-start | bytes 110600 | tf_op jit(solution)/shard_map/ppermute | solution.py:31
  20.5 5.1 %collective-permute-start.8 = (f32[72,128]{1,0:T(8,128)S(1)}, f32[72,128]{1,0:T(8,128)S(1)}, u32[]{:S(2)}, u32[]{:S(2)}) collective-permute-start(f32[72,128]{1,0:T(8,128)S(1)} %get-tuple-element.95), channel_id=1, source_target_pairs={{0,8},{1,9},{2,10},{3,11},{4,12},{5,13},{6,14},{7,15},{8,0},{9,1},... | collective-permute-start | bytes 110600 | tf_op jit(solution)/shard_map/ppermute | solution.py:31
  21.3 4.3 %collective-permute-start.10 = (f32[40,128]{1,0:T(8,128)S(1)}, f32[40,128]{1,0:T(8,128)S(1)}, u32[]{:S(2)}, u32[]{:S(2)}) collective-permute-start(f32[40,128]{1,0:T(8,128)S(1)} %slice_add_fusion.15), channel_id=1, source_target_pairs={{0,17},{1,16},{2,19},{3,18},{4,21},{5,20},{6,23},{7,22},{8,25},{9,... | collective-permute-start | bytes 61448 | tf_op jit(solution)/shard_map/ppermute | solution.py:31
  25.6 1.3 %collective-permute-start.11 = (f32[40,128]{1,0:T(8,128)S(1)}, f32[40,128]{1,0:T(8,128)S(1)}, u32[]{:S(2)}, u32[]{:S(2)}) collective-permute-start(f32[40,128]{1,0:T(8,128)S(1)} %slice_add_fusion.13), channel_id=1, source_target_pairs={{0,1},{1,0},{2,3},{3,2},{4,5},{5,4},{6,7},{7,6},{8,9},{9,8},{10,11... | collective-permute-start | bytes 61448 | tf_op jit(solution)/shard_map/ppermute | solution.py:31
  29.9 1.3 %collective-permute-start.12 = (f32[112,128]{1,0:T(8,128)S(1)}, f32[112,128]{1,0:T(8,128)S(1)}, u32[]{:S(2)}, u32[]{:S(2)}) collective-permute-start(f32[112,128]{1,0:T(8,128)S(1)} %get-tuple-element.75), channel_id=1, source_target_pairs={{0,1},{1,0},{2,3},{3,2},{4,5},{5,4},{6,7},{7,6},{8,9},{9,8},{10,11... | collective-permute-start | bytes 172040 | tf_op jit(solution)/shard_map/ppermute | solution.py:31
  31.2 4.2 %collective-permute-start.15 = (f32[48,128]{1,0:T(8,128)S(1)}, f32[48,128]{1,0:T(8,128)S(1)}, u32[]{:S(2)}, u32[]{:S(2)}) collective-permute-start(f32[48,128]{1,0:T(8,128)S(1)} %pad_maximum_fusion.7), channel_id=1, source_target_pairs={{0,7},{1,6},{2,5},{3,4},{4,3},{5,2},{6,1},{7,0},{8,15},{9,14},{10,... | collective-permute-start | bytes 73736 | tf_op jit(solution)/shard_map/ppermute | solution.py:31
  32.5 3.5 %collective-permute-start.14 = (f32[48,128]{1,0:T(8,128)S(1)}, f32[48,128]{1,0:T(8,128)S(1)}, u32[]{:S(2)}, u32[]{:S(2)}) collective-permute-start(f32[48,128]{1,0:T(8,128)S(1)} %pad_maximum_fusion.7), channel_id=1, source_target_pairs={{0,5},{1,4},{2,7},{3,6},{4,1},{5,0},{6,3},{7,2},{8,13},{9,12},{10,... | collective-permute-start | bytes 73736 | tf_op jit(solution)/shard_map/ppermute | solution.py:31
  33.2 3.3 %collective-permute-start.13 = (f32[48,128]{1,0:T(8,128)S(1)}, f32[48,128]{1,0:T(8,128)S(1)}, u32[]{:S(2)}, u32[]{:S(2)}) collective-permute-start(f32[48,128]{1,0:T(8,128)S(1)} %pad_maximum_fusion.7), channel_id=1, source_target_pairs={{0,3},{1,2},{2,1},{3,0},{4,7},{5,6},{6,5},{7,4},{8,11},{9,10},{10,... | collective-permute-start | bytes 73736 | tf_op jit(solution)/shard_map/ppermute | solution.py:31
  36.5 5.3 %collective-permute-start.17 = (f32[72,128]{1,0:T(8,128)S(1)}, f32[72,128]{1,0:T(8,128)S(1)}, u32[]{:S(2)}, u32[]{:S(2)}) collective-permute-start(f32[72,128]{1,0:T(8,128)S(1)} %get-tuple-element.92), channel_id=1, source_target_pairs={{0,25},{1,24},{2,27},{3,26},{4,29},{5,28},{6,31},{7,30},{8,17},{9,... | collective-permute-start | bytes 110600 | tf_op jit(solution)/shard_map/ppermute | solution.py:31
  38.6 4.1 %collective-permute-start.16 = (f32[72,128]{1,0:T(8,128)S(1)}, f32[72,128]{1,0:T(8,128)S(1)}, u32[]{:S(2)}, u32[]{:S(2)}) collective-permute-start(f32[72,128]{1,0:T(8,128)S(1)} %get-tuple-element.93), channel_id=1, source_target_pairs={{0,9},{1,8},{2,11},{3,10},{4,13},{5,12},{6,15},{7,14},{8,1},{9,0},... | collective-permute-start | bytes 110600 | tf_op jit(solution)/shard_map/ppermute | solution.py:31
  38.8 4.1 %collective-permute-start.18 = (f32[40,128]{1,0:T(8,128)S(1)}, f32[40,128]{1,0:T(8,128)S(1)}, u32[]{:S(2)}, u32[]{:S(2)}) collective-permute-start(f32[40,128]{1,0:T(8,128)S(1)} %slice_add_fusion.9), channel_id=1, source_target_pairs={{0,17},{1,16},{2,19},{3,18},{4,21},{5,20},{6,23},{7,22},{8,25},{9,... | collective-permute-start | bytes 61448 | tf_op jit(solution)/shard_map/ppermute | solution.py:31
  46.0 1.3 %collective-permute-start.19 = (f32[112,128]{1,0:T(8,128)S(1)}, f32[112,128]{1,0:T(8,128)S(1)}, u32[]{:S(2)}, u32[]{:S(2)}) collective-permute-start(f32[112,128]{1,0:T(8,128)S(1)} %get-tuple-element.80), channel_id=1, source_target_pairs={{0,1},{1,0},{2,3},{3,2},{4,5},{5,4},{6,7},{7,6},{8,9},{9,8},{10,11... | collective-permute-start | bytes 172040 | tf_op jit(solution)/shard_map/ppermute | solution.py:31
  47.3 4.2 %collective-permute-start.22 = (f32[48,128]{1,0:T(8,128)S(1)}, f32[48,128]{1,0:T(8,128)S(1)}, u32[]{:S(2)}, u32[]{:S(2)}) collective-permute-start(f32[48,128]{1,0:T(8,128)S(1)} %pad_maximum_fusion.8), channel_id=1, source_target_pairs={{0,7},{1,6},{2,5},{3,4},{4,3},{5,2},{6,1},{7,0},{8,15},{9,14},{10,... | collective-permute-start | bytes 73736 | tf_op jit(solution)/shard_map/ppermute | solution.py:31
  48.6 3.5 %collective-permute-start.21 = (f32[48,128]{1,0:T(8,128)S(1)}, f32[48,128]{1,0:T(8,128)S(1)}, u32[]{:S(2)}, u32[]{:S(2)}) collective-permute-start(f32[48,128]{1,0:T(8,128)S(1)} %pad_maximum_fusion.8), channel_id=1, source_target_pairs={{0,5},{1,4},{2,7},{3,6},{4,1},{5,0},{6,3},{7,2},{8,13},{9,12},{10,... | collective-permute-start | bytes 73736 | tf_op jit(solution)/shard_map/ppermute | solution.py:31
  50.1 3.3 %collective-permute-start.20 = (f32[48,128]{1,0:T(8,128)S(1)}, f32[48,128]{1,0:T(8,128)S(1)}, u32[]{:S(2)}, u32[]{:S(2)}) collective-permute-start(f32[48,128]{1,0:T(8,128)S(1)} %pad_maximum_fusion.8), channel_id=1, source_target_pairs={{0,3},{1,2},{2,1},{3,0},{4,7},{5,6},{6,5},{7,4},{8,11},{9,10},{10,... | collective-permute-start | bytes 73736 | tf_op jit(solution)/shard_map/ppermute | solution.py:31
  53.4 5.4 %collective-permute-start.24 = (f32[72,128]{1,0:T(8,128)S(1)}, f32[72,128]{1,0:T(8,128)S(1)}, u32[]{:S(2)}, u32[]{:S(2)}) collective-permute-start(f32[72,128]{1,0:T(8,128)S(1)} %get-tuple-element.90), channel_id=1, source_target_pairs={{0,25},{1,24},{2,27},{3,26},{4,29},{5,28},{6,31},{7,30},{8,17},{9,... | collective-permute-start | bytes 110600 | tf_op jit(solution)/shard_map/ppermute | solution.py:31
  55.0 3.8 %collective-permute-start.23 = (f32[72,128]{1,0:T(8,128)S(1)}, f32[72,128]{1,0:T(8,128)S(1)}, u32[]{:S(2)}, u32[]{:S(2)}) collective-permute-start(f32[72,128]{1,0:T(8,128)S(1)} %get-tuple-element.91), channel_id=1, source_target_pairs={{0,9},{1,8},{2,11},{3,10},{4,13},{5,12},{6,15},{7,14},{8,1},{9,0},... | collective-permute-start | bytes 110600 | tf_op jit(solution)/shard_map/ppermute | solution.py:31
  55.5 4.1 %collective-permute-start.25 = (f32[40,128]{1,0:T(8,128)S(1)}, f32[40,128]{1,0:T(8,128)S(1)}, u32[]{:S(2)}, u32[]{:S(2)}) collective-permute-start(f32[40,128]{1,0:T(8,128)S(1)} %slice_add_fusion.3), channel_id=1, source_target_pairs={{0,17},{1,16},{2,19},{3,18},{4,21},{5,20},{6,23},{7,22},{8,25},{9,... | collective-permute-start | bytes 61448 | tf_op jit(solution)/shard_map/ppermute | solution.py:31
